TPU v7x, 32 devices: a whole 2x2x4 slice. The times are simulated.
32 devices in a mesh: seq: 8 (over z, x), tp: 4 (over y, core).
Axes of the slice: x: 2, y: 2, z: 4, core: 2. Of those that a mesh axis runs over, the one named last changes fastest.
Arguments:
- token_ids: int32 [8192], P('seq'), may hold values from 0 to 511
- embed_table: bfloat16 [512, 2048], P(None, 'tp'), may hold values from -6 to 6
- norm_gain: float32 [2048], replicated, may hold values from 0.1 to 1.9
- in_weight: bfloat16 [2048, 3, 2048], P('seq', None, 'tp'), may hold values from -0.125 to 0.125
- short_filter: float32 [7, 3, 2048], P(None, None, 'tp'), may hold values from -2.4 to 2.4
- long_filter: bfloat16 [128, 128], P('tp'), may hold values from -0.5390625 to 0.5390625
- long_skip: float32 [2048], P('tp'), may hold values from -3 to 3
- out_weight: bfloat16 [2048, 2048], P('tp', 'seq'), may hold values from -0.125 to 0.125
Outputs:
- mixed: bfloat16 [8192, 2048], P('seq', 'tp')
All inputs are finite; a program needn't handle non-finite values.
Results may differ from a plain program's by a relative error of at most 0.012.
Values may be sent and summed in bfloat16 or wider, within the bound.
No kernel may reach another device: no remote copies, remote signals or barrier semaphores. Data moves between devices by JAX's collectives and lax.ppermute only.
A program may use at most 64 MiB of HBM per device.

v0:
```python
import jax
import jax.numpy as jnp
from jax import lax
from jax.sharding import PartitionSpec as P


def from_behind(block, axis, distance):
    devices = range(lax.axis_size(axis))
    route = [(i - distance, i) for i in devices if i - distance in devices]
    return lax.ppermute(block, axis, route)


def short_conv(extended, short_filter, out_length):
    short_taps = short_filter.shape[0]
    running = jnp.zeros((out_length,) + extended.shape[1:], jnp.float32)
    for tap_index in range(short_taps):
        begin = short_taps - 1 - tap_index
        running = running + short_filter[tap_index][None] * extended[
            begin : begin + out_length
        ].astype(jnp.float32)
    return running


def body(
    token_ids, embed_table, norm_gain, in_weight, short_filter, long_filter, long_skip, out_weight
):
    tok_count = token_ids.shape[0]
    vocab_size = embed_table.shape[0]
    local_width = embed_table.shape[1]
    onehot = (token_ids[:, None] == jnp.arange(vocab_size, dtype=jnp.int32)[None, :]).astype(
        jnp.bfloat16
    )
    own_feats = jnp.dot(onehot, embed_table, preferred_element_type=jnp.float32).astype(
        jnp.bfloat16
    )
    features = lax.all_gather(own_feats, "tp", axis=1, tiled=True)
    widened = features.astype(jnp.float32)
    scaled = (
        widened
        * lax.rsqrt(jnp.mean(widened * widened, axis=1, keepdims=True) + 1e-06)
        * norm_gain[None, :]
    )
    normed = scaled.astype(jnp.bfloat16)
    projected = jnp.einsum(
        "td,dsc->tsc",
        normed,
        lax.all_gather(in_weight, "seq", axis=0, tiled=True),
        preferred_element_type=jnp.float32,
    ).astype(jnp.bfloat16)
    tap_count = long_filter.shape[1]
    short_taps = short_filter.shape[0]
    rim_rows = from_behind(projected[tok_count - short_taps + 1 :], "seq", 1)
    extended = jnp.concatenate([rim_rows, projected], axis=0)
    featured = short_conv(extended, short_filter, tok_count)
    queries = featured[:, 0]
    gated_kv = (featured[:, 1] * featured[:, 2]).astype(jnp.bfloat16)
    earlier = from_behind(gated_kv[tok_count - tap_count :], "seq", 1)
    product = jnp.concatenate([earlier, gated_kv], axis=0)
    groups_here = long_filter.shape[0]
    group_size = local_width // groups_here
    positions = jnp.arange(tap_count, dtype=jnp.int32)
    differ = positions[:, None, None] - positions[None, :, None]
    target = positions[None, None, :]
    near_pick = (differ == target).astype(jnp.float32)
    far_pick = (differ + tap_count == target).astype(jnp.float32)
    filter_f32 = long_filter.astype(jnp.float32)
    near_band = jnp.einsum("isj,gj->gis", near_pick, filter_f32).astype(jnp.bfloat16)
    far_band = jnp.einsum("isj,gj->gis", far_pick, filter_f32).astype(jnp.bfloat16)
    blocks = product.reshape(tok_count // tap_count + 1, tap_count, groups_here, group_size)
    convolved = jnp.einsum(
        "gis,bsgc->bigc", near_band, blocks[1:], preferred_element_type=jnp.float32
    )
    convolved = convolved + jnp.einsum(
        "gis,bsgc->bigc", far_band, blocks[:-1], preferred_element_type=jnp.float32
    )
    convolved = convolved.reshape(tok_count, local_width) + long_skip[None, :] * product[
        tap_count:
    ].astype(jnp.float32)
    gated = (queries * convolved).astype(jnp.bfloat16)
    partials = jnp.dot(
        gated,
        lax.all_gather(out_weight, "seq", axis=1, tiled=True),
        preferred_element_type=jnp.float32,
    )
    own_share = lax.psum_scatter(
        partials.astype(jnp.bfloat16), "tp", scatter_dimension=1, tiled=True
    ).astype(jnp.float32)
    return (own_feats.astype(jnp.float32) + own_share).astype(jnp.bfloat16)


def solution(mesh):
    placed = (
        P("seq"),
        P(None, "tp"),
        P(),
        P("seq", None, "tp"),
        P(None, None, "tp"),
        P("tp", None),
        P("tp"),
        P("tp", "seq"),
    )
    return jax.shard_map(
        body, mesh=mesh, in_specs=placed, out_specs=P("seq", "tp"), check_vma=False
    )
```

profile of v0, /device:TPU:0, one launch (start us, length us, event | category | flops | bytes accessed | tf_op | source)
XLA Modules:
  0.0 261.1 jit_solution(2425309109599497290)
XLA Ops:
  6.5 0.0 copy-start
  6.5 0.0 all-gather.4.cloned.1.call-start
  6.5 1.0 copy-done
  7.6 2.4 fusion.24
  10.0 0.0 all-gather.4.cloned.1.call-update
  10.0 0.0 all-gather.6.cloned.1.call-start
  10.1 0.7 all-gather.6.cloned.1.call-update
  10.8 0.0 all-gather.8.cloned.1.call-start
  10.8 0.7 all-gather.8.cloned.1.call-update
  11.5 0.0 reduce-scatter.2.cloned.1.call-start
  11.6 1.2 fusion.38
  12.8 0.0 copy-start.6
  12.8 5.8 %fusion.3 = bf16[128,128,32]{1,2,0:T(8,128)(2,1)} fusion(s32[128,128]{1,0:T(8,128)S(1)} %iota_subtract_fusion, bf16[32,128]{1,0:T(8,128)(2,1)} %param.13), kind=kOutput, calls=%fused_computation.7 | convolution fusion | flops 136314880 | bytes 1122304 | tf_op jit(solution)/shard_map/isj,gj->gis/dot_general | solution.py:67
  18.6 0.0 copy-done.5
  18.6 5.1 %fusion.4 = bf16[128,128,32]{1,2,0:T(8,128)(2,1)} fusion(s32[128,128]{1,0:T(8,128)S(1)} %broadcast_add_fusion, bf16[32,128]{1,0:T(8,128)(2,1)S(1)} %copy-done.5), kind=kOutput, calls=%fused_computation.8 | convolution fusion | flops 136314880 | bytes 1122304 | tf_op jit(solution)/shard_map/isj,gj->gis/dot_general | solution.py:68
  23.7 23.6 %all-gather.4.cloned.1.call-done = bf16[1024,2048]{1,0:T(8,128)(2,1)} async-done(((bf16[1024,512]{1,0:T(8,128)(2,1)}), bf16[1024,2048]{1,0:T(8,128)(2,1)}) %all-gather.4.cloned.1.call-update) | async-done | bytes 4194320 | tf_op jit(solution)/shard_map/all_gather | solution.py:36
  47.4 3.1 %fusion = f32[1024]{0:T(1024)S(1)} fusion(bf16[1024,2048]{1,0:T(8,128)(2,1)} %all-gather.4.cloned.1.call-done), kind=kLoop, calls=%fused_computation.2 | loop fusion | flops 6290432 | bytes 4198400 | tf_op jit(solution)/shard_map/reduce_sum | solution.py:40
  50.5 98.2 %all-gather.6.cloned.1.call-done = bf16[2048,3,512]{2,0,1:T(8,128)(2,1)} async-done(((bf16[256,3,512]{2,0,1:T(8,128)(2,1)}), bf16[2048,3,512]{2,0,1:T(8,128)(2,1)}) %all-gather.6.cloned.1.call-update) | async-done | bytes 6291472 | tf_op jit(solution)/shard_map/all_gather | solution.py:47
  148.6 0.0 copy-done.6
  148.6 10.5 %fusion.17 = bf16[1024,3,512]{2,0,1:T(8,128)(2,1)S(1)} fusion(bf16[2048,3,512]{2,0,1:T(8,128)(2,1)} %all-gather.6.cloned.1.call-done, bf16[1024,2048]{1,0:T(8,128)(2,1)} %all-gather.4.cloned.1.call-done, f32[2048]{0:T(1024)S(1)} %copy-done.6, f32[1024]{0:T(1024)S(1)} %add_rsqrt_fusion), kind=kOutput, calls=%fused_computation.31 | convolution fusion | flops 6452412416 | bytes 13643776 | tf_op jit(solution)/shard_map/td,dsc->tsc/dot_general | solution.py:44
  159.2 2.5 collective-permute-start
  161.7 1.5 collective-permute-done
  163.2 5.6 %multiply_add_fusion = f32[1024,3,512]{2,0,1:T(8,128)S(1)} fusion(bf16[1024,3,512]{2,0,1:T(8,128)(2,1)S(1)} %fusion.17, bf16[6,3,512]{2,0,1:T(8,128)(2,1)S(1)} %collective-permute-done, f32[3,512]{1,0:T(4,128)S(1)} %get-tuple-element.12, f32[3,512]{1,0:T(4,128)S(1)} %get-tuple-element.13, f32[3,512]{1,0:T(4,128)S(1)} %get-tuple-element.14, ...), kind=kLoop, calls=%fused_computation.14 | loop fusion | flops 59768832 | bytes 9498624 | tf_op jit(solution)/shard_map/add | solution.py:18
  168.8 0.0 copy-start.1
  168.8 2.7 %copy-done.1 = f32[1024,3,512]{2,0,1:T(8,128)} copy-done((f32[1024,3,512]{2,0,1:T(8,128)}, f32[1024,3,512]{2,0,1:T(8,128)S(1)}, u32[]{:S(2)}) %copy-start.1) | copy-done | bytes 6291480
  171.4 0.4 fusion.20
  171.8 0.0 copy-start.3
  171.8 0.5 copy.12
  172.4 0.0 copy-start.2
  172.4 4.7 %collective-permute-start.1 = (bf16[128,512]{1,0:T(8,128)(2,1)S(1)}, bf16[128,512]{1,0:T(8,128)(2,1)S(1)}, u32[]{:S(2)}, u32[]{:S(2)}) collective-permute-start(bf16[128,512]{1,0:T(8,128)(2,1)S(1)} %slice_bitcast_fusion.1), channel_id=1, source_target_pairs={{0,4},{4,8},{8,12},{12,16},{16,20},{20,24},{24,28},{1,5},{5,9},{9,... | collective-permute-start | bytes 393224 | tf_op jit(solution)/shard_map/ppermute | solution.py:10
  177.0 0.3 copy.29
  177.3 2.1 fusion.26
  179.5 0.0 copy-done.2
  179.5 0.4 fusion.42
  179.8 1.9 collective-permute-done.1
  181.8 1.1 pad_maximum_fusion.1
  182.8 2.3 copy.14
  185.1 1.5 copy.30
  186.6 2.1 add_bitcast_fusion
  188.7 0.0 copy-start.7
  188.7 0.9 copy.16
  189.6 0.5 copy.52
  190.1 1.8 copy.17
  191.9 9.7 %all-gather.8.cloned.1.call-done = bf16[512,2048]{1,0:T(8,128)(2,1)} async-done(((bf16[512,256]{1,0:T(8,128)(2,1)}), bf16[512,2048]{1,0:T(8,128)(2,1)}) %all-gather.8.cloned.1.call-update) | async-done | bytes 2097168 | tf_op jit(solution)/shard_map/all_gather | solution.py:82
  201.6 7.6 %convolution_convert_fusion = bf16[1024,2048]{1,0:T(8,128)(2,1)} fusion(bf16[512,2048]{1,0:T(8,128)(2,1)} %all-gather.8.cloned.1.call-done, f32[1024,3,512]{2,0,1:T(8,128)} %copy-done.1, f32[1024,512]{1,0:T(8,128)} %copy.17, f32[512]{0:T(512)S(1)} %copy-done.7, bf16[1024,1,512]{2,0,1:T(8,128)(2,1)} %copy-done.3), kind=kOutput, calls=%fused_computation.21 | convolution fusion | flops 2152202240 | bytes 11536384 | tf_op jit(solution)/shard_map/dot_general | solution.py:80
  209.2 0.0 reduce-scatter.2.cloned.1.call-update
  209.2 42.9 %reduce-scatter.2.cloned.1.call-done = bf16[1024,512]{1,0:T(8,128)(2,1)} async-done(((bf16[1024,2048]{1,0:T(8,128)(2,1)}), bf16[1024,512]{1,0:T(8,128)(2,1)}) %reduce-scatter.2.cloned.1.call-update) | async-done | bytes 1048592 | tf_op jit(solution)/shard_map/reduce_scatter | solution.py:85
  252.1 2.5 add_convert_fusion
  (14 shorter events, 0.1 us)
Async XLA Ops:
  6.5 1.0 copy-start
  6.5 12.1 %copy-start.5 = (bf16[32,128]{1,0:T(8,128)(2,1)S(1)}, bf16[32,128]{1,0:T(8,128)(2,1)}, u32[]{:S(2)}) copy-start(bf16[32,128]{1,0:T(8,128)(2,1)} %param.13) | copy-start | bytes 24580
  6.5 40.9 %all-gather.4.cloned.1.call-start = ((), (), s32[]{:S(2)}) async-start(), calls=%async_computation.1 | async-start | bytes 5242880 | tf_op jit(solution)/shard_map/all_gather | solution.py:36
  10.0 138.6 %all-gather.6.cloned.1.call-start = ((), (), s32[]{:S(2)}) async-start(), calls=%async_computation.2 | async-start | bytes 7077888 | tf_op jit(solution)/shard_map/all_gather | solution.py:47
  10.8 190.8 %all-gather.8.cloned.1.call-start = ((), (), s32[]{:S(2)}) async-start(), calls=%async_computation.3 | async-start | bytes 2359296 | tf_op jit(solution)/shard_map/all_gather | solution.py:82
  11.5 240.6 %reduce-scatter.2.cloned.1.call-start = ((), (), s32[]{:S(2)}) async-start(), calls=%async_computation.4 | async-start | bytes 5242880 | tf_op jit(solution)/shard_map/reduce_scatter | solution.py:85
  12.8 135.8 %copy-start.6 = (f32[2048]{0:T(1024)S(1)}, f32[2048]{0:T(1024)}, u32[]{:S(2)}) copy-start(f32[2048]{0:T(1024)} %param.10) | copy-start | bytes 24580
  159.2 4.0 %collective-permute-start = (bf16[6,3,512]{2,0,1:T(8,128)(2,1)S(1)}, bf16[6,3,512]{2,0,1:T(8,128)(2,1)S(1)}, u32[]{:S(2)}, u32[]{:S(2)}) collective-permute-start(bf16[6,3,512]{2,0,1:T(8,128)(2,1)S(1)} %slice.86), channel_id=1, source_target_pairs={{0,4},{4,8},{8,12},{12,16},{16,20},{20,24},{24,28},{1,5},{5,9},{9,... | collective-permute-start | bytes 55304 | tf_op jit(solution)/shard_map/ppermute | solution.py:10
  168.8 2.7 %copy-start.1 = (f32[1024,3,512]{2,0,1:T(8,128)}, f32[1024,3,512]{2,0,1:T(8,128)S(1)}, u32[]{:S(2)}) copy-start(f32[1024,3,512]{2,0,1:T(8,128)S(1)} %multiply_add_fusion) | copy-start | bytes 18874372
  171.8 5.5 %copy-start.3 = (bf16[1024,1,512]{2,0,1:T(8,128)(2,1)}, bf16[1024,1,512]{2,0,1:T(8,128)(2,1)S(1)}, u32[]{:S(2)}) copy-start(bf16[1024,1,512]{2,0,1:T(8,128)(2,1)S(1)} %fusion.20) | copy-start | bytes 3145732
  172.4 7.1 %copy-start.2 = (f32[1024,3,512]{2,0,1:T(8,128)S(1)}, f32[1024,3,512]{2,0,1:T(8,128)}, u32[]{:S(2)}) copy-start(f32[1024,3,512]{2,0,1:T(8,128)} %copy-done.1) | copy-start | bytes 18874372
  172.4 9.4 %collective-permute-start.1 = (bf16[128,512]{1,0:T(8,128)(2,1)S(1)}, bf16[128,512]{1,0:T(8,128)(2,1)S(1)}, u32[]{:S(2)}, u32[]{:S(2)}) collective-permute-start(bf16[128,512]{1,0:T(8,128)(2,1)S(1)} %slice_bitcast_fusion.1), channel_id=1, source_target_pairs={{0,4},{4,8},{8,12},{12,16},{16,20},{20,24},{24,28},{1,5},{5,9},{9,... | collective-permute-start | bytes 393224 | tf_op jit(solution)/shard_map/ppermute | solution.py:10
  188.7 12.9 %copy-start.7 = (f32[512]{0:T(512)S(1)}, f32[512]{0:T(512)}, u32[]{:S(2)}) copy-start(f32[512]{0:T(512)} %param.14) | copy-start | bytes 6148
  191.9 60.2 %copy-start.4 = (bf16[1024,512]{1,0:T(8,128)(2,1)S(1)}, bf16[1024,512]{1,0:T(8,128)(2,1)}, u32[]{:S(2)}) copy-start(bf16[1024,512]{1,0:T(8,128)(2,1)} %fusion.24) | copy-start | bytes 3145732
Sparse Core Ops, SparseCore 0:
  10.1 37.2 all-gather.3
  49.6 99.0 all-gather.5
  150.7 50.8 all-gather.7
  209.3 42.7 reduce-scatter.1
where the time goes:
time: 262 us; the launch traced here: 261 us
  waiting for transfers between devices  179 us (68%)
  matrix products  35.6 us (14%)
  between operations  13.3 us (5%)
  other arithmetic  12.9 us (5%)
  local copies, waits for them, and re-layouts  12.7 us (5%)
  starting transfers between devices  7.26 us (3%)
    all_gather x1, waiting for transfers between devices, body(): lax.all_gather(in_weight, 'seq', axis=0, tiled=True)  98.2 us
    reduce_scatter x1, waiting for transfers between devices, body(): lax.psum_scatter(partials.astype(jnp.bfloat16), 'tp', scatter_dimension=1...  42.9 us
    all_gather x1, waiting for transfers between devices, body(): features = lax.all_gather(own_feats, 'tp', axis=1, tiled=True)  23.6 us
    dot_general x1, matrix products, body(): jnp.einsum('td,dsc->tsc', normed, lax.all_gather(in_weight, 'seq', axis=0...  10.5 us
    all_gather x1, waiting for transfers between devices, body(): lax.all_gather(out_weight, 'seq', axis=1, tiled=True)  9.71 us
    dot_general x1, matrix products, body(): jnp.dot(gated, lax.all_gather(out_weight, 'seq', axis=1, tiled=True), pre...  7.56 us
    ppermute x2, starting transfers between devices, from_behind(): return lax.ppermute(block, axis, route)  7.14 us
    unnamed x23, local copies, waits for them, and re-layouts  5.97 us
  transfers between devices with their start and end apart: 6, of which 6 were waited for; matrix products, arithmetic and copies ran while one was open for 17% of the time, Pallas kernels for 0%

commit v1 on v0

v1 whole, which is shorter than its diff:
```python
import functools

import jax
import jax.numpy as jnp
from jax import lax
from jax.experimental import pallas as pl
from jax.experimental.pallas import tpu as pltpu
from jax.sharding import PartitionSpec as P

BF = jnp.bfloat16
F32 = jnp.float32
VMEM_LIMIT = 48 * 1024 * 1024
WHOLE = pl.BlockSpec(memory_space=pltpu.VMEM)
SCALARS = pl.BlockSpec(memory_space=pltpu.SMEM)


def swap(block, axis, offset):
    count = lax.axis_size(axis)
    return lax.ppermute(block, axis, [(i, i ^ offset) for i in range(count)])


def doubled(blocks, axis, offsets):
    for offset in offsets:
        blocks = blocks + [swap(block, axis, offset) for block in blocks]
    return blocks


def call(kernel, out_shape, count, flops, moved, **more):
    return pl.pallas_call(
        kernel,
        out_shape=out_shape,
        in_specs=more.pop("in_specs", [WHOLE] * count),
        compiler_params=pltpu.CompilerParams(vmem_limit_bytes=VMEM_LIMIT),
        cost_estimate=pl.CostEstimate(flops=flops, bytes_accessed=moved, transcendentals=0),
        **more,
    )


def onehot_kernel(ids_ref, out_ref):
    rows = lax.broadcasted_iota(jnp.int32, out_ref.shape, 0)
    out_ref[...] = (rows == ids_ref[...]).astype(F32).astype(BF)


def embed_kernel(onehot_ref, table_ref, out_ref):
    tokens = out_ref.shape[0]
    halo = onehot_ref.shape[1] - tokens
    out_ref[...] = lax.dot_general(
        onehot_ref[:, halo:], table_ref[...], (((0,), (0,)), ((), ())), preferred_element_type=F32
    ).astype(BF)


def band_kernel(filter_ref, out_ref):
    groups, taps = filter_ref.shape
    row = lax.broadcasted_iota(jnp.int32, (taps, taps), 0)
    col = lax.broadcasted_iota(jnp.int32, (taps, taps), 1)
    for g in range(groups):
        line = jnp.broadcast_to(filter_ref[g : g + 1, :].astype(F32), (taps, taps))
        ring = pltpu.roll(line, 0, 1, stride=1, stride_axis=0)
        out_ref[g, :taps, :] = jnp.where(col < row, ring, 0.0).astype(BF)
        out_ref[g, taps:, :] = jnp.where(col >= row, ring, 0.0).astype(BF)


def norm_kernel(where_ref, gain_ref, *refs):
    blocks, out_ref = refs[:-1], refs[-1]
    total = 0.0
    for block in blocks:
        wide = block[...].astype(F32)
        total = total + jnp.sum(wide * wide, axis=1, keepdims=True)
    scale = lax.rsqrt(total / (len(blocks) * blocks[0].shape[1]) + 1e-06)
    for j, block in enumerate(blocks):
        gain = gain_ref[where_ref[1] ^ j]
        out_ref[j] = (block[...].astype(F32) * scale * gain).astype(BF)


def project_kernel(where_ref, weight_ref, normed_ref, out_ref):
    pieces, _, depth = weight_ref.shape
    blocks = normed_ref.shape[0]
    each = pieces // blocks
    total = jnp.zeros(out_ref.shape, F32)
    for j in range(blocks):
        for r in range(each):
            total = total + lax.dot_general(
                weight_ref[(where_ref[1] ^ j) * each + r],
                normed_ref[j, :, r * depth : (r + 1) * depth],
                (((1,), (1,)), ((), ())),
                preferred_element_type=F32,
            )
    out_ref[...] = total.astype(BF)


def mixer_kernel(
    group_size, short_taps, where_ref, onehot_ref, param_ref, band_ref, *refs
):
    pieces, out_ref, proj_ref, gate_ref = refs[:-3], refs[-3], refs[-2], refs[-1]
    tokens = out_ref.shape[0]
    taps = band_ref.shape[2]
    length = onehot_ref.shape[1]
    halo = length - tokens
    width = pieces[0].shape[0] // 3
    inner = width // group_size
    blocks = tokens // taps
    for p, piece in enumerate(pieces):
        place = (where_ref[0] & (len(pieces) - 1)) ^ p
        proj_ref[...] = jnp.dot(piece[...], onehot_ref[...], preferred_element_type=F32)
        for g in range(inner):
            lower = g * group_size

            def taken(s):
                rows = pl.ds(s * width + lower, group_size)
                line = proj_ref[rows, :]
                factors = param_ref[place, rows, :]
                total = factors[:, 0:1] * line
                for lag in range(1, short_taps):
                    total = total + factors[:, lag : lag + 1] * pltpu.roll(line, lag, 1)
                return total

            product = (taken(1) * taken(2))[:, halo - taps :].astype(BF)
            stacked = jnp.concatenate(
                [product[:, b * taps : (b + 2) * taps] for b in range(blocks)], axis=0
            )
            mixed = jnp.dot(
                stacked, band_ref[place * inner + g], preferred_element_type=F32
            )
            conv = jnp.concatenate(
                [mixed[b * group_size : (b + 1) * group_size] for b in range(blocks)], axis=1
            )
            skip = param_ref[place, pl.ds(lower, group_size), :][:, short_taps : short_taps + 1]
            conv = conv + skip * product[:, taps:].astype(F32)
            gated = taken(0)[:, halo:] * conv
            begin = pl.multiple_of(place * width + lower, group_size)
            gate_ref[pl.ds(begin, group_size), :] = gated
    out_ref[...] = gate_ref[...].T.astype(BF)


def out_kernel(chunks, half, where_ref, *refs):
    gates, weights, out_ref, lhs_ref = refs[: 2 * chunks], refs[2 * chunks : -2], refs[-2], refs[-1]
    lane = gates[0].shape[1]
    depth = chunks * lane
    for side in range(2):
        for m in range(chunks):
            begin = pl.multiple_of(side * depth + (where_ref[2] ^ m) * lane, lane)
            lhs_ref[:, pl.ds(begin, lane)] = gates[side * chunks + m][...]
    weight = weights[0]
    count, cols = weight.shape[0] // 2, weight.shape[2]
    tokens = out_ref.shape[0]
    rows = min(tokens, 256)
    for b in range(count):
        place = ((where_ref[3] ^ half) * count + b) ^ where_ref[4]
        for begin in range(0, tokens, rows):
            out_ref[begin : begin + rows, b * cols : (b + 1) * cols] = jnp.dot(
                lhs_ref[begin : begin + rows, :], weight[place], preferred_element_type=F32
            ).astype(out_ref.dtype)


def final_kernel(embed_ref, own_ref, other_ref, out_ref):
    out_ref[...] = (
        embed_ref[...].astype(F32) + own_ref[...] + other_ref[...].astype(F32)
    ).astype(BF)


def body(
    token_ids, embed_table, norm_gain, in_weight, short_filter, long_filter, long_skip, out_weight
):
    seq, tp = lax.axis_index("seq"), lax.axis_index("tp")
    n, m = lax.axis_size("seq"), lax.axis_size("tp")
    tokens = token_ids.shape[0]
    vocab, width = embed_table.shape
    depth = in_weight.shape[0]
    groups, taps = long_filter.shape
    short_taps = short_filter.shape[0]
    piece = width // n
    chunks = 4
    per_chunk = n // chunks
    halo = 2 * taps
    top = n // 2
    upper = (seq >= top).astype(jnp.int32)
    core, row = tp & 1, tp >> 1

    weight = in_weight.reshape(depth, 3, n, piece).transpose(2, 1, 3, 0).reshape(n, 3 * piece, depth)
    weight = lax.all_to_all(weight, "seq", split_axis=0, concat_axis=0, tiled=True)

    table_row = swap(embed_table, "tp", 2)
    table_core = swap(embed_table, "tp", 1)
    table_both = swap(table_row, "tp", 1)

    tail = lax.ppermute(token_ids[tokens - halo :], "seq", [(i, i + 1) for i in range(n - 1)])
    tail = jnp.where(seq == 0, -1, tail)
    ids = jnp.concatenate([tail, token_ids])[None, :]
    length = tokens + halo

    chunk_at = (seq // per_chunk).astype(jnp.int32)
    same_side = row == upper
    base = jnp.where(same_side, seq, seq ^ top) & (top - 1)
    where = jnp.stack([seq, tp, chunk_at, core, base]).astype(jnp.int32)

    onehot = call(
        onehot_kernel, jax.ShapeDtypeStruct((vocab, length), BF), 1, vocab * length, 2 * vocab * length
    )(ids)
    embedded = call(
        embed_kernel,
        jax.ShapeDtypeStruct((tokens, width), BF),
        2,
        2 * tokens * vocab * width,
        2 * tokens * (vocab + width),
    )(onehot, embed_table)
    bands = call(
        band_kernel,
        jax.ShapeDtypeStruct((groups, 2 * taps, taps), BF),
        1,
        groups * taps * taps * 8,
        groups * taps * taps * 4,
    )(long_filter)
    params = short_filter.reshape(short_taps, 3, n, piece).transpose(2, 1, 3, 0)
    skips = jnp.broadcast_to(long_skip.reshape(n, 1, piece, 1), (n, 3, piece, 1))
    params = jnp.concatenate([params, skips], axis=3).reshape(n, 3 * piece, short_taps + 1)

    normed = call(
        norm_kernel,
        jax.ShapeDtypeStruct((m, vocab, width), BF),
        6,
        8 * m * vocab * width,
        4 * m * vocab * width,
        in_specs=[SCALARS] + [WHOLE] * 5,
    )(where, norm_gain.reshape(m, 1, width), embed_table, table_core, table_row, table_both)

    projected = call(
        project_kernel,
        jax.ShapeDtypeStruct((3 * piece, vocab), BF),
        3,
        2 * 3 * piece * vocab * m * width,
        2 * m * width * (vocab + 3 * piece),
        in_specs=[SCALARS, WHOLE, WHOLE],
    )(where, weight, normed)

    low = []
    bit = 1
    while bit < per_chunk:
        low.append(bit)
        bit *= 2
    first = projected
    second = swap(first, "seq", per_chunk)
    third = swap(first, "seq", 2 * per_chunk)
    fourth = swap(third, "seq", per_chunk)

    gates, row_gates = [], []
    chunk_width = per_chunk * piece
    mixer = functools.partial(mixer_kernel, width // groups, short_taps)
    for index, start in enumerate((first, second, third, fourth)):
        pieces = doubled([start], "seq", low)
        at = jnp.stack([seq, chunk_at ^ index]).astype(jnp.int32)
        inner = chunk_width * groups // width
        gate = pl.pallas_call(
            mixer,
            grid_spec=pltpu.PrefetchScalarGridSpec(
                num_scalar_prefetch=1,
                grid=(1,),
                in_specs=[
                    pl.BlockSpec((vocab, length), lambda i, s: (0, 0)),
                    pl.BlockSpec((per_chunk, 3 * piece, short_taps + 1), lambda i, s: (s[1], 0, 0)),
                    pl.BlockSpec((inner, 2 * taps, taps), lambda i, s: (s[1], 0, 0)),
                ]
                + [pl.BlockSpec((3 * piece, vocab), lambda i, s: (0, 0))] * len(pieces),
                out_specs=pl.BlockSpec((tokens, chunk_width), lambda i, s: (0, 0)),
                scratch_shapes=[
                    pltpu.VMEM((3 * piece, length), F32),
                    pltpu.VMEM((chunk_width, tokens), F32),
                ],
            ),
            out_shape=jax.ShapeDtypeStruct((tokens, chunk_width), BF),
            compiler_params=pltpu.CompilerParams(vmem_limit_bytes=VMEM_LIMIT),
            cost_estimate=pl.CostEstimate(
                flops=2 * 3 * chunk_width * length * vocab,
                bytes_accessed=4 * vocab * length,
                transcendentals=0,
            ),
        )(at, onehot, params, bands, *pieces)
        gates.append(gate)
        row_gates.append(swap(gate, "tp", 2))

    mids = []
    bit = 2
    while bit < top:
        mids.append(bit)
        bit *= 2
    near = doubled([out_weight], "seq", mids)
    far = doubled([swap(out_weight, "seq", top)], "seq", mids)
    near, far = jnp.stack(near), jnp.stack(far)
    kept = jnp.where(same_side, near, far)
    given = swap(jnp.where(same_side, far, near), "tp", 2)
    both = jnp.concatenate([kept, given], axis=1)
    across = swap(both, "seq", 1)
    columns = jnp.stack([both, across], axis=1).reshape(top, 2 * width, out_weight.shape[1])

    def out_part(half, kind):
        count = 2 * chunks
        return call(
            functools.partial(out_kernel, chunks, half),
            jax.ShapeDtypeStruct((tokens, width), kind),
            count + 2,
            2 * tokens * 2 * width * width,
            4 * tokens * width + 4 * width * width,
            in_specs=[SCALARS] + [WHOLE] * (count + 1),
            scratch_shapes=[pltpu.VMEM((tokens, 2 * width), BF)],
        )(where, *gates, *row_gates, columns)

    sent = swap(out_part(1, BF), "tp", 1)
    own = out_part(0, F32)
    return call(
        final_kernel,
        jax.ShapeDtypeStruct((tokens, width), BF),
        3,
        2 * tokens * width,
        8 * tokens * width,
    )(embedded, own, sent)


def solution(mesh):
    placed = (
        P("seq"),
        P(None, "tp"),
        P(),
        P("seq", None, "tp"),
        P(None, None, "tp"),
        P("tp", None),
        P("tp"),
        P("tp", "seq"),
    )
    return jax.shard_map(
        body, mesh=mesh, in_specs=placed, out_specs=P("seq", "tp"), check_vma=False
    )
```

time: 262 us -> 131 us (0.50)
  waiting for transfers between devices: 179 us -> 45.2 us
  matrix products: 35.6 us -> 0 us
  Pallas kernels: 0 us -> 35.5 us
  starting transfers between devices: 7.26 us -> 36 us
  between operations: 13.3 us -> 0.28 us
  other arithmetic: 12.9 us -> 5.12 us
  local copies, waits for them, and re-layouts: 12.7 us -> 7.78 us
    all_gather x3 -> x0, waiting for transfers between devices: 132 us -> none  [the longest x1 98.2 us: body(): lax.all_gather(in_weight, 'seq', axis=0, tiled=True)]
    reduce_scatter x1 -> x0, waiting for transfers between devices: 42.9 us -> none  [body(): lax.psum_scatter(partials.astype(jnp.bfloat16), 'tp', scatter_dimension=1...]
    ppermute x2 -> x21, waiting for transfers between devices: 3.4 us -> 45.2 us  [the longest x20 45.2 us: swap(): return lax.ppermute(block, axis, [(i, i ^ offset) for i in range(count)])]
    dot_general x7 -> x0, matrix products: 35.6 us -> none  [the longest x1 10.5 us: body(): jnp.einsum('td,dsc->tsc', normed, lax.all_gather(in_weight, 'seq', axis=0...]
    pallas_call x0 -> x12, Pallas kernels: none -> 35.5 us  [the longest x4 23.3 us: body(): pl.pallas_call(mixer, grid_spec=pltpu.PrefetchScalarGridSpec(num_scalar_p...]
    ppermute x2 -> x21, starting transfers between devices: 7.14 us -> 32.1 us  [the longest x20 28.7 us: swap(): return lax.ppermute(block, axis, [(i, i ^ offset) for i in range(count)])]
    add x2 -> x0, other arithmetic: 5.61 us -> none  [the longest x1 5.6 us: short_conv(): running + short_filter[tap_index][None] * extended[begin:begin + out_leng...]
    another operation x0 -> x6, other arithmetic: none -> 4.21 us  [the longest x2 3.91 us: body(): jnp.stack([both, across], axis=1)]
  transfers between devices with their start and end apart: 6 -> 22, of which waited for: 6 -> 9; matrix products, arithmetic and copies ran while one was open for 17% -> 6% of each run, Pallas kernels for 0% -> 24%
where the time goes in v1:
time: 131 us; the launch traced here: 130 us
  waiting for transfers between devices  45.2 us (35%)
  starting transfers between devices  36 us (27%)
  Pallas kernels  35.5 us (27%)
  local copies, waits for them, and re-layouts  7.78 us (6%)
  other arithmetic  5.12 us (4%)
    ppermute x20, waiting for transfers between devices, swap(): return lax.ppermute(block, axis, [(i, i ^ offset) for i in range(count)])  45.2 us
    ppermute x20, starting transfers between devices, swap(): return lax.ppermute(block, axis, [(i, i ^ offset) for i in range(count)])  28.7 us
    pallas_call x4, Pallas kernels, body(): pl.pallas_call(mixer, grid_spec=pltpu.PrefetchScalarGridSpec(num_scalar_p...  23.3 us
    unnamed x31, local copies, waits for them, and re-layouts  6.16 us
    pallas_call x2, Pallas kernels, out_part(): call(functools.partial(out_kernel, chunks, half), jax.ShapeDtypeStruct((t...  5.98 us
    all_to_all x1, starting transfers between devices, body(): lax.all_to_all(weight, 'seq', split_axis=0, concat_axis=0, tiled=True)  3.91 us
    another operation x2, other arithmetic, body(): jnp.stack([both, across], axis=1)  3.91 us
    ppermute x1, starting transfers between devices, body(): lax.ppermute(token_ids[tokens - halo:], 'seq', [(i, i + 1) for i in range...  3.38 us
  transfers between devices with their start and end apart: 22, of which 9 were waited for; matrix products, arithmetic and copies ran while one was open for 6% of the time, Pallas kernels for 24%

profile of v1, /device:TPU:0, one launch (start us, length us, event | category | flops | bytes accessed | tf_op | source)
XLA Modules:
  0.0 129.9 jit_solution(14653106983093482908)
XLA Ops:
  0.0 4.0 %collective-permute-start.16 = (bf16[512,256]{1,0:T(8,128)(2,1)}, bf16[512,256]{1,0:T(8,128)(2,1)S(1)}, u32[]{:S(2)}, u32[]{:S(2)}) collective-permute-start(bf16[512,256]{1,0:T(8,128)(2,1)} %param.15), channel_id=1, source_target_pairs={{0,16},{4,20},{8,24},{12,28},{16,0},{20,4},{24,8},{28,12},{1,17},{... | collective-permute-start | bytes 786440 | tf_op jit(solution)/shard_map/ppermute | solution.py:19
  4.0 1.4 %copy.26 = bf16[256,3,512]{0,2,1:T(8,128)(2,1)S(1)} copy(bf16[256,3,512]{2,0,1:T(8,128)(2,1)} %param.11) | data formatting | bytes 1572864 | tf_op args[3]
  5.4 0.9 copy.27
  6.4 3.9 %all-to-all-start = ((bf16[8,192,256]{2,1,0:T(8,128)(2,1)}), bf16[8,192,256]{2,1,0:T(8,128)(2,1)S(1)}, u32[]{:S(2)}, u32[]{:S(2)}) async-start(bf16[8,192,256]{2,1,0:T(8,128)(2,1)} %bitcast.9), calls=%async_computation | async-start | bytes 1572864 | tf_op jit(solution)/shard_map/all_to_all | solution.py:180
  10.3 2.0 %collective-permute-start.15 = (bf16[512,256]{1,0:T(8,128)(2,1)S(1)}, bf16[512,256]{1,0:T(8,128)(2,1)S(1)}, u32[]{:S(2)}, u32[]{:S(2)}) collective-permute-start(bf16[512,256]{1,0:T(8,128)(2,1)S(1)} %copy-done.11), channel_id=1, source_target_pairs={{0,8},{4,12},{8,0},{12,4},{16,24},{20,28},{24,16},{28,20},{1,9},{5... | collective-permute-start | bytes 786440 | tf_op jit(solution)/shard_map/ppermute | solution.py:19
  12.3 6.0 %collective-permute-done.16 = bf16[512,256]{1,0:T(8,128)(2,1)S(1)} collective-permute-done((bf16[512,256]{1,0:T(8,128)(2,1)}, bf16[512,256]{1,0:T(8,128)(2,1)S(1)}, u32[]{:S(2)}, u32[]{:S(2)}) %collective-permute-start.16) | collective-permute-done | bytes 262176 | tf_op jit(solution)/shard_map/ppermute | solution.py:19
  18.3 6.7 %collective-permute-start.17 = (bf16[512,256]{1,0:T(8,128)(2,1)S(1)}, bf16[512,256]{1,0:T(8,128)(2,1)S(1)}, u32[]{:S(2)}, u32[]{:S(2)}) collective-permute-start(bf16[512,256]{1,0:T(8,128)(2,1)S(1)} %collective-permute-done.16), channel_id=1, source_target_pairs={{0,8},{4,12},{8,0},{12,4},{16,24},{20,28},{24,16},{28,20},{1,9},{5... | collective-permute-start | bytes 786440 | tf_op jit(solution)/shard_map/ppermute | solution.py:19
  24.9 1.5 %collective-permute-start.2 = (bf16[512,512]{1,0:T(8,128)(2,1)S(1)}, bf16[512,512]{1,0:T(8,128)(2,1)S(1)}, u32[]{:S(2)}, u32[]{:S(2)}) collective-permute-start(bf16[512,512]{1,0:T(8,128)(2,1)S(1)} %copy-done.1), channel_id=1, source_target_pairs={{0,2},{1,3},{2,0},{3,1},{4,6},{5,7},{6,4},{7,5},{8,10},{9,11},{10,... | collective-permute-start | bytes 1572872 | tf_op jit(solution)/shard_map/ppermute | solution.py:19
  26.5 8.1 %collective-permute-done.15 = bf16[512,256]{1,0:T(8,128)(2,1)S(1)} collective-permute-done((bf16[512,256]{1,0:T(8,128)(2,1)S(1)}, bf16[512,256]{1,0:T(8,128)(2,1)S(1)}, u32[]{:S(2)}, u32[]{:S(2)}) %collective-permute-start.15) | collective-permute-done | bytes 262176 | tf_op jit(solution)/shard_map/ppermute | solution.py:19
  34.6 5.5 %collective-permute-done.17 = bf16[512,256]{1,0:T(8,128)(2,1)S(1)} collective-permute-done((bf16[512,256]{1,0:T(8,128)(2,1)S(1)}, bf16[512,256]{1,0:T(8,128)(2,1)S(1)}, u32[]{:S(2)}, u32[]{:S(2)}) %collective-permute-start.17) | collective-permute-done | bytes 262176 | tf_op jit(solution)/shard_map/ppermute | solution.py:19
  40.1 0.9 broadcast_select_fusion.1
  41.0 1.5 %collective-permute-start.18 = (bf16[2,512,256]{2,1,0:T(8,128)(2,1)}, bf16[2,512,256]{2,1,0:T(8,128)(2,1)}, u32[]{:S(2)}, u32[]{:S(2)}) collective-permute-start(bf16[2,512,256]{2,1,0:T(8,128)(2,1)} %get-tuple-element.8), channel_id=1, source_target_pairs={{0,2},{1,3},{2,0},{3,1},{4,6},{5,7},{6,4},{7,5},{8,10},{9,11},{10,... | collective-permute-start | bytes 1572872 | tf_op jit(solution)/shard_map/ppermute | solution.py:19
  42.5 0.5 collective-permute-start.3
  43.1 3.4 %collective-permute-start = (s32[256]{0:T(256)S(1)}, s32[256]{0:T(256)S(1)}, u32[]{:S(2)}, u32[]{:S(2)}) collective-permute-start(s32[256]{0:T(256)S(1)} %slice.3), channel_id=1, source_target_pairs={{0,4},{4,8},{8,12},{12,16},{16,20},{20,24},{24,28},{1,5},{5,9},{9,... | collective-permute-start | bytes 3080 | tf_op jit(solution)/shard_map/ppermute | solution.py:186
  46.5 8.6 %collective-permute-done.18 = bf16[2,512,256]{2,1,0:T(8,128)(2,1)} collective-permute-done((bf16[2,512,256]{2,1,0:T(8,128)(2,1)}, bf16[2,512,256]{2,1,0:T(8,128)(2,1)}, u32[]{:S(2)}, u32[]{:S(2)}) %collective-permute-start.18) | collective-permute-done | bytes 524320 | tf_op jit(solution)/shard_map/ppermute | solution.py:19
  55.2 2.5 %fusion = (bf16[2,1,1024,256]{3,2,0,1:T(8,128)(2,1)}, bf16[2,1024,256]{2,1,0:T(8,128)(2,1)}) fusion(bf16[2,512,256]{2,1,0:T(8,128)(2,1)} %collective-permute-done.18, bf16[2,512,256]{2,1,0:T(8,128)(2,1)S(1)} %get-tuple-element.7), kind=kLoop, calls=%fused_computation.13 | loop fusion | flops 2097152 | bytes 3145728 | tf_op jit(solution)/shard_map/stack | solution.py:292
  57.7 1.5 %collective-permute-start.19 = (bf16[2,1024,256]{2,1,0:T(8,128)(2,1)}, bf16[2,1024,256]{2,1,0:T(8,128)(2,1)}, u32[]{:S(2)}, u32[]{:S(2)}) collective-permute-start(bf16[2,1024,256]{2,1,0:T(8,128)(2,1)} %get-tuple-element.6), channel_id=1, source_target_pairs={{0,4},{4,0},{8,12},{12,8},{16,20},{20,16},{24,28},{28,24},{1,5},{5... | collective-permute-start | bytes 3145736 | tf_op jit(solution)/shard_map/ppermute | solution.py:19
  59.5 0.8 copy-done.4
  60.3 0.8 copy-done.6
  61.1 1.0 copy-done.3
  62.2 1.0 copy-done.5
  63.2 1.0 copy-done.7
  64.2 1.5 %shard_map.85.normed_ref = bf16[4,512,512]{2,1,0:T(8,128)(2,1)S(1)} custom-call(s32[5]{0:T(128)S(1)} %stack.76.where_ref, f32[4,1,512]{2,1,0:T(1,128)S(1)} %bitcast.31, bf16[512,512]{1,0:T(8,128)(2,1)S(1)} %copy-done.1, bf16[512,512]{1,0:T(8,128)(2,1)S(1)} %copy-done.5, bf16[512,512]{1,0:T(8,128)(2,1)S(1)} %copy-done.3, bf16[512,512]{1,0:T(8,128)(2,1)S(1)} %copy-done.7), custom_call_target="tpu_custom_call" | custom-call | flops 8388608 | bytes 4194304 | tf_op jit(solution)/shard_map/pallas_call | solution.py:217
  65.8 2.0 %shard_map.86.refs_0_ = bf16[192,512]{1,0:T(8,128)(2,1)} custom-call(s32[5]{0:T(128)S(1)} %stack.76.where_ref, bf16[8,192,256]{2,1,0:T(8,128)(2,1)S(1)} %all-to-all-done.weight_ref, bf16[4,512,512]{2,1,0:T(8,128)(2,1)S(1)} %shard_map.85.normed_ref), custom_call_target="tpu_custom_call" | custom-call | flops 402653184 | bytes 2883584 | tf_op jit(solution)/shard_map/pallas_call | solution.py:226
  67.8 0.4 collective-permute-start.7
  68.4 0.3 copy.25
  68.7 0.4 shard_map.84.band_ref
  69.1 2.5 %collective-permute-start.5 = (bf16[192,512]{1,0:T(8,128)(2,1)}, bf16[192,512]{1,0:T(8,128)(2,1)S(1)}, u32[]{:S(2)}, u32[]{:S(2)}) collective-permute-start(bf16[192,512]{1,0:T(8,128)(2,1)} %shard_map.86.refs_0_), channel_id=1, source_target_pairs={{0,8},{4,12},{8,0},{12,4},{16,24},{20,28},{24,16},{28,20},{1,9},{5... | collective-permute-start | bytes 589832 | tf_op jit(solution)/shard_map/ppermute | solution.py:19
  71.6 1.7 %collective-permute-start.4 = (bf16[192,512]{1,0:T(8,128)(2,1)}, bf16[192,512]{1,0:T(8,128)(2,1)S(1)}, u32[]{:S(2)}, u32[]{:S(2)}) collective-permute-start(bf16[192,512]{1,0:T(8,128)(2,1)} %shard_map.86.refs_0_), channel_id=1, source_target_pairs={{0,4},{4,0},{8,12},{12,8},{16,20},{20,16},{24,28},{28,24},{1,5},{5... | collective-permute-start | bytes 589832 | tf_op jit(solution)/shard_map/ppermute | solution.py:19
  73.3 5.3 %collective-permute-done.7.refs_0_ = bf16[192,512]{1,0:T(8,128)(2,1)S(1)} collective-permute-done((bf16[192,512]{1,0:T(8,128)(2,1)}, bf16[192,512]{1,0:T(8,128)(2,1)S(1)}, u32[]{:S(2)}, u32[]{:S(2)}) %collective-permute-start.7) | collective-permute-done | bytes 196640 | tf_op jit(solution)/shard_map/ppermute | solution.py:19
  78.6 0.9 collective-permute-start.8
  79.6 1.0 collective-permute-start.6
  80.6 4.7 %collective-permute-done.9.refs_0_ = bf16[192,512]{1,0:T(8,128)(2,1)S(1)} collective-permute-done((bf16[192,512]{1,0:T(8,128)(2,1)S(1)}, bf16[192,512]{1,0:T(8,128)(2,1)S(1)}, u32[]{:S(2)}, u32[]{:S(2)}) %collective-permute-start.9) | collective-permute-done | bytes 196640 | tf_op jit(solution)/shard_map/ppermute | solution.py:19
  85.6 2.6 %collective-permute-done.4.refs_1_ = bf16[192,512]{1,0:T(8,128)(2,1)S(1)} collective-permute-done((bf16[192,512]{1,0:T(8,128)(2,1)}, bf16[192,512]{1,0:T(8,128)(2,1)S(1)}, u32[]{:S(2)}, u32[]{:S(2)}) %collective-permute-start.4) | collective-permute-done | bytes 196640 | tf_op jit(solution)/shard_map/ppermute | solution.py:19
  88.2 6.4 %shard_map.87.refs_0_ = bf16[1024,128]{1,0:T(8,128)(2,1)S(1)} custom-call(s32[2]{0:T(128)S(1)} %pad_add_fusion.1.where_ref, bf16[512,1280]{1,0:T(8,128)(2,1)S(1)} %shard_map.82.onehot_ref, f32[8,192,8]{2,1,0:T(8,128)S(1)} %bitcast.25, bf16[32,256,128]{2,1,0:T(8,128)(2,1)S(1)} %shard_map.84.band_ref, bf16[192,512]{1,0:T(8,128)(2,1)} %shard_map.86.refs_0_, ...), custom_call_target="tpu_custom_call" | custom-call | flops 503316480 | bytes 2621440 | tf_op jit(solution)/shard_map/pallas_call | solution.py:252
  94.6 1.6 %collective-permute-start.11 = (bf16[1024,128]{1,0:T(8,128)(2,1)S(1)}, bf16[1024,128]{1,0:T(8,128)(2,1)S(1)}, u32[]{:S(2)}, u32[]{:S(2)}) collective-permute-start(bf16[1024,128]{1,0:T(8,128)(2,1)S(1)} %shard_map.87.refs_0_), channel_id=1, source_target_pairs={{0,2},{1,3},{2,0},{3,1},{4,6},{5,7},{6,4},{7,5},{8,10},{9,11},{10,... | collective-permute-start | bytes 786440 | tf_op jit(solution)/shard_map/ppermute | solution.py:19
  96.2 5.6 %shard_map.89.refs_2_ = bf16[1024,128]{1,0:T(8,128)(2,1)S(1)} custom-call(s32[2]{0:T(128)S(1)} %pad_add_fusion.3.where_ref, bf16[512,1280]{1,0:T(8,128)(2,1)S(1)} %shard_map.82.onehot_ref, f32[8,192,8]{2,1,0:T(8,128)S(1)} %bitcast.26, bf16[32,256,128]{2,1,0:T(8,128)(2,1)S(1)} %shard_map.84.band_ref, bf16[192,512]{1,0:T(8,128)(2,1)S(1)} %collective-permute-done.7.refs_0_, ...), custom_call_target="tpu_custom_call" | custom-call | flops 503316480 | bytes 2621440 | tf_op jit(solution)/shard_map/pallas_call | solution.py:252
  101.8 0.6 collective-permute-start.13
  102.4 5.7 %shard_map.88.refs_1_ = bf16[1024,128]{1,0:T(8,128)(2,1)S(1)} custom-call(s32[2]{0:T(128)S(1)} %pad_add_fusion.2.where_ref, bf16[512,1280]{1,0:T(8,128)(2,1)S(1)} %shard_map.82.onehot_ref, f32[8,192,8]{2,1,0:T(8,128)S(1)} %bitcast.27, bf16[32,256,128]{2,1,0:T(8,128)(2,1)S(1)} %shard_map.84.band_ref, bf16[192,512]{1,0:T(8,128)(2,1)S(1)} %collective-permute-done.5.refs_0_, ...), custom_call_target="tpu_custom_call" | custom-call | flops 503316480 | bytes 2621440 | tf_op jit(solution)/shard_map/pallas_call | solution.py:252
  108.1 1.6 %collective-permute-start.12 = (bf16[1024,128]{1,0:T(8,128)(2,1)S(1)}, bf16[1024,128]{1,0:T(8,128)(2,1)S(1)}, u32[]{:S(2)}, u32[]{:S(2)}) collective-permute-start(bf16[1024,128]{1,0:T(8,128)(2,1)S(1)} %shard_map.88.refs_1_), channel_id=1, source_target_pairs={{0,2},{1,3},{2,0},{3,1},{4,6},{5,7},{6,4},{7,5},{8,10},{9,11},{10,... | collective-permute-start | bytes 786440 | tf_op jit(solution)/shard_map/ppermute | solution.py:19
  109.7 5.6 %shard_map.90.refs_3_ = bf16[1024,128]{1,0:T(8,128)(2,1)S(1)} custom-call(s32[2]{0:T(128)S(1)} %pad_add_fusion.4.where_ref, bf16[512,1280]{1,0:T(8,128)(2,1)S(1)} %shard_map.82.onehot_ref, f32[8,192,8]{2,1,0:T(8,128)S(1)} %bitcast.28, bf16[32,256,128]{2,1,0:T(8,128)(2,1)S(1)} %shard_map.84.band_ref, bf16[192,512]{1,0:T(8,128)(2,1)S(1)} %collective-permute-done.9.refs_0_, ...), custom_call_target="tpu_custom_call" | custom-call | flops 503316480 | bytes 2621440 | tf_op jit(solution)/shard_map/pallas_call | solution.py:252
  115.3 0.6 collective-permute-start.14
  115.9 1.4 %pad_maximum_fusion = bf16[2,2,1024,256]{3,2,0,1:T(8,128)(2,1)S(1)} fusion(bf16[2,1,1024,256]{3,2,0,1:T(8,128)(2,1)} %bitcast.19, bf16[2,1,1024,256]{3,2,0,1:T(8,128)(2,1)S(1)} %copy-done.10), kind=kLoop, calls=%fused_computation | loop fusion | flops 1048576 | bytes 4194304 | tf_op jit(solution)/shard_map/stack | solution.py:292
  117.5 4.2 %collective-permute-done.14.refs_7_ = bf16[1024,128]{1,0:T(8,128)(2,1)S(1)} collective-permute-done((bf16[1024,128]{1,0:T(8,128)(2,1)S(1)}, bf16[1024,128]{1,0:T(8,128)(2,1)S(1)}, u32[]{:S(2)}, u32[]{:S(2)}) %collective-permute-start.14) | collective-permute-done | bytes 262176 | tf_op jit(solution)/shard_map/ppermute | solution.py:19
  121.7 2.5 %shard_map.92 = bf16[1024,512]{1,0:T(8,128)(2,1)S(1)} custom-call(s32[5]{0:T(128)S(1)} %stack.76.where_ref, bf16[1024,128]{1,0:T(8,128)(2,1)S(1)} %shard_map.87.refs_0_, bf16[1024,128]{1,0:T(8,128)(2,1)S(1)} %shard_map.88.refs_1_, bf16[1024,128]{1,0:T(8,128)(2,1)S(1)} %shard_map.89.refs_2_, bf16[1024,128]{1,0:T(8,128)(2,1)S(1)} %shard_map.90.refs_3_, ...), custom_call_target="tpu_custom_call" | custom-call | flops 1073741824 | bytes 3145728 | tf_op jit(solution)/shard_map/pallas_call | solution.py:296
  124.3 0.7 shard_map.83.embed_ref
  125.0 3.5 %shard_map.91.own_ref = f32[1024,512]{1,0:T(8,128)S(1)} custom-call(s32[5]{0:T(128)S(1)} %stack.76.where_ref, bf16[1024,128]{1,0:T(8,128)(2,1)S(1)} %shard_map.87.refs_0_, bf16[1024,128]{1,0:T(8,128)(2,1)S(1)} %shard_map.88.refs_1_, bf16[1024,128]{1,0:T(8,128)(2,1)S(1)} %shard_map.89.refs_2_, bf16[1024,128]{1,0:T(8,128)(2,1)S(1)} %shard_map.90.refs_3_, ...), custom_call_target="tpu_custom_call" | custom-call | flops 1073741824 | bytes 3145728 | tf_op jit(solution)/shard_map/pallas_call | solution.py:296
  128.6 1.4 %shard_map.93 = bf16[1024,512]{1,0:T(8,128)(2,1)} custom-call(bf16[1024,512]{1,0:T(8,128)(2,1)S(1)} %shard_map.83.embed_ref, f32[1024,512]{1,0:T(8,128)S(1)} %shard_map.91.own_ref, bf16[1024,512]{1,0:T(8,128)(2,1)S(1)} %collective-permute-done.20.other_ref), custom_call_target="tpu_custom_call" | custom-call | flops 1048576 | bytes 4194304 | tf_op jit(solution)/shard_map/pallas_call | solution.py:308
  (58 shorter events, 1.2 us)
Async XLA Ops:
  0.0 10.3 %copy-start.11 = (bf16[512,256]{1,0:T(8,128)(2,1)S(1)}, bf16[512,256]{1,0:T(8,128)(2,1)}, u32[]{:S(2)}) copy-start(bf16[512,256]{1,0:T(8,128)(2,1)} %param.15) | copy-start | bytes 786436
  0.0 24.9 %copy-start.1 = (bf16[512,512]{1,0:T(8,128)(2,1)S(1)}, bf16[512,512]{1,0:T(8,128)(2,1)}, u32[]{:S(2)}) copy-start(bf16[512,512]{1,0:T(8,128)(2,1)} %refs_0_.1) | copy-start | bytes 1572868
  0.0 18.3 %collective-permute-start.16 = (bf16[512,256]{1,0:T(8,128)(2,1)}, bf16[512,256]{1,0:T(8,128)(2,1)S(1)}, u32[]{:S(2)}, u32[]{:S(2)}) collective-permute-start(bf16[512,256]{1,0:T(8,128)(2,1)} %param.15), channel_id=1, source_target_pairs={{0,16},{4,20},{8,24},{12,28},{16,0},{20,4},{24,8},{28,12},{1,17},{... | collective-permute-start | bytes 786440 | tf_op jit(solution)/shard_map/ppermute | solution.py:19
  6.4 36.7 %copy-start.13 = (s32[1024]{0:T(1024)S(1)}, s32[1024]{0:T(1024)}, u32[]{:S(2)}) copy-start(s32[1024]{0:T(1024)} %param.8) | copy-start | bytes 12292
  6.4 59.4 %all-to-all-start = ((bf16[8,192,256]{2,1,0:T(8,128)(2,1)}), bf16[8,192,256]{2,1,0:T(8,128)(2,1)S(1)}, u32[]{:S(2)}, u32[]{:S(2)}) async-start(bf16[8,192,256]{2,1,0:T(8,128)(2,1)} %bitcast.9), calls=%async_computation | async-start | bytes 1572864 | tf_op jit(solution)/shard_map/all_to_all | solution.py:180
  10.3 24.3 %collective-permute-start.15 = (bf16[512,256]{1,0:T(8,128)(2,1)S(1)}, bf16[512,256]{1,0:T(8,128)(2,1)S(1)}, u32[]{:S(2)}, u32[]{:S(2)}) collective-permute-start(bf16[512,256]{1,0:T(8,128)(2,1)S(1)} %copy-done.11), channel_id=1, source_target_pairs={{0,8},{4,12},{8,0},{12,4},{16,24},{20,28},{24,16},{28,20},{1,9},{5... | collective-permute-start | bytes 786440 | tf_op jit(solution)/shard_map/ppermute | solution.py:19
  18.3 21.8 %collective-permute-start.17 = (bf16[512,256]{1,0:T(8,128)(2,1)S(1)}, bf16[512,256]{1,0:T(8,128)(2,1)S(1)}, u32[]{:S(2)}, u32[]{:S(2)}) collective-permute-start(bf16[512,256]{1,0:T(8,128)(2,1)S(1)} %collective-permute-done.16), channel_id=1, source_target_pairs={{0,8},{4,12},{8,0},{12,4},{16,24},{20,28},{24,16},{28,20},{1,9},{5... | collective-permute-start | bytes 786440 | tf_op jit(solution)/shard_map/ppermute | solution.py:19
  24.9 17.6 %collective-permute-start.2 = (bf16[512,512]{1,0:T(8,128)(2,1)S(1)}, bf16[512,512]{1,0:T(8,128)(2,1)S(1)}, u32[]{:S(2)}, u32[]{:S(2)}) collective-permute-start(bf16[512,512]{1,0:T(8,128)(2,1)S(1)} %copy-done.1), channel_id=1, source_target_pairs={{0,2},{1,3},{2,0},{3,1},{4,6},{5,7},{6,4},{7,5},{8,10},{9,11},{10,... | collective-permute-start | bytes 1572872 | tf_op jit(solution)/shard_map/ppermute | solution.py:19
  41.0 18.2 %copy-start.12 = (f32[7,3,512]{2,0,1:T(8,128)S(1)}, f32[7,3,512]{2,0,1:T(8,128)}, u32[]{:S(2)}) copy-start(f32[7,3,512]{2,0,1:T(8,128)} %param.12) | copy-start | bytes 129028
  41.0 18.3 %copy-start.14 = (f32[512]{0:T(512)S(1)}, f32[512]{0:T(512)}, u32[]{:S(2)}) copy-start(f32[512]{0:T(512)} %param.14) | copy-start | bytes 6148
  41.0 20.1 %copy-start.8 = (f32[2048]{0:T(1024)S(1)}, f32[2048]{0:T(1024)}, u32[]{:S(2)}) copy-start(f32[2048]{0:T(1024)} %param.10) | copy-start | bytes 24580
  41.0 14.2 %collective-permute-start.18 = (bf16[2,512,256]{2,1,0:T(8,128)(2,1)}, bf16[2,512,256]{2,1,0:T(8,128)(2,1)}, u32[]{:S(2)}, u32[]{:S(2)}) collective-permute-start(bf16[2,512,256]{2,1,0:T(8,128)(2,1)} %get-tuple-element.8), channel_id=1, source_target_pairs={{0,2},{1,3},{2,0},{3,1},{4,6},{5,7},{6,4},{7,5},{8,10},{9,11},{10,... | collective-permute-start | bytes 1572872 | tf_op jit(solution)/shard_map/ppermute | solution.py:19
  42.5 17.0 %collective-permute-start.1 = (bf16[512,512]{1,0:T(8,128)(2,1)S(1)}, bf16[512,512]{1,0:T(8,128)(2,1)S(1)}, u32[]{:S(2)}, u32[]{:S(2)}) collective-permute-start(bf16[512,512]{1,0:T(8,128)(2,1)S(1)} %copy-done.1), channel_id=1, source_target_pairs={{0,1},{1,0},{2,3},{3,2},{4,5},{5,4},{6,7},{7,6},{8,9},{9,8},{10,11... | collective-permute-start | bytes 1572872 | tf_op jit(solution)/shard_map/ppermute | solution.py:19
  42.5 17.8 %copy-start.2 = (bf16[512,512]{1,0:T(8,128)(2,1)}, bf16[512,512]{1,0:T(8,128)(2,1)S(1)}, u32[]{:S(2)}) copy-start(bf16[512,512]{1,0:T(8,128)(2,1)S(1)} %collective-permute-done.2.refs_2_) | copy-start | bytes 1572868
  42.5 17.8 %collective-permute-start.3 = (bf16[512,512]{1,0:T(8,128)(2,1)S(1)}, bf16[512,512]{1,0:T(8,128)(2,1)S(1)}, u32[]{:S(2)}, u32[]{:S(2)}) collective-permute-start(bf16[512,512]{1,0:T(8,128)(2,1)S(1)} %collective-permute-done.2.refs_2_), channel_id=1, source_target_pairs={{0,1},{1,0},{2,3},{3,2},{4,5},{5,4},{6,7},{7,6},{8,9},{9,8},{10,11... | collective-permute-start | bytes 1572872 | tf_op jit(solution)/shard_map/ppermute | solution.py:19
  43.1 35.5 %collective-permute-start = (s32[256]{0:T(256)S(1)}, s32[256]{0:T(256)S(1)}, u32[]{:S(2)}, u32[]{:S(2)}) collective-permute-start(s32[256]{0:T(256)S(1)} %slice.3), channel_id=1, source_target_pairs={{0,4},{4,8},{8,12},{12,16},{16,20},{20,24},{24,28},{1,5},{5,9},{9,... | collective-permute-start | bytes 3080 | tf_op jit(solution)/shard_map/ppermute | solution.py:186
  57.7 58.2 %collective-permute-start.19 = (bf16[2,1024,256]{2,1,0:T(8,128)(2,1)}, bf16[2,1024,256]{2,1,0:T(8,128)(2,1)}, u32[]{:S(2)}, u32[]{:S(2)}) collective-permute-start(bf16[2,1024,256]{2,1,0:T(8,128)(2,1)} %get-tuple-element.6), channel_id=1, source_target_pairs={{0,4},{4,0},{8,12},{12,8},{16,20},{20,16},{24,28},{28,24},{1,5},{5... | collective-permute-start | bytes 3145736 | tf_op jit(solution)/shard_map/ppermute | solution.py:19
  59.5 0.8 copy-start.4
  60.3 0.8 copy-start.6
  61.1 1.0 copy-start.3
  62.2 1.0 copy-start.5
  63.2 1.0 copy-start.7
  65.7 3.0 %copy-start.9 = (bf16[32,128]{1,0:T(8,128)(2,1)S(1)}, bf16[32,128]{1,0:T(8,128)(2,1)}, u32[]{:S(2)}) copy-start(bf16[32,128]{1,0:T(8,128)(2,1)} %filter_ref.1) | copy-start | bytes 24580
  67.8 10.7 %collective-permute-start.7 = (bf16[192,512]{1,0:T(8,128)(2,1)}, bf16[192,512]{1,0:T(8,128)(2,1)S(1)}, u32[]{:S(2)}, u32[]{:S(2)}) collective-permute-start(bf16[192,512]{1,0:T(8,128)(2,1)} %shard_map.86.refs_0_), channel_id=1, source_target_pairs={{0,16},{4,20},{8,24},{12,28},{16,0},{20,4},{24,8},{28,12},{1,17},{... | collective-permute-start | bytes 589832 | tf_op jit(solution)/shard_map/ppermute | solution.py:19
  69.1 10.5 %collective-permute-start.5 = (bf16[192,512]{1,0:T(8,128)(2,1)}, bf16[192,512]{1,0:T(8,128)(2,1)S(1)}, u32[]{:S(2)}, u32[]{:S(2)}) collective-permute-start(bf16[192,512]{1,0:T(8,128)(2,1)} %shard_map.86.refs_0_), channel_id=1, source_target_pairs={{0,8},{4,12},{8,0},{12,4},{16,24},{20,28},{24,16},{28,20},{1,9},{5... | collective-permute-start | bytes 589832 | tf_op jit(solution)/shard_map/ppermute | solution.py:19
  71.6 16.6 %collective-permute-start.4 = (bf16[192,512]{1,0:T(8,128)(2,1)}, bf16[192,512]{1,0:T(8,128)(2,1)S(1)}, u32[]{:S(2)}, u32[]{:S(2)}) collective-permute-start(bf16[192,512]{1,0:T(8,128)(2,1)} %shard_map.86.refs_0_), channel_id=1, source_target_pairs={{0,4},{4,0},{8,12},{12,8},{16,20},{20,16},{24,28},{28,24},{1,5},{5... | collective-permute-start | bytes 589832 | tf_op jit(solution)/shard_map/ppermute | solution.py:19
  78.6 6.8 %collective-permute-start.9 = (bf16[192,512]{1,0:T(8,128)(2,1)S(1)}, bf16[192,512]{1,0:T(8,128)(2,1)S(1)}, u32[]{:S(2)}, u32[]{:S(2)}) collective-permute-start(bf16[192,512]{1,0:T(8,128)(2,1)S(1)} %collective-permute-done.7.refs_0_), channel_id=1, source_target_pairs={{0,8},{4,12},{8,0},{12,4},{16,24},{20,28},{24,16},{28,20},{1,9},{5... | collective-permute-start | bytes 589832 | tf_op jit(solution)/shard_map/ppermute | solution.py:19
  78.6 17.7 %collective-permute-start.8 = (bf16[192,512]{1,0:T(8,128)(2,1)S(1)}, bf16[192,512]{1,0:T(8,128)(2,1)S(1)}, u32[]{:S(2)}, u32[]{:S(2)}) collective-permute-start(bf16[192,512]{1,0:T(8,128)(2,1)S(1)} %collective-permute-done.7.refs_0_), channel_id=1, source_target_pairs={{0,4},{4,0},{8,12},{12,8},{16,20},{20,16},{24,28},{28,24},{1,5},{5... | collective-permute-start | bytes 589832 | tf_op jit(solution)/shard_map/ppermute | solution.py:19
  79.6 22.8 %collective-permute-start.6 = (bf16[192,512]{1,0:T(8,128)(2,1)S(1)}, bf16[192,512]{1,0:T(8,128)(2,1)S(1)}, u32[]{:S(2)}, u32[]{:S(2)}) collective-permute-start(bf16[192,512]{1,0:T(8,128)(2,1)S(1)} %collective-permute-done.5.refs_0_), channel_id=1, source_target_pairs={{0,4},{4,0},{8,12},{12,8},{16,20},{20,16},{24,28},{28,24},{1,5},{5... | collective-permute-start | bytes 589832 | tf_op jit(solution)/shard_map/ppermute | solution.py:19
  85.3 24.4 %collective-permute-start.10 = (bf16[192,512]{1,0:T(8,128)(2,1)S(1)}, bf16[192,512]{1,0:T(8,128)(2,1)S(1)}, u32[]{:S(2)}, u32[]{:S(2)}) collective-permute-start(bf16[192,512]{1,0:T(8,128)(2,1)S(1)} %collective-permute-done.9.refs_0_), channel_id=1, source_target_pairs={{0,4},{4,0},{8,12},{12,8},{16,20},{20,16},{24,28},{28,24},{1,5},{5... | collective-permute-start | bytes 589832 | tf_op jit(solution)/shard_map/ppermute | solution.py:19
  94.6 22.8 %collective-permute-start.11 = (bf16[1024,128]{1,0:T(8,128)(2,1)S(1)}, bf16[1024,128]{1,0:T(8,128)(2,1)S(1)}, u32[]{:S(2)}, u32[]{:S(2)}) collective-permute-start(bf16[1024,128]{1,0:T(8,128)(2,1)S(1)} %shard_map.87.refs_0_), channel_id=1, source_target_pairs={{0,2},{1,3},{2,0},{3,1},{4,6},{5,7},{6,4},{7,5},{8,10},{9,11},{10,... | collective-permute-start | bytes 786440 | tf_op jit(solution)/shard_map/ppermute | solution.py:19
  101.8 15.7 %collective-permute-start.13 = (bf16[1024,128]{1,0:T(8,128)(2,1)S(1)}, bf16[1024,128]{1,0:T(8,128)(2,1)S(1)}, u32[]{:S(2)}, u32[]{:S(2)}) collective-permute-start(bf16[1024,128]{1,0:T(8,128)(2,1)S(1)} %shard_map.89.refs_2_), channel_id=1, source_target_pairs={{0,2},{1,3},{2,0},{3,1},{4,6},{5,7},{6,4},{7,5},{8,10},{9,11},{10,... | collective-permute-start | bytes 786440 | tf_op jit(solution)/shard_map/ppermute | solution.py:19
  108.1 7.7 %copy-start.10 = (bf16[2,1,1024,256]{3,2,0,1:T(8,128)(2,1)S(1)}, bf16[2,1,1024,256]{3,2,0,1:T(8,128)(2,1)}, u32[]{:S(2)}) copy-start(bf16[2,1,1024,256]{3,2,0,1:T(8,128)(2,1)} %get-tuple-element.5) | copy-start | bytes 3145732
  108.1 9.3 %collective-permute-start.12 = (bf16[1024,128]{1,0:T(8,128)(2,1)S(1)}, bf16[1024,128]{1,0:T(8,128)(2,1)S(1)}, u32[]{:S(2)}, u32[]{:S(2)}) collective-permute-start(bf16[1024,128]{1,0:T(8,128)(2,1)S(1)} %shard_map.88.refs_1_), channel_id=1, source_target_pairs={{0,2},{1,3},{2,0},{3,1},{4,6},{5,7},{6,4},{7,5},{8,10},{9,11},{10,... | collective-permute-start | bytes 786440 | tf_op jit(solution)/shard_map/ppermute | solution.py:19
  115.3 6.4 %collective-permute-start.14 = (bf16[1024,128]{1,0:T(8,128)(2,1)S(1)}, bf16[1024,128]{1,0:T(8,128)(2,1)S(1)}, u32[]{:S(2)}, u32[]{:S(2)}) collective-permute-start(bf16[1024,128]{1,0:T(8,128)(2,1)S(1)} %shard_map.90.refs_3_), channel_id=1, source_target_pairs={{0,2},{1,3},{2,0},{3,1},{4,6},{5,7},{6,4},{7,5},{8,10},{9,11},{10,... | collective-permute-start | bytes 786440 | tf_op jit(solution)/shard_map/ppermute | solution.py:19
  117.4 6.8 %copy-start = (bf16[2,2,1024,256]{3,2,1,0:T(8,128)(2,1)}, bf16[2,2,1024,256]{3,2,1,0:T(8,128)(2,1)S(1)}, u32[]{:S(2)}) copy-start(bf16[2,2,1024,256]{3,2,1,0:T(8,128)(2,1)S(1)} %copy.28) | copy-start | bytes 6291460
  124.2 4.3 %collective-permute-start.20 = (bf16[1024,512]{1,0:T(8,128)(2,1)S(1)}, bf16[1024,512]{1,0:T(8,128)(2,1)S(1)}, u32[]{:S(2)}, u32[]{:S(2)}) collective-permute-start(bf16[1024,512]{1,0:T(8,128)(2,1)S(1)} %shard_map.92), channel_id=1, source_target_pairs={{0,1},{1,0},{2,3},{3,2},{4,5},{5,4},{6,7},{7,6},{8,9},{9,8},{10,11... | collective-permute-start | bytes 3145736 | tf_op jit(solution)/shard_map/ppermute | solution.py:19

commit v2 on v0

v2 whole, which is shorter than its diff:
```python
import functools

import jax
import jax.numpy as jnp
from jax import lax
from jax.experimental import pallas as pl
from jax.experimental.pallas import tpu as pltpu
from jax.sharding import PartitionSpec as P

BF = jnp.bfloat16
F32 = jnp.float32
MIB = 1024 * 1024
WHOLE = pl.BlockSpec(memory_space=pltpu.VMEM)
SCALARS = pl.BlockSpec(memory_space=pltpu.SMEM)


def swap(block, axis, offset):
    count = lax.axis_size(axis)
    return lax.ppermute(block, axis, [(i, i ^ offset) for i in range(count)])


def cost_us(time):
    return int(time * 1.1e9)


def call(kernel, out_shape, count, flops, moved, room=12, **more):
    return pl.pallas_call(
        kernel,
        out_shape=out_shape,
        in_specs=more.pop("in_specs", [WHOLE] * count),
        compiler_params=pltpu.CompilerParams(vmem_limit_bytes=room * MIB),
        cost_estimate=pl.CostEstimate(flops=flops, bytes_accessed=moved, transcendentals=0),
        **more,
    )


def after(value, *earlier):
    return lax.optimization_barrier((value, earlier))[0]


def turn_kernel(where_ref, weight_ref, *refs):
    out_refs, turned_ref = refs[:-1], refs[-1]
    top = len(out_refs)
    rows = out_refs[0].shape[1]
    piece = rows // 3
    for s in range(3):
        turned_ref[...] = weight_ref[s].astype(F32).T.astype(BF).reshape(turned_ref.shape)
        for offset, out_ref in enumerate(out_refs):
            for far in range(2):
                place = where_ref[0] ^ (offset + far * top)
                out_ref[far, s * piece : (s + 1) * piece, :] = turned_ref[place]


def onehot(ids, vocab):
    entries = lax.broadcasted_iota(jnp.int32, (ids.shape[0], vocab), 1)
    return (entries == ids).astype(F32).astype(BF)


def embed_kernel(ids_ref, table_ref, out_ref):
    halo = ids_ref.shape[0] - out_ref.shape[0]
    out_ref[...] = jnp.dot(
        onehot(ids_ref[halo:, :], table_ref.shape[0]), table_ref[...], preferred_element_type=F32
    ).astype(BF)


def band_kernel(filter_ref, out_ref):
    groups, taps = filter_ref.shape
    row = lax.broadcasted_iota(jnp.int32, (taps, taps), 0)
    col = lax.broadcasted_iota(jnp.int32, (taps, taps), 1)
    for g in range(groups):
        line = jnp.broadcast_to(filter_ref[g : g + 1, :].astype(F32), (taps, taps))
        ring = pltpu.roll(line, 0, 1, stride=1, stride_axis=0)
        out_ref[g, :taps, :] = jnp.where(col < row, ring, 0.0).astype(BF)
        out_ref[g, taps:, :] = jnp.where(col >= row, ring, 0.0).astype(BF)


def norm_kernel(where_ref, gain_ref, *refs):
    blocks, out_ref, kept_ref, sem = refs[:-3], refs[-3], refs[-2], refs[-1]
    pieces, _, depth = out_ref.shape
    each = pieces // len(blocks)
    total = 0.0
    for block in blocks:
        wide = block[...].astype(F32)
        total = total + jnp.sum(wide * wide, axis=1, keepdims=True)
    scale = lax.rsqrt(total / (len(blocks) * blocks[0].shape[1]) + 1e-06)
    for j, block in enumerate(blocks):
        place = where_ref[1] ^ j
        result = (block[...].astype(F32) * scale * gain_ref[place]).astype(BF)
        for r in range(each):
            kept_ref[place * each + r] = result[:, r * depth : (r + 1) * depth]
    copy = pltpu.make_async_copy(kept_ref, out_ref, sem)
    copy.start()
    copy.wait()


def project_kernel(where_ref, normed_ref, crossing_ref, *refs):
    parts, out_ref, kept_ref, sem = refs[:-3], refs[-3], refs[-2], refs[-1]
    top = len(parts)
    copy = pltpu.make_async_copy(normed_ref, kept_ref, sem)
    copy.start()
    copy.wait()
    total = jnp.zeros(out_ref.shape, F32)
    for offset in range(2 * top):
        weight = parts[offset][0] if offset < top else crossing_ref[offset - top]
        total = total + lax.dot_general(
            weight,
            kept_ref[where_ref[0] ^ offset],
            (((1,), (1,)), ((), ())),
            preferred_element_type=F32,
        )
    out_ref[...] = total.astype(BF)


def mixer_kernel(
    group_size, where_ref, ids_ref, short_ref, skip_ref, band_ref, *refs
):
    pieces = refs[:-6]
    out_ref, rows_ref, proj_ref, product_ref, turned_ref, conv_ref = refs[-6:]
    tokens, width = out_ref.shape
    short_taps = short_ref.shape[0]
    taps = band_ref.shape[2]
    length, vocab = ids_ref.shape[0], rows_ref.shape[1]
    halo = length - tokens
    piece = width // len(pieces)
    blocks = tokens // taps
    for p, block in enumerate(pieces):
        place = (where_ref[0] & (len(pieces) - 1)) ^ p
        for s in range(3):
            begin = pl.multiple_of(s * width + place * piece, piece)
            rows_ref[pl.ds(begin, piece), :] = block[s * piece : (s + 1) * piece, :]
    step = 2 * taps
    for begin in range(0, length, step):
        count = min(step, length - begin)
        result = lax.dot_general(
            onehot(ids_ref[begin : begin + count, :], vocab),
            rows_ref[...],
            (((1,), (1,)), ((), ())),
            preferred_element_type=F32,
        )
        for s in range(3):
            proj_ref[s, begin : begin + count, :] = result[:, s * width : (s + 1) * width]

    def taken(s, begin):
        total = short_ref[0, s : s + 1, :] * proj_ref[s, begin : begin + taps, :]
        for lag in range(1, short_taps):
            total = total + short_ref[lag, s : s + 1, :] * proj_ref[s, begin - lag : begin - lag + taps, :]
        return total

    for b in range(blocks + 1):
        begin = halo + (b - 1) * taps
        product = (taken(1, begin) * taken(2, begin)).astype(BF).astype(F32)
        product_ref[b * taps : (b + 1) * taps, :] = product
        turned_ref[:, b * taps : (b + 1) * taps] = product.T.astype(BF)
    for g in range(width // group_size):
        rows = slice(g * group_size, (g + 1) * group_size)
        stacked = jnp.concatenate(
            [turned_ref[rows, b * taps : (b + 2) * taps] for b in range(blocks)], axis=0
        )
        mixed = jnp.dot(stacked, band_ref[g], preferred_element_type=F32)
        for b in range(blocks):
            conv_ref[rows, b * taps : (b + 1) * taps] = mixed[b * group_size : (b + 1) * group_size]
    for b in range(blocks):
        conv = conv_ref[:, b * taps : (b + 1) * taps].T
        conv = conv + skip_ref[...] * product_ref[(b + 1) * taps : (b + 2) * taps, :]
        gated = taken(0, halo + b * taps) * conv
        out_ref[b * taps : (b + 1) * taps, :] = gated.astype(BF)


def most_kernel(chunks, where_ref, *refs):
    count = 2 * chunks - 1
    gates, weights, out_ref, last_ref, lhs_ref, rhs_ref = (
        refs[:count], refs[count:-4], refs[-4], refs[-3], refs[-2], refs[-1]
    )
    tokens, lane = gates[0].shape
    width = chunks * lane
    top, _, cols = rhs_ref.shape
    for index, weight in enumerate(weights):
        offset, side = index // 2, index % 2
        rhs_ref[offset ^ where_ref[4], side * width : (side + 1) * width, :] = weight[...]
    for index, gate in enumerate(gates):
        side, m = index // chunks, index % chunks
        begin = pl.multiple_of(side * width + (where_ref[2] ^ m) * lane, lane)
        lhs_ref[:, pl.ds(begin, lane)] = gate[...]
    missing = pl.multiple_of(width + (where_ref[2] ^ (chunks - 1)) * lane, lane)
    lhs_ref[:, pl.ds(missing, lane)] = jnp.zeros((tokens, lane), BF)
    rows = min(tokens, 256)
    for half in range(2):
        for b in range(top // 2):
            place = (where_ref[3] ^ half) * (top // 2) + b
            at = slice(b * cols, (b + 1) * cols)
            last_ref[half, :, at] = rhs_ref[place, pl.ds(missing, lane), :]
            for begin in range(0, tokens, rows):
                out_ref[half, begin : begin + rows, at] = jnp.dot(
                    lhs_ref[begin : begin + rows, :], rhs_ref[place], preferred_element_type=F32
                )


def sent_kernel(most_ref, gate_ref, weight_ref, out_ref):
    out_ref[...] = (
        most_ref[0] + jnp.dot(gate_ref[...], weight_ref[0], preferred_element_type=F32)
    ).astype(BF)


def final_kernel(most_ref, gate_ref, weight_ref, embed_ref, other_ref, out_ref):
    own = most_ref[0] + jnp.dot(gate_ref[...], weight_ref[0], preferred_element_type=F32)
    out_ref[...] = (embed_ref[...].astype(F32) + own + other_ref[...].astype(F32)).astype(BF)


def body(
    token_ids, embed_table, norm_gain, in_weight, short_filter, long_filter, long_skip, out_weight
):
    chunks = 4
    n, minor = 2 * chunks, lax.axis_size("seq") // (2 * chunks)
    device, tp, m = lax.axis_index("seq"), lax.axis_index("tp"), lax.axis_size("tp")
    seq = device // minor
    tokens = token_ids.shape[0]
    vocab, width = embed_table.shape
    groups, taps = long_filter.shape
    short_taps = short_filter.shape[0]
    piece = width // n
    per_chunk = n // chunks
    lane = per_chunk * piece
    halo = taps + 16 * -(-(short_taps - 1) // 16)
    length = tokens + halo
    top = n // 2
    upper = (seq >= top).astype(jnp.int32)
    core, row = tp & 1, tp >> 1
    same_side = row == upper
    chunk_at = seq // per_chunk
    where = jnp.stack([seq, tp, chunk_at, core, seq & (top - 1)]).astype(jnp.int32)

    def over(block, offset):
        return swap(block, "seq", offset * minor)

    if minor > 1:
        parts = [[g * minor + j for j in range(minor)] for g in range(n)]
        in_weight = lax.all_gather(in_weight, "seq", axis=0, tiled=True, axis_index_groups=parts)
        out_weight = lax.all_gather(out_weight, "seq", axis=1, tiled=True, axis_index_groups=parts)
    depth = in_weight.shape[0]

    near = [out_weight]
    far = [over(out_weight, top)]

    parts = call(
        turn_kernel,
        [jax.ShapeDtypeStruct((2, 3 * piece, depth), BF)] * top,
        2,
        cost_us(1.0),
        4 * 3 * width * depth,
        in_specs=[SCALARS, WHOLE],
        scratch_shapes=[pltpu.VMEM((n, piece, depth), BF)],
    )(where, in_weight.transpose(1, 0, 2))
    parts = [over(part, offset) if offset else part for offset, part in enumerate(parts)]

    table_row = swap(embed_table, "tp", 2)
    table_core = swap(embed_table, "tp", 1)
    table_both = swap(table_row, "tp", 1)

    crossing = after(jnp.stack([part[1] for part in parts]), far[0], table_row, table_core)
    crossing = over(crossing, top)

    tail = lax.ppermute(token_ids[tokens - halo :], "seq", [(i, i + 1) for i in range(n * minor - 1)])
    tail = jnp.where(device == 0, -1, tail)
    ids = jnp.concatenate([tail, token_ids])[:, None]

    embedded = call(
        embed_kernel, jax.ShapeDtypeStruct((tokens, width), BF), 2, cost_us(1.0), 2 * tokens * width
    )(ids, embed_table)
    bands = call(
        band_kernel, jax.ShapeDtypeStruct((groups, 2 * taps, taps), BF), 1, cost_us(0.5), groups * taps
    )(long_filter)

    near.append(over(near[0], 2))
    far.append(over(far[0], 2))
    normed = call(
        norm_kernel,
        jax.ShapeDtypeStruct((n, vocab, depth), BF),
        6,
        cost_us(1.5),
        4 * m * vocab * width,
        in_specs=[SCALARS] + [WHOLE] * 5,
        out_specs=pl.BlockSpec(memory_space=pltpu.HBM),
        scratch_shapes=[pltpu.VMEM((n, vocab, depth), BF), pltpu.SemaphoreType.DMA],
    )(where, norm_gain.reshape(m, 1, width), embed_table, table_core, table_row, table_both)

    halves = []
    for one, two in zip(near, far, strict=True):
        kept = jnp.where(same_side, one, two)
        given = jnp.where(same_side, two, one)
        given = swap(given, "tp", 2)
        halves += [kept, given, over(kept, 1), over(given, 1)]

    projected = call(
        project_kernel,
        jax.ShapeDtypeStruct((3 * piece, vocab), BF),
        3,
        cost_us(2.0),
        2 * m * width * (vocab + 3 * piece),
        in_specs=[SCALARS, pl.BlockSpec(memory_space=pltpu.HBM)] + [WHOLE] * (top + 1),
        scratch_shapes=[pltpu.VMEM((n, vocab, depth), BF), pltpu.SemaphoreType.DMA],
    )(where, normed, crossing, *parts)

    starts = [projected, over(projected, 2), over(projected, top)]
    gates, row_gates = [], []
    for index in range(chunks):
        if index == 1:
            starts[2] = after(starts[2], gates[0])
            starts.append(over(starts[2], 2))
        pieces = [starts[index], over(starts[index], 1)]
        at = jnp.stack([seq, chunk_at ^ index]).astype(jnp.int32)
        if index == 0:
            at = after(at, *halves)
        gate = pl.pallas_call(
            functools.partial(mixer_kernel, width // groups),
            grid_spec=pltpu.PrefetchScalarGridSpec(
                num_scalar_prefetch=1,
                grid=(1,),
                in_specs=[
                    pl.BlockSpec((length, 1), lambda i, s: (0, 0)),
                    pl.BlockSpec((short_taps, 3, lane), lambda i, s: (0, 0, s[1])),
                    pl.BlockSpec((1, lane), lambda i, s: (0, s[1])),
                    pl.BlockSpec((lane * groups // width, 2 * taps, taps), lambda i, s: (s[1], 0, 0)),
                ]
                + [pl.BlockSpec((3 * piece, vocab), lambda i, s: (0, 0))] * len(pieces),
                out_specs=pl.BlockSpec((tokens, lane), lambda i, s: (0, 0)),
                scratch_shapes=[
                    pltpu.VMEM((3 * lane, vocab), BF),
                    pltpu.VMEM((3, length, lane), F32),
                    pltpu.VMEM((tokens + taps, lane), F32),
                    pltpu.VMEM((lane, tokens + taps), BF),
                    pltpu.VMEM((lane, tokens), F32),
                ],
            ),
            out_shape=jax.ShapeDtypeStruct((tokens, lane), BF),
            compiler_params=pltpu.CompilerParams(vmem_limit_bytes=12 * MIB),
            cost_estimate=pl.CostEstimate(
                flops=cost_us(3.5), bytes_accessed=4 * vocab * length, transcendentals=0
            ),
        )(at, ids, short_filter, long_skip[None, :], bands, *pieces)
        gates.append(gate)
        row_gates.append(swap(gate, "tp", 2))

    most, last = call(
        functools.partial(most_kernel, chunks),
        [
            jax.ShapeDtypeStruct((2, tokens, width), F32),
            jax.ShapeDtypeStruct((2, lane, width), BF),
        ],
        2 * chunks + 2 * top,
        cost_us(4.0),
        8 * tokens * width,
        room=24,
        in_specs=[SCALARS] + [WHOLE] * (2 * chunks - 1 + 2 * top),
        scratch_shapes=[
            pltpu.VMEM((tokens, 2 * width), BF),
            pltpu.VMEM((top, 2 * width, width * 2 // top), BF),
        ],
    )(where, *gates, *row_gates[:-1], *halves)

    def half_spec(shape, half):
        return pl.BlockSpec((1,) + shape, lambda i: (half, 0, 0))

    rows = tokens // 4
    def stepped(kernel, half, more):
        return pl.pallas_call(
            kernel,
            grid=(tokens // rows,),
            in_specs=[
                pl.BlockSpec((1, rows, width), lambda i: (half, i, 0)),
                pl.BlockSpec((rows, lane), lambda i: (i, 0)),
                pl.BlockSpec((1, lane, width), lambda i: (half, 0, 0)),
            ]
            + [pl.BlockSpec((rows, width), lambda i: (i, 0))] * more,
            out_specs=pl.BlockSpec((rows, width), lambda i: (i, 0)),
            out_shape=jax.ShapeDtypeStruct((tokens, width), BF),
            compiler_params=pltpu.CompilerParams(vmem_limit_bytes=12 * MIB),
            cost_estimate=pl.CostEstimate(
                flops=cost_us(1.5), bytes_accessed=8 * tokens * width, transcendentals=0
            ),
        )

    sent = swap(stepped(sent_kernel, 1, 0)(most, row_gates[-1], last), "tp", 1)
    return stepped(final_kernel, 0, 2)(most, row_gates[-1], last, embedded, sent)


def solution(mesh):
    placed = (
        P("seq"),
        P(None, "tp"),
        P(),
        P("seq", None, "tp"),
        P(None, None, "tp"),
        P("tp", None),
        P("tp"),
        P("tp", "seq"),
    )
    return jax.shard_map(
        body, mesh=mesh, in_specs=placed, out_specs=P("seq", "tp"), check_vma=False
    )
```

time: 262 us -> 101 us (0.39)
  waiting for transfers between devices: 179 us -> 45.4 us
  matrix products: 35.6 us -> 0 us
  starting transfers between devices: 7.26 us -> 32.7 us
  Pallas kernels: 0 us -> 20.8 us
  between operations: 13.3 us -> 0.3 us
  other arithmetic: 12.9 us -> 0.52 us
  local copies, waits for them, and re-layouts: 12.7 us -> 1.6 us
    all_gather x3 -> x0, waiting for transfers between devices: 132 us -> none  [the longest x1 98.2 us: body(): lax.all_gather(in_weight, 'seq', axis=0, tiled=True)]
    reduce_scatter x1 -> x0, waiting for transfers between devices: 42.9 us -> none  [body(): lax.psum_scatter(partials.astype(jnp.bfloat16), 'tp', scatter_dimension=1...]
    ppermute x2 -> x29, waiting for transfers between devices: 3.4 us -> 45.4 us  [the longest x28 45.4 us: swap(): return lax.ppermute(block, axis, [(i, i ^ offset) for i in range(count)])]
    dot_general x7 -> x0, matrix products: 35.6 us -> none  [the longest x1 10.5 us: body(): jnp.einsum('td,dsc->tsc', normed, lax.all_gather(in_weight, 'seq', axis=0...]
    ppermute x2 -> x29, starting transfers between devices: 7.14 us -> 32.7 us  [the longest x28 29.3 us: swap(): return lax.ppermute(block, axis, [(i, i ^ offset) for i in range(count)])]
    pallas_call x0 -> x12, Pallas kernels: none -> 20.8 us  [the longest x4 8.6 us: body(): pl.pallas_call(functools.partial(mixer_kernel, width // groups), grid_spe...]
    add x2 -> x0, other arithmetic: 5.61 us -> none  [the longest x1 5.6 us: short_conv(): running + short_filter[tap_index][None] * extended[begin:begin + out_leng...]
    unnamed x23 -> x17, local copies, waits for them, and re-layouts: 5.97 us -> 1.2 us
  transfers between devices with their start and end apart: 6 -> 29, of which waited for: 6 -> 12; matrix products, arithmetic and copies ran while one was open for 17% -> 1% of each run, Pallas kernels for 0% -> 18%
where the time goes in v2:
time: 101 us
  waiting for transfers between devices  45.4 us (45%)
  starting transfers between devices  32.7 us (32%)
  Pallas kernels  20.8 us (21%)
  local copies, waits for them, and re-layouts  1.6 us (2%)
    ppermute x28, waiting for transfers between devices, swap(): return lax.ppermute(block, axis, [(i, i ^ offset) for i in range(count)])  45.4 us
    ppermute x28, starting transfers between devices, swap(): return lax.ppermute(block, axis, [(i, i ^ offset) for i in range(count)])  29.3 us
    pallas_call x4, Pallas kernels, body(): pl.pallas_call(functools.partial(mixer_kernel, width // groups), grid_spe...  8.6 us
    pallas_call x1, Pallas kernels, body(): call(functools.partial(most_kernel, chunks), [jax.ShapeDtypeStruct((2, to...  3.65 us
    ppermute x1, starting transfers between devices, body(): lax.ppermute(token_ids[tokens - halo:], 'seq', [(i, i + 1) for i in range...  3.45 us
    pallas_call x1, Pallas kernels, body(): stepped(final_kernel, 0, 2)(most, row_gates[-1], last, embedded, sent)  2.13 us
  transfers between devices with their start and end apart: 29, of which 12 were waited for; matrix products, arithmetic and copies ran while one was open for 1% of the time, Pallas kernels for 18%

profile of v2, /device:TPU:0, one launch (start us, length us, event | category | flops | bytes accessed | tf_op | source)
XLA Modules:
  0.0 101.3 jit_solution(5083890451587868123)
XLA Ops:
  0.0 3.0 %collective-permute-start.11 = (bf16[512,512]{1,0:T(8,128)(2,1)}, bf16[512,512]{1,0:T(8,128)(2,1)S(1)}, u32[]{:S(2)}, u32[]{:S(2)}) collective-permute-start(bf16[512,512]{1,0:T(8,128)(2,1)} %table_ref.1), channel_id=1, source_target_pairs={{0,2},{1,3},{2,0},{3,1},{4,6},{5,7},{6,4},{7,5},{8,10},{9,11},{10,... | collective-permute-start | bytes 1572872 | tf_op jit(solution)/shard_map/ppermute | solution.py:19
  3.1 1.1 %copy-done.1 = bf16[256,3,512]{2,0,1:T(8,128)(2,1)S(1)} copy-done((bf16[256,3,512]{2,0,1:T(8,128)(2,1)S(1)}, bf16[256,3,512]{2,0,1:T(8,128)(2,1)}, u32[]{:S(2)}) %copy-start.1) | copy-done | bytes 786456
  4.2 0.8 shard_map.84
  5.0 1.6 %collective-permute-start.13 = (bf16[2,192,256]{2,1,0:T(8,128)(2,1)S(1)}, bf16[2,192,256]{2,1,0:T(8,128)(2,1)S(1)}, u32[]{:S(2)}, u32[]{:S(2)}) collective-permute-start(bf16[2,192,256]{2,1,0:T(8,128)(2,1)S(1)} %get-tuple-element.16), channel_id=1, source_target_pairs={{0,4},{4,0},{8,12},{12,8},{16,20},{20,16},{24,28},{28,24},{1,5},{5... | collective-permute-start | bytes 589832 | tf_op jit(solution)/shard_map/ppermute | solution.py:19
  6.6 2.6 %collective-permute-start = (bf16[512,256]{1,0:T(8,128)(2,1)S(1)}, bf16[512,256]{1,0:T(8,128)(2,1)S(1)}, u32[]{:S(2)}, u32[]{:S(2)}) collective-permute-start(bf16[512,256]{1,0:T(8,128)(2,1)S(1)} %copy-done.5), channel_id=1, source_target_pairs={{0,16},{4,20},{8,24},{12,28},{16,0},{20,4},{24,8},{28,12},{1,17},{... | collective-permute-start | bytes 786440 | tf_op jit(solution)/shard_map/ppermute | solution.py:19
  9.2 1.6 %collective-permute-start.14 = (bf16[2,192,256]{2,1,0:T(8,128)(2,1)S(1)}, bf16[2,192,256]{2,1,0:T(8,128)(2,1)S(1)}, u32[]{:S(2)}, u32[]{:S(2)}) collective-permute-start(bf16[2,192,256]{2,1,0:T(8,128)(2,1)S(1)} %get-tuple-element.17), channel_id=1, source_target_pairs={{0,8},{4,12},{8,0},{12,4},{16,24},{20,28},{24,16},{28,20},{1,9},{5... | collective-permute-start | bytes 589832 | tf_op jit(solution)/shard_map/ppermute | solution.py:19
  10.8 0.4 collective-permute-start.15
  11.5 0.4 shard_map.82.band_ref
  12.0 9.6 %collective-permute-done.14.refs_2_ = bf16[2,192,256]{2,1,0:T(8,128)(2,1)S(1)} collective-permute-done((bf16[2,192,256]{2,1,0:T(8,128)(2,1)S(1)}, bf16[2,192,256]{2,1,0:T(8,128)(2,1)S(1)}, u32[]{:S(2)}, u32[]{:S(2)}) %collective-permute-start.14) | collective-permute-done | bytes 196640 | tf_op jit(solution)/shard_map/ppermute | solution.py:19
  21.6 1.1 %collective-permute-start.4 = (bf16[512,256]{1,0:T(8,128)(2,1)S(1)}, bf16[512,256]{1,0:T(8,128)(2,1)S(1)}, u32[]{:S(2)}, u32[]{:S(2)}) collective-permute-start(bf16[512,256]{1,0:T(8,128)(2,1)S(1)} %copy-done.5), channel_id=1, source_target_pairs={{0,8},{4,12},{8,0},{12,4},{16,24},{20,28},{24,16},{28,20},{1,9},{5... | collective-permute-start | bytes 786440 | tf_op jit(solution)/shard_map/ppermute | solution.py:19
  22.7 3.0 %collective-permute-done.15.refs_3_ = bf16[2,192,256]{2,1,0:T(8,128)(2,1)S(1)} collective-permute-done((bf16[2,192,256]{2,1,0:T(8,128)(2,1)S(1)}, bf16[2,192,256]{2,1,0:T(8,128)(2,1)S(1)}, u32[]{:S(2)}, u32[]{:S(2)}) %collective-permute-start.15) | collective-permute-done | bytes 196640 | tf_op jit(solution)/shard_map/ppermute | solution.py:19
  25.7 3.4 %collective-permute-start.9 = (s32[144]{0:T(256)S(1)}, s32[144]{0:T(256)S(1)}, u32[]{:S(2)}, u32[]{:S(2)}) collective-permute-start(s32[144]{0:T(256)S(1)} %slice.15), channel_id=1, source_target_pairs={{0,4},{4,8},{8,12},{12,16},{16,20},{20,24},{24,28},{1,5},{5,9},{9,... | collective-permute-start | bytes 1736 | tf_op jit(solution)/shard_map/ppermute | solution.py:262
  29.2 1.2 %collective-permute-start.5 = (bf16[512,256]{1,0:T(8,128)(2,1)S(1)}, bf16[512,256]{1,0:T(8,128)(2,1)S(1)}, u32[]{:S(2)}, u32[]{:S(2)}) collective-permute-start(bf16[512,256]{1,0:T(8,128)(2,1)S(1)} %collective-permute-done), channel_id=1, source_target_pairs={{0,8},{4,12},{8,0},{12,4},{16,24},{20,28},{24,16},{28,20},{1,9},{5... | collective-permute-start | bytes 786440 | tf_op jit(solution)/shard_map/ppermute | solution.py:19
  30.6 0.6 collective-permute-start.1
  31.1 1.8 %collective-permute-start.16 = (bf16[4,192,256]{2,1,0:T(8,128)(2,1)S(1)}, bf16[4,192,256]{2,1,0:T(8,128)(2,1)S(1)}, u32[]{:S(2)}, u32[]{:S(2)}) collective-permute-start(bf16[4,192,256]{2,1,0:T(8,128)(2,1)S(1)} %pad_maximum_fusion), channel_id=1, source_target_pairs={{0,16},{4,20},{8,24},{12,28},{16,0},{20,4},{24,8},{28,12},{1,17},{... | collective-permute-start | bytes 1179656 | tf_op jit(solution)/shard_map/ppermute | solution.py:19
  32.9 3.8 %collective-permute-done.5 = bf16[512,256]{1,0:T(8,128)(2,1)S(1)} collective-permute-done((bf16[512,256]{1,0:T(8,128)(2,1)S(1)}, bf16[512,256]{1,0:T(8,128)(2,1)S(1)}, u32[]{:S(2)}, u32[]{:S(2)}) %collective-permute-start.5) | collective-permute-done | bytes 262176 | tf_op jit(solution)/shard_map/ppermute | solution.py:19
  36.9 2.5 %collective-permute-start.2 = (bf16[512,256]{1,0:T(8,128)(2,1)S(1)}, bf16[512,256]{1,0:T(8,128)(2,1)S(1)}, u32[]{:S(2)}, u32[]{:S(2)}) collective-permute-start(bf16[512,256]{1,0:T(8,128)(2,1)S(1)} %get-tuple-element.26.refs_7_), channel_id=1, source_target_pairs={{0,4},{4,0},{8,12},{12,8},{16,20},{20,16},{24,28},{28,24},{1,5},{5... | collective-permute-start | bytes 786440 | tf_op jit(solution)/shard_map/ppermute | solution.py:19
  39.4 2.0 %shard_map.83.normed_ref = bf16[8,512,256]{2,1,0:T(8,128)(2,1)S(1)} custom-call(s32[5]{0:T(128)S(1)} %stack.52.where_ref, f32[4,1,512]{2,1,0:T(1,128)S(1)} %bitcast.12, bf16[512,512]{1,0:T(8,128)(2,1)S(1)} %copy-done.2, bf16[512,512]{1,0:T(8,128)(2,1)S(1)} %collective-permute-done.10.refs_1_, bf16[512,512]{1,0:T(8,128)(2,1)S(1)} %collective-permute-done.11.refs_2_, ...), custom_call_target="tpu_custom_call" | custom-call | flops 1650000000 | bytes 4194304 | tf_op jit(solution)/shard_map/pallas_call | solution.py:275
  41.5 3.5 %collective-permute-done.6.refs_12_ = bf16[512,256]{1,0:T(8,128)(2,1)S(1)} collective-permute-done((bf16[512,256]{1,0:T(8,128)(2,1)S(1)}, bf16[512,256]{1,0:T(8,128)(2,1)S(1)}, u32[]{:S(2)}, u32[]{:S(2)}) %collective-permute-start.6) | collective-permute-done | bytes 262176 | tf_op jit(solution)/shard_map/ppermute | solution.py:19
  45.0 0.7 collective-permute-start.3
  45.6 6.1 %collective-permute-done.16.crossing_ref = bf16[4,192,256]{2,1,0:T(8,128)(2,1)S(1)} collective-permute-done((bf16[4,192,256]{2,1,0:T(8,128)(2,1)S(1)}, bf16[4,192,256]{2,1,0:T(8,128)(2,1)S(1)}, u32[]{:S(2)}, u32[]{:S(2)}) %collective-permute-start.16) | collective-permute-done | bytes 393248 | tf_op jit(solution)/shard_map/ppermute | solution.py:19
  51.7 0.4 collective-permute-start.8
  52.1 1.5 %shard_map.85.refs_0_ = bf16[192,512]{1,0:T(8,128)(2,1)S(1)} custom-call(s32[5]{0:T(128)S(1)} %stack.52.where_ref, bf16[8,512,256]{2,1,0:T(8,128)(2,1)S(1)} %shard_map.83.normed_ref, bf16[4,192,256]{2,1,0:T(8,128)(2,1)S(1)} %collective-permute-done.16.crossing_ref, bf16[2,192,256]{2,1,0:T(8,128)(2,1)S(1)} %get-tuple-element.15.refs_0_, ...), custom_call_target="tpu_custom_call" | custom-call | flops 2200000000 | bytes 2883584 | tf_op jit(solution)/shard_map/pallas_call | solution.py:293
  53.7 1.7 %collective-permute-start.17 = (bf16[192,512]{1,0:T(8,128)(2,1)S(1)}, bf16[192,512]{1,0:T(8,128)(2,1)S(1)}, u32[]{:S(2)}, u32[]{:S(2)}) collective-permute-start(bf16[192,512]{1,0:T(8,128)(2,1)S(1)} %shard_map.85.refs_0_), channel_id=1, source_target_pairs={{0,4},{4,0},{8,12},{12,8},{16,20},{20,16},{24,28},{28,24},{1,5},{5... | collective-permute-start | bytes 589832 | tf_op jit(solution)/shard_map/ppermute | solution.py:19
  55.4 0.2 broadcast_in_dim.16.ids_ref
  55.7 1.9 %collective-permute-start.18 = (bf16[192,512]{1,0:T(8,128)(2,1)S(1)}, bf16[192,512]{1,0:T(8,128)(2,1)S(1)}, u32[]{:S(2)}, u32[]{:S(2)}) collective-permute-start(bf16[192,512]{1,0:T(8,128)(2,1)S(1)} %shard_map.85.refs_0_), channel_id=1, source_target_pairs={{0,8},{4,12},{8,0},{12,4},{16,24},{20,28},{24,16},{28,20},{1,9},{5... | collective-permute-start | bytes 589832 | tf_op jit(solution)/shard_map/ppermute | solution.py:19
  57.6 3.9 %collective-permute-done.8.refs_14_ = bf16[512,256]{1,0:T(8,128)(2,1)S(1)} collective-permute-done((bf16[512,256]{1,0:T(8,128)(2,1)S(1)}, bf16[512,256]{1,0:T(8,128)(2,1)S(1)}, u32[]{:S(2)}, u32[]{:S(2)}) %collective-permute-start.8) | collective-permute-done | bytes 262176 | tf_op jit(solution)/shard_map/ppermute | solution.py:19
  61.6 3.2 %collective-permute-done.17.refs_1_ = bf16[192,512]{1,0:T(8,128)(2,1)S(1)} collective-permute-done((bf16[192,512]{1,0:T(8,128)(2,1)S(1)}, bf16[192,512]{1,0:T(8,128)(2,1)S(1)}, u32[]{:S(2)}, u32[]{:S(2)}) %collective-permute-start.17) | collective-permute-done | bytes 196640 | tf_op jit(solution)/shard_map/ppermute | solution.py:19
  64.8 2.1 %shard_map.86.refs_0_ = bf16[1024,128]{1,0:T(8,128)(2,1)S(1)} custom-call(s32[2]{0:T(128)S(1)} %pad_add_fusion.1.where_ref, s32[1168,1]{1,0:T(8,128)S(1)} %broadcast_in_dim.16.ids_ref, f32[7,3,512]{2,1,0:T(4,128)S(1)} %copy.14.short_ref, f32[1,512]{1,0:T(1,128)S(1)} %bitcast.13, bf16[32,256,128]{2,1,0:T(8,128)(2,1)S(1)} %shard_map.82.band_ref, ...), custom_call_target="tpu_custom_call" | custom-call | flops 3849999872 | bytes 2392064 | tf_op jit(solution)/shard_map/pallas_call | solution.py:313
  67.0 1.2 %collective-permute-start.21 = (bf16[192,512]{1,0:T(8,128)(2,1)S(1)}, bf16[192,512]{1,0:T(8,128)(2,1)S(1)}, u32[]{:S(2)}, u32[]{:S(2)}) collective-permute-start(bf16[192,512]{1,0:T(8,128)(2,1)S(1)} %collective-permute-done.20.refs_0_), channel_id=1, source_target_pairs={{0,4},{4,0},{8,12},{12,8},{16,20},{20,16},{24,28},{28,24},{1,5},{5... | collective-permute-start | bytes 589832 | tf_op jit(solution)/shard_map/ppermute | solution.py:19
  68.3 0.3 collective-permute-start.22
  68.6 1.8 %collective-permute-start.24 = (bf16[1024,128]{1,0:T(8,128)(2,1)S(1)}, bf16[1024,128]{1,0:T(8,128)(2,1)S(1)}, u32[]{:S(2)}, u32[]{:S(2)}) collective-permute-start(bf16[1024,128]{1,0:T(8,128)(2,1)S(1)} %shard_map.86.refs_0_), channel_id=1, source_target_pairs={{0,2},{1,3},{2,0},{3,1},{4,6},{5,7},{6,4},{7,5},{8,10},{9,11},{10,... | collective-permute-start | bytes 786440 | tf_op jit(solution)/shard_map/ppermute | solution.py:19
  70.4 0.9 collective-permute-start.19
  71.3 3.5 %collective-permute-done.21.refs_1_ = bf16[192,512]{1,0:T(8,128)(2,1)S(1)} collective-permute-done((bf16[192,512]{1,0:T(8,128)(2,1)S(1)}, bf16[192,512]{1,0:T(8,128)(2,1)S(1)}, u32[]{:S(2)}, u32[]{:S(2)}) %collective-permute-start.21) | collective-permute-done | bytes 196640 | tf_op jit(solution)/shard_map/ppermute | solution.py:19
  74.9 2.2 %shard_map.88.refs_2_ = bf16[1024,128]{1,0:T(8,128)(2,1)S(1)} custom-call(s32[2]{0:T(128)S(1)} %pad_add_fusion.3.where_ref, s32[1168,1]{1,0:T(8,128)S(1)} %broadcast_in_dim.16.ids_ref, f32[7,3,512]{2,1,0:T(4,128)S(1)} %copy.14.short_ref, f32[1,512]{1,0:T(1,128)S(1)} %bitcast.14, bf16[32,256,128]{2,1,0:T(8,128)(2,1)S(1)} %shard_map.82.band_ref, ...), custom_call_target="tpu_custom_call" | custom-call | flops 3849999872 | bytes 2392064 | tf_op jit(solution)/shard_map/pallas_call | solution.py:313
  77.0 1.3 %collective-permute-start.26 = (bf16[1024,128]{1,0:T(8,128)(2,1)S(1)}, bf16[1024,128]{1,0:T(8,128)(2,1)S(1)}, u32[]{:S(2)}, u32[]{:S(2)}) collective-permute-start(bf16[1024,128]{1,0:T(8,128)(2,1)S(1)} %shard_map.88.refs_2_), channel_id=1, source_target_pairs={{0,2},{1,3},{2,0},{3,1},{4,6},{5,7},{6,4},{7,5},{8,10},{9,11},{10,... | collective-permute-start | bytes 786440 | tf_op jit(solution)/shard_map/ppermute | solution.py:19
  78.3 0.4 collective-permute-start.23
  78.8 2.2 %shard_map.87.refs_1_ = bf16[1024,128]{1,0:T(8,128)(2,1)S(1)} custom-call(s32[2]{0:T(128)S(1)} %pad_add_fusion.2.where_ref, s32[1168,1]{1,0:T(8,128)S(1)} %broadcast_in_dim.16.ids_ref, f32[7,3,512]{2,1,0:T(4,128)S(1)} %copy.14.short_ref, f32[1,512]{1,0:T(1,128)S(1)} %bitcast.15, bf16[32,256,128]{2,1,0:T(8,128)(2,1)S(1)} %shard_map.82.band_ref, ...), custom_call_target="tpu_custom_call" | custom-call | flops 3849999872 | bytes 2392064 | tf_op jit(solution)/shard_map/pallas_call | solution.py:313
  80.9 1.1 %collective-permute-start.25 = (bf16[1024,128]{1,0:T(8,128)(2,1)S(1)}, bf16[1024,128]{1,0:T(8,128)(2,1)S(1)}, u32[]{:S(2)}, u32[]{:S(2)}) collective-permute-start(bf16[1024,128]{1,0:T(8,128)(2,1)S(1)} %shard_map.87.refs_1_), channel_id=1, source_target_pairs={{0,2},{1,3},{2,0},{3,1},{4,6},{5,7},{6,4},{7,5},{8,10},{9,11},{10,... | collective-permute-start | bytes 786440 | tf_op jit(solution)/shard_map/ppermute | solution.py:19
  82.1 1.9 %collective-permute-done.23.refs_1_ = bf16[192,512]{1,0:T(8,128)(2,1)S(1)} collective-permute-done((bf16[192,512]{1,0:T(8,128)(2,1)S(1)}, bf16[192,512]{1,0:T(8,128)(2,1)S(1)}, u32[]{:S(2)}, u32[]{:S(2)}) %collective-permute-start.23) | collective-permute-done | bytes 196640 | tf_op jit(solution)/shard_map/ppermute | solution.py:19
  84.0 2.1 %shard_map.89.refs_3_ = bf16[1024,128]{1,0:T(8,128)(2,1)S(1)} custom-call(s32[2]{0:T(128)S(1)} %pad_add_fusion.4.where_ref, s32[1168,1]{1,0:T(8,128)S(1)} %broadcast_in_dim.16.ids_ref, f32[7,3,512]{2,1,0:T(4,128)S(1)} %copy.14.short_ref, f32[1,512]{1,0:T(1,128)S(1)} %bitcast.16, bf16[32,256,128]{2,1,0:T(8,128)(2,1)S(1)} %shard_map.82.band_ref, ...), custom_call_target="tpu_custom_call" | custom-call | flops 3849999872 | bytes 2392064 | tf_op jit(solution)/shard_map/pallas_call | solution.py:313
  86.2 0.9 collective-permute-start.27
  87.0 4.8 %collective-permute-done.25.refs_5_ = bf16[1024,128]{1,0:T(8,128)(2,1)S(1)} collective-permute-done((bf16[1024,128]{1,0:T(8,128)(2,1)S(1)}, bf16[1024,128]{1,0:T(8,128)(2,1)S(1)}, u32[]{:S(2)}, u32[]{:S(2)}) %collective-permute-start.25) | collective-permute-done | bytes 262176 | tf_op jit(solution)/shard_map/ppermute | solution.py:19
  91.8 3.7 %shard_map.90 = (f32[2,1024,512]{2,1,0:T(8,128)S(1)}, bf16[2,128,512]{2,1,0:T(8,128)(2,1)S(1)}) custom-call(s32[5]{0:T(128)S(1)} %stack.52.where_ref, bf16[1024,128]{1,0:T(8,128)(2,1)S(1)} %shard_map.86.refs_0_, bf16[1024,128]{1,0:T(8,128)(2,1)S(1)} %shard_map.87.refs_1_, bf16[1024,128]{1,0:T(8,128)(2,1)S(1)} %shard_map.88.refs_2_, ...), custom_call_target="tpu_custom_call" | custom-call | flops 4400000000 | bytes 4194304 | tf_op jit(solution)/shard_map/pallas_call | solution.py:343
  95.5 0.9 shard_map.92
  96.5 0.8 shard_map.91.embed_ref
  97.3 1.9 %collective-permute-done.28.other_ref = bf16[1024,512]{1,0:T(8,128)(2,1)S(1)} collective-permute-done((bf16[1024,512]{1,0:T(8,128)(2,1)S(1)}, bf16[1024,512]{1,0:T(8,128)(2,1)S(1)}, u32[]{:S(2)}, u32[]{:S(2)}) %collective-permute-start.28) | collective-permute-done | bytes 1048608 | tf_op jit(solution)/shard_map/ppermute | solution.py:19
  99.1 2.1 %shard_map.93 = bf16[1024,512]{1,0:T(8,128)(2,1)} custom-call(f32[2,1024,512]{2,1,0:T(8,128)S(1)} %get-tuple-element.21.most_ref, bf16[1024,128]{1,0:T(8,128)(2,1)S(1)} %collective-permute-done.27.gate_ref, bf16[2,128,512]{2,1,0:T(8,128)(2,1)S(1)} %get-tuple-element.22.weight_ref, bf16[1024,512]{1,0:T(8,128)(2,1)S(1)} %shard_map.91.embed_ref, ...), custom_call_target="tpu_custom_call" | custom-call | flops 1650000000 | bytes 4194304 | tf_op jit(solution)/shard_map/pallas_call | solution.py:383
  (55 shorter events, 1.3 us)
Async XLA Ops:
  0.0 30.4 %collective-permute-start.11 = (bf16[512,512]{1,0:T(8,128)(2,1)}, bf16[512,512]{1,0:T(8,128)(2,1)S(1)}, u32[]{:S(2)}, u32[]{:S(2)}) collective-permute-start(bf16[512,512]{1,0:T(8,128)(2,1)} %table_ref.1), channel_id=1, source_target_pairs={{0,2},{1,3},{2,0},{3,1},{4,6},{5,7},{6,4},{7,5},{8,10},{9,11},{10,... | collective-permute-start | bytes 1572872 | tf_op jit(solution)/shard_map/ppermute | solution.py:19
  3.1 1.1 %copy-start.1 = (bf16[256,3,512]{2,0,1:T(8,128)(2,1)S(1)}, bf16[256,3,512]{2,0,1:T(8,128)(2,1)}, u32[]{:S(2)}) copy-start(bf16[256,3,512]{2,0,1:T(8,128)(2,1)} %param.11) | copy-start | bytes 2359300
  4.2 2.4 %copy-start.5 = (bf16[512,256]{1,0:T(8,128)(2,1)S(1)}, bf16[512,256]{1,0:T(8,128)(2,1)}, u32[]{:S(2)}) copy-start(bf16[512,256]{1,0:T(8,128)(2,1)} %param.15) | copy-start | bytes 786436
  4.2 7.0 %copy-start.7 = (s32[1024]{0:T(1024)S(1)}, s32[1024]{0:T(1024)}, u32[]{:S(2)}) copy-start(s32[1024]{0:T(1024)} %param.8) | copy-start | bytes 12292
  4.2 7.1 %copy-start.6 = (f32[7,3,512]{2,0,1:T(8,128)S(1)}, f32[7,3,512]{2,0,1:T(8,128)}, u32[]{:S(2)}) copy-start(f32[7,3,512]{2,0,1:T(8,128)} %param.12) | copy-start | bytes 129028
  4.2 7.3 %copy-start.2 = (bf16[512,512]{1,0:T(8,128)(2,1)S(1)}, bf16[512,512]{1,0:T(8,128)(2,1)}, u32[]{:S(2)}) copy-start(bf16[512,512]{1,0:T(8,128)(2,1)} %table_ref.1) | copy-start | bytes 1572868
  4.2 7.3 %copy-start = (bf16[32,128]{1,0:T(8,128)(2,1)S(1)}, bf16[32,128]{1,0:T(8,128)(2,1)}, u32[]{:S(2)}) copy-start(bf16[32,128]{1,0:T(8,128)(2,1)} %filter_ref.1) | copy-start | bytes 24580
  5.0 6.4 %collective-permute-start.13 = (bf16[2,192,256]{2,1,0:T(8,128)(2,1)S(1)}, bf16[2,192,256]{2,1,0:T(8,128)(2,1)S(1)}, u32[]{:S(2)}, u32[]{:S(2)}) collective-permute-start(bf16[2,192,256]{2,1,0:T(8,128)(2,1)S(1)} %get-tuple-element.16), channel_id=1, source_target_pairs={{0,4},{4,0},{8,12},{12,8},{16,20},{20,16},{24,28},{28,24},{1,5},{5... | collective-permute-start | bytes 589832 | tf_op jit(solution)/shard_map/ppermute | solution.py:19
  6.6 22.5 %collective-permute-start = (bf16[512,256]{1,0:T(8,128)(2,1)S(1)}, bf16[512,256]{1,0:T(8,128)(2,1)S(1)}, u32[]{:S(2)}, u32[]{:S(2)}) collective-permute-start(bf16[512,256]{1,0:T(8,128)(2,1)S(1)} %copy-done.5), channel_id=1, source_target_pairs={{0,16},{4,20},{8,24},{12,28},{16,0},{20,4},{24,8},{28,12},{1,17},{... | collective-permute-start | bytes 786440 | tf_op jit(solution)/shard_map/ppermute | solution.py:19
  9.2 12.3 %collective-permute-start.14 = (bf16[2,192,256]{2,1,0:T(8,128)(2,1)S(1)}, bf16[2,192,256]{2,1,0:T(8,128)(2,1)S(1)}, u32[]{:S(2)}, u32[]{:S(2)}) collective-permute-start(bf16[2,192,256]{2,1,0:T(8,128)(2,1)S(1)} %get-tuple-element.17), channel_id=1, source_target_pairs={{0,8},{4,12},{8,0},{12,4},{16,24},{20,28},{24,16},{28,20},{1,9},{5... | collective-permute-start | bytes 589832 | tf_op jit(solution)/shard_map/ppermute | solution.py:19
  10.8 14.9 %collective-permute-start.15 = (bf16[2,192,256]{2,1,0:T(8,128)(2,1)S(1)}, bf16[2,192,256]{2,1,0:T(8,128)(2,1)S(1)}, u32[]{:S(2)}, u32[]{:S(2)}) collective-permute-start(bf16[2,192,256]{2,1,0:T(8,128)(2,1)S(1)} %get-tuple-element.18), channel_id=1, source_target_pairs={{0,12},{4,8},{8,4},{12,0},{16,28},{20,24},{24,20},{28,16},{1,13},{... | collective-permute-start | bytes 589832 | tf_op jit(solution)/shard_map/ppermute | solution.py:19
  11.5 19.1 %collective-permute-start.10 = (bf16[512,512]{1,0:T(8,128)(2,1)S(1)}, bf16[512,512]{1,0:T(8,128)(2,1)S(1)}, u32[]{:S(2)}, u32[]{:S(2)}) collective-permute-start(bf16[512,512]{1,0:T(8,128)(2,1)S(1)} %copy-done.2), channel_id=1, source_target_pairs={{0,1},{1,0},{2,3},{3,2},{4,5},{5,4},{6,7},{7,6},{8,9},{9,8},{10,11... | collective-permute-start | bytes 1572872 | tf_op jit(solution)/shard_map/ppermute | solution.py:19
  11.9 27.5 %copy-start.3 = (f32[2048]{0:T(1024)S(1)}, f32[2048]{0:T(1024)}, u32[]{:S(2)}) copy-start(f32[2048]{0:T(1024)} %param.10) | copy-start | bytes 24580
  21.6 9.6 %collective-permute-start.4 = (bf16[512,256]{1,0:T(8,128)(2,1)S(1)}, bf16[512,256]{1,0:T(8,128)(2,1)S(1)}, u32[]{:S(2)}, u32[]{:S(2)}) collective-permute-start(bf16[512,256]{1,0:T(8,128)(2,1)S(1)} %copy-done.5), channel_id=1, source_target_pairs={{0,8},{4,12},{8,0},{12,4},{16,24},{20,28},{24,16},{28,20},{1,9},{5... | collective-permute-start | bytes 786440 | tf_op jit(solution)/shard_map/ppermute | solution.py:19
  25.7 28.0 %collective-permute-start.9 = (s32[144]{0:T(256)S(1)}, s32[144]{0:T(256)S(1)}, u32[]{:S(2)}, u32[]{:S(2)}) collective-permute-start(s32[144]{0:T(256)S(1)} %slice.15), channel_id=1, source_target_pairs={{0,4},{4,8},{8,12},{12,16},{16,20},{20,24},{24,28},{1,5},{5,9},{9,... | collective-permute-start | bytes 1736 | tf_op jit(solution)/shard_map/ppermute | solution.py:262
  29.2 7.6 %collective-permute-start.5 = (bf16[512,256]{1,0:T(8,128)(2,1)S(1)}, bf16[512,256]{1,0:T(8,128)(2,1)S(1)}, u32[]{:S(2)}, u32[]{:S(2)}) collective-permute-start(bf16[512,256]{1,0:T(8,128)(2,1)S(1)} %collective-permute-done), channel_id=1, source_target_pairs={{0,8},{4,12},{8,0},{12,4},{16,24},{20,28},{24,16},{28,20},{1,9},{5... | collective-permute-start | bytes 786440 | tf_op jit(solution)/shard_map/ppermute | solution.py:19
  30.4 6.5 %collective-permute-start.12 = (bf16[512,512]{1,0:T(8,128)(2,1)S(1)}, bf16[512,512]{1,0:T(8,128)(2,1)S(1)}, u32[]{:S(2)}, u32[]{:S(2)}) collective-permute-start(bf16[512,512]{1,0:T(8,128)(2,1)S(1)} %collective-permute-done.11.refs_2_), channel_id=1, source_target_pairs={{0,1},{1,0},{2,3},{3,2},{4,5},{5,4},{6,7},{7,6},{8,9},{9,8},{10,11... | collective-permute-start | bytes 1572872 | tf_op jit(solution)/shard_map/ppermute | solution.py:19
  30.6 10.8 %collective-permute-start.1 = (bf16[512,256]{1,0:T(8,128)(2,1)S(1)}, bf16[512,256]{1,0:T(8,128)(2,1)S(1)}, u32[]{:S(2)}, u32[]{:S(2)}) collective-permute-start(bf16[512,256]{1,0:T(8,128)(2,1)S(1)} %get-tuple-element.25), channel_id=1, source_target_pairs={{0,2},{1,3},{2,0},{3,1},{4,6},{5,7},{6,4},{7,5},{8,10},{9,11},{10,... | collective-permute-start | bytes 786440 | tf_op jit(solution)/shard_map/ppermute | solution.py:19
  31.1 20.6 %collective-permute-start.16 = (bf16[4,192,256]{2,1,0:T(8,128)(2,1)S(1)}, bf16[4,192,256]{2,1,0:T(8,128)(2,1)S(1)}, u32[]{:S(2)}, u32[]{:S(2)}) collective-permute-start(bf16[4,192,256]{2,1,0:T(8,128)(2,1)S(1)} %pad_maximum_fusion), channel_id=1, source_target_pairs={{0,16},{4,20},{8,24},{12,28},{16,0},{20,4},{24,8},{28,12},{1,17},{... | collective-permute-start | bytes 1179656 | tf_op jit(solution)/shard_map/ppermute | solution.py:19
  36.7 8.2 %collective-permute-start.6 = (bf16[512,256]{1,0:T(8,128)(2,1)S(1)}, bf16[512,256]{1,0:T(8,128)(2,1)S(1)}, u32[]{:S(2)}, u32[]{:S(2)}) collective-permute-start(bf16[512,256]{1,0:T(8,128)(2,1)S(1)} %get-tuple-element.23), channel_id=1, source_target_pairs={{0,2},{1,3},{2,0},{3,1},{4,6},{5,7},{6,4},{7,5},{8,10},{9,11},{10,... | collective-permute-start | bytes 786440 | tf_op jit(solution)/shard_map/ppermute | solution.py:19
  36.9 18.7 %collective-permute-start.2 = (bf16[512,256]{1,0:T(8,128)(2,1)S(1)}, bf16[512,256]{1,0:T(8,128)(2,1)S(1)}, u32[]{:S(2)}, u32[]{:S(2)}) collective-permute-start(bf16[512,256]{1,0:T(8,128)(2,1)S(1)} %get-tuple-element.26.refs_7_), channel_id=1, source_target_pairs={{0,4},{4,0},{8,12},{12,8},{16,20},{20,16},{24,28},{28,24},{1,5},{5... | collective-permute-start | bytes 786440 | tf_op jit(solution)/shard_map/ppermute | solution.py:19
  41.4 23.4 %copy-start.4 = (f32[512]{0:T(512)S(1)}, f32[512]{0:T(512)}, u32[]{:S(2)}) copy-start(f32[512]{0:T(512)} %param.14) | copy-start | bytes 6148
  41.4 14.4 %collective-permute-start.7 = (bf16[512,256]{1,0:T(8,128)(2,1)S(1)}, bf16[512,256]{1,0:T(8,128)(2,1)S(1)}, u32[]{:S(2)}, u32[]{:S(2)}) collective-permute-start(bf16[512,256]{1,0:T(8,128)(2,1)S(1)} %get-tuple-element.24.refs_11_), channel_id=1, source_target_pairs={{0,4},{4,0},{8,12},{12,8},{16,20},{20,16},{24,28},{28,24},{1,5},{5... | collective-permute-start | bytes 786440 | tf_op jit(solution)/shard_map/ppermute | solution.py:19
  45.0 12.7 %collective-permute-start.3 = (bf16[512,256]{1,0:T(8,128)(2,1)S(1)}, bf16[512,256]{1,0:T(8,128)(2,1)S(1)}, u32[]{:S(2)}, u32[]{:S(2)}) collective-permute-start(bf16[512,256]{1,0:T(8,128)(2,1)S(1)} %collective-permute-done.1.refs_8_), channel_id=1, source_target_pairs={{0,4},{4,0},{8,12},{12,8},{16,20},{20,16},{24,28},{28,24},{1,5},{5... | collective-permute-start | bytes 786440 | tf_op jit(solution)/shard_map/ppermute | solution.py:19
  51.7 9.9 %collective-permute-start.8 = (bf16[512,256]{1,0:T(8,128)(2,1)S(1)}, bf16[512,256]{1,0:T(8,128)(2,1)S(1)}, u32[]{:S(2)}, u32[]{:S(2)}) collective-permute-start(bf16[512,256]{1,0:T(8,128)(2,1)S(1)} %collective-permute-done.6.refs_12_), channel_id=1, source_target_pairs={{0,4},{4,0},{8,12},{12,8},{16,20},{20,16},{24,28},{28,24},{1,5},{5... | collective-permute-start | bytes 786440 | tf_op jit(solution)/shard_map/ppermute | solution.py:19
  53.7 11.1 %collective-permute-start.17 = (bf16[192,512]{1,0:T(8,128)(2,1)S(1)}, bf16[192,512]{1,0:T(8,128)(2,1)S(1)}, u32[]{:S(2)}, u32[]{:S(2)}) collective-permute-start(bf16[192,512]{1,0:T(8,128)(2,1)S(1)} %shard_map.85.refs_0_), channel_id=1, source_target_pairs={{0,4},{4,0},{8,12},{12,8},{16,20},{20,16},{24,28},{28,24},{1,5},{5... | collective-permute-start | bytes 589832 | tf_op jit(solution)/shard_map/ppermute | solution.py:19
  55.7 11.3 %collective-permute-start.20 = (bf16[192,512]{1,0:T(8,128)(2,1)S(1)}, bf16[192,512]{1,0:T(8,128)(2,1)S(1)}, u32[]{:S(2)}, u32[]{:S(2)}) collective-permute-start(bf16[192,512]{1,0:T(8,128)(2,1)S(1)} %shard_map.85.refs_0_), channel_id=1, source_target_pairs={{0,16},{4,20},{8,24},{12,28},{16,0},{20,4},{24,8},{28,12},{1,17},{... | collective-permute-start | bytes 589832 | tf_op jit(solution)/shard_map/ppermute | solution.py:19
  55.7 14.7 %collective-permute-start.18 = (bf16[192,512]{1,0:T(8,128)(2,1)S(1)}, bf16[192,512]{1,0:T(8,128)(2,1)S(1)}, u32[]{:S(2)}, u32[]{:S(2)}) collective-permute-start(bf16[192,512]{1,0:T(8,128)(2,1)S(1)} %shard_map.85.refs_0_), channel_id=1, source_target_pairs={{0,8},{4,12},{8,0},{12,4},{16,24},{20,28},{24,16},{28,20},{1,9},{5... | collective-permute-start | bytes 589832 | tf_op jit(solution)/shard_map/ppermute | solution.py:19
  67.0 7.9 %collective-permute-start.21 = (bf16[192,512]{1,0:T(8,128)(2,1)S(1)}, bf16[192,512]{1,0:T(8,128)(2,1)S(1)}, u32[]{:S(2)}, u32[]{:S(2)}) collective-permute-start(bf16[192,512]{1,0:T(8,128)(2,1)S(1)} %collective-permute-done.20.refs_0_), channel_id=1, source_target_pairs={{0,4},{4,0},{8,12},{12,8},{16,20},{20,16},{24,28},{28,24},{1,5},{5... | collective-permute-start | bytes 589832 | tf_op jit(solution)/shard_map/ppermute | solution.py:19
  68.3 10.0 %collective-permute-start.22 = (bf16[192,512]{1,0:T(8,128)(2,1)S(1)}, bf16[192,512]{1,0:T(8,128)(2,1)S(1)}, u32[]{:S(2)}, u32[]{:S(2)}) collective-permute-start(bf16[192,512]{1,0:T(8,128)(2,1)S(1)} %collective-permute-done.20.refs_0_), channel_id=1, source_target_pairs={{0,8},{4,12},{8,0},{12,4},{16,24},{20,28},{24,16},{28,20},{1,9},{5... | collective-permute-start | bytes 589832 | tf_op jit(solution)/shard_map/ppermute | solution.py:19
  68.6 18.4 %collective-permute-start.24 = (bf16[1024,128]{1,0:T(8,128)(2,1)S(1)}, bf16[1024,128]{1,0:T(8,128)(2,1)S(1)}, u32[]{:S(2)}, u32[]{:S(2)}) collective-permute-start(bf16[1024,128]{1,0:T(8,128)(2,1)S(1)} %shard_map.86.refs_0_), channel_id=1, source_target_pairs={{0,2},{1,3},{2,0},{3,1},{4,6},{5,7},{6,4},{7,5},{8,10},{9,11},{10,... | collective-permute-start | bytes 786440 | tf_op jit(solution)/shard_map/ppermute | solution.py:19
  70.4 8.4 %collective-permute-start.19 = (bf16[192,512]{1,0:T(8,128)(2,1)S(1)}, bf16[192,512]{1,0:T(8,128)(2,1)S(1)}, u32[]{:S(2)}, u32[]{:S(2)}) collective-permute-start(bf16[192,512]{1,0:T(8,128)(2,1)S(1)} %collective-permute-done.18.refs_0_), channel_id=1, source_target_pairs={{0,4},{4,0},{8,12},{12,8},{16,20},{20,16},{24,28},{28,24},{1,5},{5... | collective-permute-start | bytes 589832 | tf_op jit(solution)/shard_map/ppermute | solution.py:19
  77.0 10.0 %collective-permute-start.26 = (bf16[1024,128]{1,0:T(8,128)(2,1)S(1)}, bf16[1024,128]{1,0:T(8,128)(2,1)S(1)}, u32[]{:S(2)}, u32[]{:S(2)}) collective-permute-start(bf16[1024,128]{1,0:T(8,128)(2,1)S(1)} %shard_map.88.refs_2_), channel_id=1, source_target_pairs={{0,2},{1,3},{2,0},{3,1},{4,6},{5,7},{6,4},{7,5},{8,10},{9,11},{10,... | collective-permute-start | bytes 786440 | tf_op jit(solution)/shard_map/ppermute | solution.py:19
  78.3 5.7 %collective-permute-start.23 = (bf16[192,512]{1,0:T(8,128)(2,1)S(1)}, bf16[192,512]{1,0:T(8,128)(2,1)S(1)}, u32[]{:S(2)}, u32[]{:S(2)}) collective-permute-start(bf16[192,512]{1,0:T(8,128)(2,1)S(1)} %collective-permute-done.22.refs_0_), channel_id=1, source_target_pairs={{0,4},{4,0},{8,12},{12,8},{16,20},{20,16},{24,28},{28,24},{1,5},{5... | collective-permute-start | bytes 589832 | tf_op jit(solution)/shard_map/ppermute | solution.py:19
  80.9 10.9 %collective-permute-start.25 = (bf16[1024,128]{1,0:T(8,128)(2,1)S(1)}, bf16[1024,128]{1,0:T(8,128)(2,1)S(1)}, u32[]{:S(2)}, u32[]{:S(2)}) collective-permute-start(bf16[1024,128]{1,0:T(8,128)(2,1)S(1)} %shard_map.87.refs_1_), channel_id=1, source_target_pairs={{0,2},{1,3},{2,0},{3,1},{4,6},{5,7},{6,4},{7,5},{8,10},{9,11},{10,... | collective-permute-start | bytes 786440 | tf_op jit(solution)/shard_map/ppermute | solution.py:19
  86.2 9.3 %collective-permute-start.27 = (bf16[1024,128]{1,0:T(8,128)(2,1)S(1)}, bf16[1024,128]{1,0:T(8,128)(2,1)S(1)}, u32[]{:S(2)}, u32[]{:S(2)}) collective-permute-start(bf16[1024,128]{1,0:T(8,128)(2,1)S(1)} %shard_map.89.refs_3_), channel_id=1, source_target_pairs={{0,2},{1,3},{2,0},{3,1},{4,6},{5,7},{6,4},{7,5},{8,10},{9,11},{10,... | collective-permute-start | bytes 786440 | tf_op jit(solution)/shard_map/ppermute | solution.py:19
  96.4 2.7 %collective-permute-start.28 = (bf16[1024,512]{1,0:T(8,128)(2,1)S(1)}, bf16[1024,512]{1,0:T(8,128)(2,1)S(1)}, u32[]{:S(2)}, u32[]{:S(2)}) collective-permute-start(bf16[1024,512]{1,0:T(8,128)(2,1)S(1)} %shard_map.92), channel_id=1, source_target_pairs={{0,1},{1,0},{2,3},{3,2},{4,5},{5,4},{6,7},{7,6},{8,9},{9,8},{10,11... | collective-permute-start | bytes 3145736 | tf_op jit(solution)/shard_map/ppermute | solution.py:19

commit v3 on v2

--- a/solution.py
+++ b/solution.py
@@ -39,12 +39,18 @@
 
 
 def turn_kernel(where_ref, weight_ref, *refs):
-    out_refs, turned_ref = refs[:-1], refs[-1]
+    out_refs, (held_ref, turned_ref, sems) = refs[:-3], refs[-3:]
     top = len(out_refs)
     rows = out_refs[0].shape[1]
     piece = rows // 3
-    for s in range(3):
-        turned_ref[...] = weight_ref[s].astype(F32).T.astype(BF).reshape(turned_ref.shape)
+    copies = [
+        pltpu.make_async_copy(weight_ref.at[s], held_ref.at[s], sems.at[s]) for s in range(3)
+    ]
+    for copy in copies:
+        copy.start()
+    for s, copy in enumerate(copies):
+        copy.wait()
+        turned_ref[...] = held_ref[s].astype(F32).T.astype(BF).reshape(turned_ref.shape)
         for offset, out_ref in enumerate(out_refs):
             for far in range(2):
                 place = where_ref[0] ^ (offset + far * top)
@@ -166,43 +172,55 @@
         out_ref[b * taps : (b + 1) * taps, :] = gated.astype(BF)
 
 
-def most_kernel(chunks, where_ref, *refs):
-    count = 2 * chunks - 1
-    gates, weights, out_ref, last_ref, lhs_ref, rhs_ref = (
-        refs[:count], refs[count:-4], refs[-4], refs[-3], refs[-2], refs[-1]
-    )
+def most_kernel(chunks, late, where_ref, *refs):
+    count = 2 * chunks - late
+    gates, weights, (out_ref, last_ref, lhs_ref, rhs_ref) = refs[:count], refs[count:-4], refs[-4:]
     tokens, lane = gates[0].shape
     width = chunks * lane
     top, _, cols = rhs_ref.shape
     for index, weight in enumerate(weights):
         offset, side = index // 2, index % 2
         rhs_ref[offset ^ where_ref[4], side * width : (side + 1) * width, :] = weight[...]
-    for index, gate in enumerate(gates):
+    for index in range(2 * chunks):
         side, m = index // chunks, index % chunks
         begin = pl.multiple_of(side * width + (where_ref[2] ^ m) * lane, lane)
-        lhs_ref[:, pl.ds(begin, lane)] = gate[...]
-    missing = pl.multiple_of(width + (where_ref[2] ^ (chunks - 1)) * lane, lane)
-    lhs_ref[:, pl.ds(missing, lane)] = jnp.zeros((tokens, lane), BF)
+        if index < count:
+            lhs_ref[:, pl.ds(begin, lane)] = gates[index][...]
+        else:
+            lhs_ref[:, pl.ds(begin, lane)] = jnp.zeros((tokens, lane), BF)
     rows = min(tokens, 256)
     for half in range(2):
         for b in range(top // 2):
             place = (where_ref[3] ^ half) * (top // 2) + b
             at = slice(b * cols, (b + 1) * cols)
-            last_ref[half, :, at] = rhs_ref[place, pl.ds(missing, lane), :]
+            for late_index in range(late):
+                begin = width + (where_ref[2] ^ (chunks - late + late_index)) * lane
+                last_ref[half, late_index * lane : (late_index + 1) * lane, at] = rhs_ref[
+                    place, pl.ds(pl.multiple_of(begin, lane), lane), :
+                ]
             for begin in range(0, tokens, rows):
                 out_ref[half, begin : begin + rows, at] = jnp.dot(
                     lhs_ref[begin : begin + rows, :], rhs_ref[place], preferred_element_type=F32
-                )
-
-
-def sent_kernel(most_ref, gate_ref, weight_ref, out_ref):
-    out_ref[...] = (
-        most_ref[0] + jnp.dot(gate_ref[...], weight_ref[0], preferred_element_type=F32)
-    ).astype(BF)
-
-
-def final_kernel(most_ref, gate_ref, weight_ref, embed_ref, other_ref, out_ref):
-    own = most_ref[0] + jnp.dot(gate_ref[...], weight_ref[0], preferred_element_type=F32)
+                ).astype(out_ref.dtype)
+
+
+def with_late(most_ref, weight_ref, gates):
+    total = most_ref[0].astype(F32)
+    lane = gates[0].shape[1]
+    for index, gate in enumerate(gates):
+        weight = weight_ref[0, index * lane : (index + 1) * lane, :]
+        total = total + jnp.dot(gate[...], weight, preferred_element_type=F32)
+    return total
+
+
+def sent_kernel(most_ref, weight_ref, *refs):
+    gates, out_ref = refs[:-1], refs[-1]
+    out_ref[...] = with_late(most_ref, weight_ref, gates).astype(BF)
+
+
+def final_kernel(most_ref, weight_ref, *refs):
+    gates, (embed_ref, other_ref, out_ref) = refs[:-3], refs[-3:]
+    own = with_late(most_ref, weight_ref, gates)
     out_ref[...] = (embed_ref[...].astype(F32) + own + other_ref[...].astype(F32)).astype(BF)
 
 
@@ -247,8 +265,12 @@
         2,
         cost_us(1.0),
         4 * 3 * width * depth,
-        in_specs=[SCALARS, WHOLE],
-        scratch_shapes=[pltpu.VMEM((n, piece, depth), BF)],
+        in_specs=[SCALARS, pl.BlockSpec(memory_space=pltpu.HBM)],
+        scratch_shapes=[
+            pltpu.VMEM((3, depth, width), BF),
+            pltpu.VMEM((n, piece, depth), BF),
+            pltpu.SemaphoreType.DMA((3,)),
+        ],
     )(where, in_weight.transpose(1, 0, 2))
     parts = [over(part, offset) if offset else part for offset, part in enumerate(parts)]
 
@@ -259,16 +281,13 @@
     crossing = after(jnp.stack([part[1] for part in parts]), far[0], table_row, table_core)
     crossing = over(crossing, top)
 
-    tail = lax.ppermute(token_ids[tokens - halo :], "seq", [(i, i + 1) for i in range(n * minor - 1)])
-    tail = jnp.where(device == 0, -1, tail)
-    ids = jnp.concatenate([tail, token_ids])[:, None]
-
-    embedded = call(
-        embed_kernel, jax.ShapeDtypeStruct((tokens, width), BF), 2, cost_us(1.0), 2 * tokens * width
-    )(ids, embed_table)
     bands = call(
         band_kernel, jax.ShapeDtypeStruct((groups, 2 * taps, taps), BF), 1, cost_us(0.5), groups * taps
     )(long_filter)
+
+    tail = lax.ppermute(after(token_ids, table_both)[tokens - halo :], "seq", [(i, i + 1) for i in range(n * minor - 1)])
+    tail = jnp.where(device == 0, -1, tail)
+    ids = jnp.concatenate([tail, token_ids])[:, None]
 
     near.append(over(near[0], 2))
     far.append(over(far[0], 2))
@@ -290,26 +309,34 @@
         given = swap(given, "tp", 2)
         halves += [kept, given, over(kept, 1), over(given, 1)]
 
+    parts[0] = after(parts[0], ids)
     projected = call(
         project_kernel,
         jax.ShapeDtypeStruct((3 * piece, vocab), BF),
         3,
-        cost_us(2.0),
+        cost_us(10.0),
         2 * m * width * (vocab + 3 * piece),
         in_specs=[SCALARS, pl.BlockSpec(memory_space=pltpu.HBM)] + [WHOLE] * (top + 1),
         scratch_shapes=[pltpu.VMEM((n, vocab, depth), BF), pltpu.SemaphoreType.DMA],
     )(where, normed, crossing, *parts)
 
+    embedded = call(
+        embed_kernel, jax.ShapeDtypeStruct((tokens, width), BF), 2, cost_us(1.0), 2 * tokens * width
+    )(ids, embed_table)
+    halves[-1] = over(after(halves[-3], projected), 1)
     starts = [projected, over(projected, 2), over(projected, top)]
-    gates, row_gates = [], []
+    gates, row_gates, besides = [], [], []
     for index in range(chunks):
         if index == 1:
             starts[2] = after(starts[2], gates[0])
             starts.append(over(starts[2], 2))
-        pieces = [starts[index], over(starts[index], 1)]
+        pieces = [starts[index], over(starts[index], 1) if index < 3 else over(besides[2], 2)]
+        besides.append(pieces[1])
         at = jnp.stack([seq, chunk_at ^ index]).astype(jnp.int32)
+        if index == 2:
+            at = after(at, row_gates[0])
         if index == 0:
-            at = after(at, *halves)
+            at = after(at, *halves[:-1])
         gate = pl.pallas_call(
             functools.partial(mixer_kernel, width // groups),
             grid_spec=pltpu.PrefetchScalarGridSpec(
@@ -340,36 +367,35 @@
         gates.append(gate)
         row_gates.append(swap(gate, "tp", 2))
 
+    late = 2
     most, last = call(
-        functools.partial(most_kernel, chunks),
+        functools.partial(most_kernel, chunks, late),
         [
-            jax.ShapeDtypeStruct((2, tokens, width), F32),
-            jax.ShapeDtypeStruct((2, lane, width), BF),
+            jax.ShapeDtypeStruct((2, tokens, width), BF),
+            jax.ShapeDtypeStruct((2, late * lane, width), BF),
         ],
-        2 * chunks + 2 * top,
+        0,
         cost_us(4.0),
         8 * tokens * width,
         room=24,
-        in_specs=[SCALARS] + [WHOLE] * (2 * chunks - 1 + 2 * top),
+        in_specs=[SCALARS] + [WHOLE] * (2 * chunks - late + 2 * top),
         scratch_shapes=[
             pltpu.VMEM((tokens, 2 * width), BF),
             pltpu.VMEM((top, 2 * width, width * 2 // top), BF),
         ],
-    )(where, *gates, *row_gates[:-1], *halves)
-
-    def half_spec(shape, half):
-        return pl.BlockSpec((1,) + shape, lambda i: (half, 0, 0))
+    )(where, *gates, *row_gates[:-late], *halves)
 
     rows = tokens // 4
+
     def stepped(kernel, half, more):
         return pl.pallas_call(
             kernel,
             grid=(tokens // rows,),
             in_specs=[
                 pl.BlockSpec((1, rows, width), lambda i: (half, i, 0)),
-                pl.BlockSpec((rows, lane), lambda i: (i, 0)),
-                pl.BlockSpec((1, lane, width), lambda i: (half, 0, 0)),
+                pl.BlockSpec((1, late * lane, width), lambda i: (half, 0, 0)),
             ]
+            + [pl.BlockSpec((rows, lane), lambda i: (i, 0))] * late
             + [pl.BlockSpec((rows, width), lambda i: (i, 0))] * more,
             out_specs=pl.BlockSpec((rows, width), lambda i: (i, 0)),
             out_shape=jax.ShapeDtypeStruct((tokens, width), BF),
@@ -379,8 +405,8 @@
             ),
         )
 
-    sent = swap(stepped(sent_kernel, 1, 0)(most, row_gates[-1], last), "tp", 1)
-    return stepped(final_kernel, 0, 2)(most, row_gates[-1], last, embedded, sent)
+    sent = swap(stepped(sent_kernel, 1, 0)(most, last, *row_gates[-late:]), "tp", 1)
+    return stepped(final_kernel, 0, 2)(most, last, *row_gates[-late:], embedded, sent)
 
 
 def solution(mesh):

time: 101 us -> 98 us (0.970)
  waiting for transfers between devices: 45.4 us -> 33.8 us
  Pallas kernels: 20.8 us -> 26.3 us
  local copies, waits for them, and re-layouts: 1.6 us -> 3.81 us
  other arithmetic: 0.52 us -> 1.54 us
    ppermute x28, waiting for transfers between devices: 45.4 us -> 33.8 us  [swap(): return lax.ppermute(block, axis, [(i, i ^ offset) for i in range(count)])]
    unnamed x17 -> x29, local copies, waits for them, and re-layouts: 1.2 us -> 3.37 us
    pallas_call x4, Pallas kernels: 8.6 us -> 10.5 us  [body(): pl.pallas_call(functools.partial(mixer_kernel, width // groups), grid_spe...]
    ppermute x28, starting transfers between devices: 29.3 us -> 28 us  [swap(): return lax.ppermute(block, axis, [(i, i ^ offset) for i in range(count)])]
    pallas_call x1, Pallas kernels: 0.77 us -> 1.81 us  [body(): call(embed_kernel, jax.ShapeDtypeStruct((tokens, width), BF), 2, cost_us(...]
    select_n x2, other arithmetic: 0.08 us -> 1.11 us  [body(): given = jnp.where(same_side, two, one)]
  transfers between devices with their start and end apart: 29 -> 29, of which waited for: 12 -> 13; matrix products, arithmetic and copies ran while one was open for 1% -> 2% of each run, Pallas kernels for 18% -> 23%
where the time goes in v3:
time: 98 us; the launch traced here: 97.7 us
  waiting for transfers between devices  33.8 us (34%)
  starting transfers between devices  31.9 us (33%)
  Pallas kernels  26.3 us (27%)
  local copies, waits for them, and re-layouts  3.81 us (4%)
  other arithmetic  1.54 us (2%)
    ppermute x28, waiting for transfers between devices, swap(): return lax.ppermute(block, axis, [(i, i ^ offset) for i in range(count)])  33.8 us
    ppermute x28, starting transfers between devices, swap(): return lax.ppermute(block, axis, [(i, i ^ offset) for i in range(count)])  28 us
    pallas_call x4, Pallas kernels, body(): pl.pallas_call(functools.partial(mixer_kernel, width // groups), grid_spe...  10.5 us
    pallas_call x1, Pallas kernels, body(): call(functools.partial(most_kernel, chunks, late), [jax.ShapeDtypeStruct(...  4.07 us
    ppermute x1, starting transfers between devices, body(): lax.ppermute(after(token_ids, table_both)[tokens - halo:], 'seq', [(i, i...  3.89 us
    unnamed x29, local copies, waits for them, and re-layouts  3.37 us
    pallas_call x1, Pallas kernels, body(): call(norm_kernel, jax.ShapeDtypeStruct((n, vocab, depth), BF), 6, cost_us...  2.63 us
    pallas_call x1, Pallas kernels, body(): stepped(final_kernel, 0, 2)(most, last, *row_gates[-late:], embedded, sent)  2.44 us
  transfers between devices with their start and end apart: 29, of which 13 were waited for; matrix products, arithmetic and copies ran while one was open for 2% of the time, Pallas kernels for 23%

profile of v3, /device:TPU:0, one launch (start us, length us, event | category | flops | bytes accessed | tf_op | source)
XLA Modules:
  0.0 97.7 jit_solution(18346124349394976934)
XLA Ops:
  0.0 3.0 %collective-permute-start.8 = (bf16[512,512]{1,0:T(8,128)(2,1)}, bf16[512,512]{1,0:T(8,128)(2,1)}, u32[]{:S(2)}, u32[]{:S(2)}) collective-permute-start(bf16[512,512]{1,0:T(8,128)(2,1)} %table_ref.1), channel_id=1, source_target_pairs={{0,2},{1,3},{2,0},{3,1},{4,6},{5,7},{6,4},{7,5},{8,10},{9,11},{10,... | collective-permute-start | bytes 1572872 | tf_op jit(solution)/shard_map/ppermute | solution.py:19
  3.1 1.1 %copy-done.1 = bf16[256,3,512]{2,0,1:T(8,128)(2,1)S(1)} copy-done((bf16[256,3,512]{2,0,1:T(8,128)(2,1)S(1)}, bf16[256,3,512]{2,0,1:T(8,128)(2,1)}, u32[]{:S(2)}) %copy-start.1) | copy-done | bytes 786456
  4.2 1.1 %shard_map.84 = (bf16[2,192,256]{2,1,0:T(8,128)(2,1)S(1)}, bf16[2,192,256]{2,1,0:T(8,128)(2,1)S(1)}, bf16[2,192,256]{2,1,0:T(8,128)(2,1)S(1)}, bf16[2,192,256]{2,1,0:T(8,128)(2,1)S(1)}) custom-call(s32[5]{0:T(128)S(1)} %stack.52.where_ref, bf16[3,256,512]{2,1,0:T(8,128)(2,1)S(1)} %bitcast.11), custom_call_target="tpu_custom_call" | custom-call | flops 1100000000 | bytes 1572864 | tf_op jit(solution)/shard_map/pallas_call | solution.py:262
  5.3 1.6 %collective-permute-start.12 = (bf16[2,192,256]{2,1,0:T(8,128)(2,1)S(1)}, bf16[2,192,256]{2,1,0:T(8,128)(2,1)S(1)}, u32[]{:S(2)}, u32[]{:S(2)}) collective-permute-start(bf16[2,192,256]{2,1,0:T(8,128)(2,1)S(1)} %get-tuple-element.21), channel_id=1, source_target_pairs={{0,4},{4,0},{8,12},{12,8},{16,20},{20,16},{24,28},{28,24},{1,5},{5... | collective-permute-start | bytes 589832 | tf_op jit(solution)/shard_map/ppermute | solution.py:19
  6.9 1.6 %collective-permute-start.13 = (bf16[2,192,256]{2,1,0:T(8,128)(2,1)S(1)}, bf16[2,192,256]{2,1,0:T(8,128)(2,1)S(1)}, u32[]{:S(2)}, u32[]{:S(2)}) collective-permute-start(bf16[2,192,256]{2,1,0:T(8,128)(2,1)S(1)} %get-tuple-element.22), channel_id=1, source_target_pairs={{0,8},{4,12},{8,0},{12,4},{16,24},{20,28},{24,16},{28,20},{1,9},{5... | collective-permute-start | bytes 589832 | tf_op jit(solution)/shard_map/ppermute | solution.py:19
  8.4 0.4 collective-permute-start.14
  8.9 2.6 %collective-permute-start = (bf16[512,256]{1,0:T(8,128)(2,1)}, bf16[512,256]{1,0:T(8,128)(2,1)}, u32[]{:S(2)}, u32[]{:S(2)}) collective-permute-start(bf16[512,256]{1,0:T(8,128)(2,1)} %param.15), channel_id=1, source_target_pairs={{0,16},{4,20},{8,24},{12,28},{16,0},{20,4},{24,8},{28,12},{1,17},{... | collective-permute-start | bytes 786440 | tf_op jit(solution)/shard_map/ppermute | solution.py:19
  11.6 0.7 collective-permute-done.12.refs_1_
  12.3 0.4 shard_map.82.band_ref
  12.8 7.5 %collective-permute-done.13.refs_2_ = bf16[2,192,256]{2,1,0:T(8,128)(2,1)S(1)} collective-permute-done((bf16[2,192,256]{2,1,0:T(8,128)(2,1)S(1)}, bf16[2,192,256]{2,1,0:T(8,128)(2,1)S(1)}, u32[]{:S(2)}, u32[]{:S(2)}) %collective-permute-start.13) | collective-permute-done | bytes 196640 | tf_op jit(solution)/shard_map/ppermute | solution.py:19
  20.3 4.2 %collective-permute-done.14.refs_3_ = bf16[2,192,256]{2,1,0:T(8,128)(2,1)S(1)} collective-permute-done((bf16[2,192,256]{2,1,0:T(8,128)(2,1)S(1)}, bf16[2,192,256]{2,1,0:T(8,128)(2,1)S(1)}, u32[]{:S(2)}, u32[]{:S(2)}) %collective-permute-start.14) | collective-permute-done | bytes 196640 | tf_op jit(solution)/shard_map/ppermute | solution.py:19
  24.5 2.7 %collective-permute-start.5 = (bf16[512,256]{1,0:T(8,128)(2,1)}, bf16[512,256]{1,0:T(8,128)(2,1)S(1)}, u32[]{:S(2)}, u32[]{:S(2)}) collective-permute-start(bf16[512,256]{1,0:T(8,128)(2,1)} %collective-permute-done), channel_id=1, source_target_pairs={{0,8},{4,12},{8,0},{12,4},{16,24},{20,28},{24,16},{28,20},{1,9},{5... | collective-permute-start | bytes 786440 | tf_op jit(solution)/shard_map/ppermute | solution.py:19
  27.3 1.1 %broadcast_select_fusion.2 = (bf16[512,256]{1,0:T(8,128)(2,1)S(1)}, bf16[512,256]{1,0:T(8,128)(2,1)S(1)}) fusion(bf16[512,256]{1,0:T(8,128)(2,1)} %collective-permute-done, bf16[512,256]{1,0:T(8,128)(2,1)} %param.15, pred[]{:T(512)S(6)} %eq.6), kind=kLoop, calls=%fused_computation.3 | loop fusion | flops 262144 | bytes 1048577 | tf_op jit(solution)/shard_map/jit(_where)/select_n | solution.py:308
  28.4 0.6 collective-permute-start.1
  28.9 0.5 collective-permute-start.2
  29.5 0.7 collective-permute-done.4
  30.2 2.6 %collective-permute-start.15 = (bf16[4,192,256]{2,1,0:T(8,128)(2,1)S(1)}, bf16[4,192,256]{2,1,0:T(8,128)(2,1)S(1)}, u32[]{:S(2)}, u32[]{:S(2)}) collective-permute-start(bf16[4,192,256]{2,1,0:T(8,128)(2,1)S(1)} %pad_maximum_fusion), channel_id=1, source_target_pairs={{0,16},{4,20},{8,24},{12,28},{16,0},{20,4},{24,8},{28,12},{1,17},{... | collective-permute-start | bytes 1179656 | tf_op jit(solution)/shard_map/ppermute | solution.py:19
  32.7 3.6 %collective-permute-done.5 = bf16[512,256]{1,0:T(8,128)(2,1)S(1)} collective-permute-done((bf16[512,256]{1,0:T(8,128)(2,1)}, bf16[512,256]{1,0:T(8,128)(2,1)S(1)}, u32[]{:S(2)}, u32[]{:S(2)}) %collective-permute-start.5) | collective-permute-done | bytes 262176 | tf_op jit(solution)/shard_map/ppermute | solution.py:19
  36.6 3.9 %collective-permute-start.10 = (s32[144]{0:T(256)S(1)}, s32[144]{0:T(256)S(1)}, u32[]{:S(2)}, u32[]{:S(2)}) collective-permute-start(s32[144]{0:T(256)S(1)} %slice.15), channel_id=1, source_target_pairs={{0,4},{4,8},{8,12},{12,16},{16,20},{20,24},{24,28},{1,5},{5,9},{9,... | collective-permute-start | bytes 1736 | tf_op jit(solution)/shard_map/ppermute | solution.py:288
  40.5 2.6 %shard_map.83.normed_ref = bf16[8,512,256]{2,1,0:T(8,128)(2,1)S(1)} custom-call(s32[5]{0:T(128)S(1)} %stack.52.where_ref, f32[4,1,512]{2,1,0:T(1,128)S(1)} %bitcast.12, bf16[512,512]{1,0:T(8,128)(2,1)} %table_ref.1, bf16[512,512]{1,0:T(8,128)(2,1)S(1)} %collective-permute-done.11.refs_1_, bf16[512,512]{1,0:T(8,128)(2,1)} %collective-permute-done.8.refs_2_, ...), custom_call_target="tpu_custom_call" | custom-call | flops 1650000000 | bytes 4194304 | tf_op jit(solution)/shard_map/pallas_call | solution.py:294
  43.3 0.8 collective-permute-start.3
  44.1 5.7 %collective-permute-done.15.crossing_ref = bf16[4,192,256]{2,1,0:T(8,128)(2,1)S(1)} collective-permute-done((bf16[4,192,256]{2,1,0:T(8,128)(2,1)S(1)}, bf16[4,192,256]{2,1,0:T(8,128)(2,1)S(1)}, u32[]{:S(2)}, u32[]{:S(2)}) %collective-permute-start.15) | collective-permute-done | bytes 393248 | tf_op jit(solution)/shard_map/ppermute | solution.py:19
  49.8 2.2 %shard_map.85.refs_0_ = bf16[192,512]{1,0:T(8,128)(2,1)} custom-call(s32[5]{0:T(128)S(1)} %stack.52.where_ref, bf16[8,512,256]{2,1,0:T(8,128)(2,1)S(1)} %shard_map.83.normed_ref, bf16[4,192,256]{2,1,0:T(8,128)(2,1)S(1)} %collective-permute-done.15.crossing_ref, bf16[2,192,256]{2,1,0:T(8,128)(2,1)S(1)} %get-tuple-element.25.refs_0_, ...), custom_call_target="tpu_custom_call" | custom-call | flops 11000000512 | bytes 2883584 | tf_op jit(solution)/shard_map/pallas_call | solution.py:313
  52.0 1.5 %collective-permute-start.16 = (bf16[192,512]{1,0:T(8,128)(2,1)}, bf16[192,512]{1,0:T(8,128)(2,1)}, u32[]{:S(2)}, u32[]{:S(2)}) collective-permute-start(bf16[192,512]{1,0:T(8,128)(2,1)} %shard_map.85.refs_0_), channel_id=1, source_target_pairs={{0,4},{4,0},{8,12},{12,8},{16,20},{20,16},{24,28},{28,24},{1,5},{5... | collective-permute-start | bytes 589832 | tf_op jit(solution)/shard_map/ppermute | solution.py:19
  53.6 0.7 copy-done.4
  54.4 0.7 copy-done.6
  55.1 0.7 copy-done.8
  56.1 4.2 %collective-permute-start.20 = (bf16[192,512]{1,0:T(8,128)(2,1)}, bf16[192,512]{1,0:T(8,128)(2,1)S(1)}, u32[]{:S(2)}, u32[]{:S(2)}) collective-permute-start(bf16[192,512]{1,0:T(8,128)(2,1)} %shard_map.85.refs_0_), channel_id=1, source_target_pairs={{0,16},{4,20},{8,24},{12,28},{16,0},{20,4},{24,8},{28,12},{1,17},{... | collective-permute-start | bytes 589832 | tf_op jit(solution)/shard_map/ppermute | solution.py:19
  60.3 2.6 %collective-permute-done.17.refs_0_ = bf16[192,512]{1,0:T(8,128)(2,1)} collective-permute-done((bf16[192,512]{1,0:T(8,128)(2,1)}, bf16[192,512]{1,0:T(8,128)(2,1)}, u32[]{:S(2)}, u32[]{:S(2)}) %collective-permute-start.17) | collective-permute-done | bytes 196640 | tf_op jit(solution)/shard_map/ppermute | solution.py:19
  63.2 3.2 %shard_map.86.refs_0_ = bf16[1024,128]{1,0:T(8,128)(2,1)S(1)} custom-call(s32[2]{0:T(128)S(1)} %pad_add_fusion.1.where_ref, s32[1168,1]{1,0:T(8,128)S(1)} %copy.13.ids_ref, f32[7,3,512]{2,1,0:T(4,128)S(1)} %copy.14.short_ref, f32[1,512]{1,0:T(1,128)S(1)} %bitcast.13, bf16[32,256,128]{2,1,0:T(8,128)(2,1)S(1)} %shard_map.82.band_ref, ...), custom_call_target="tpu_custom_call" | custom-call | flops 3849999872 | bytes 2392064 | tf_op jit(solution)/shard_map/pallas_call | solution.py:340
  66.3 1.3 %collective-permute-done.20.refs_0_ = bf16[192,512]{1,0:T(8,128)(2,1)S(1)} collective-permute-done((bf16[192,512]{1,0:T(8,128)(2,1)}, bf16[192,512]{1,0:T(8,128)(2,1)S(1)}, u32[]{:S(2)}, u32[]{:S(2)}) %collective-permute-start.20) | collective-permute-done | bytes 196640 | tf_op jit(solution)/shard_map/ppermute | solution.py:19
  67.6 0.6 collective-permute-start.21
  68.2 1.4 %collective-permute-start.19 = (bf16[1024,128]{1,0:T(8,128)(2,1)S(1)}, bf16[1024,128]{1,0:T(8,128)(2,1)S(1)}, u32[]{:S(2)}, u32[]{:S(2)}) collective-permute-start(bf16[1024,128]{1,0:T(8,128)(2,1)S(1)} %shard_map.86.refs_0_), channel_id=1, source_target_pairs={{0,2},{1,3},{2,0},{3,1},{4,6},{5,7},{6,4},{7,5},{8,10},{9,11},{10,... | collective-permute-start | bytes 786440 | tf_op jit(solution)/shard_map/ppermute | solution.py:19
  69.6 1.5 %collective-permute-done.18.refs_1_ = bf16[192,512]{1,0:T(8,128)(2,1)S(1)} collective-permute-done((bf16[192,512]{1,0:T(8,128)(2,1)}, bf16[192,512]{1,0:T(8,128)(2,1)S(1)}, u32[]{:S(2)}, u32[]{:S(2)}) %collective-permute-start.18) | collective-permute-done | bytes 196640 | tf_op jit(solution)/shard_map/ppermute | solution.py:19
  71.1 3.1 %shard_map.87.refs_1_ = bf16[1024,128]{1,0:T(8,128)(2,1)S(1)} custom-call(s32[2]{0:T(128)S(1)} %pad_add_fusion.2.where_ref, s32[1168,1]{1,0:T(8,128)S(1)} %copy.13.ids_ref, f32[7,3,512]{2,1,0:T(4,128)S(1)} %copy.14.short_ref, f32[1,512]{1,0:T(1,128)S(1)} %bitcast.14, bf16[32,256,128]{2,1,0:T(8,128)(2,1)S(1)} %shard_map.82.band_ref, ...), custom_call_target="tpu_custom_call" | custom-call | flops 3849999872 | bytes 2392064 | tf_op jit(solution)/shard_map/pallas_call | solution.py:340
  74.2 2.4 %collective-permute-start.24 = (bf16[1024,128]{1,0:T(8,128)(2,1)S(1)}, bf16[1024,128]{1,0:T(8,128)(2,1)S(1)}, u32[]{:S(2)}, u32[]{:S(2)}) collective-permute-start(bf16[1024,128]{1,0:T(8,128)(2,1)S(1)} %shard_map.87.refs_1_), channel_id=1, source_target_pairs={{0,2},{1,3},{2,0},{3,1},{4,6},{5,7},{6,4},{7,5},{8,10},{9,11},{10,... | collective-permute-start | bytes 786440 | tf_op jit(solution)/shard_map/ppermute | solution.py:19
  76.6 0.6 collective-permute-start.23
  77.1 0.3 collective-permute-done.19.refs_4_
  77.4 2.1 %shard_map.88.refs_2_ = bf16[1024,128]{1,0:T(8,128)(2,1)S(1)} custom-call(s32[2]{0:T(128)S(1)} %pad_add_fusion.3.where_ref, s32[1168,1]{1,0:T(8,128)S(1)} %copy.13.ids_ref, f32[7,3,512]{2,1,0:T(4,128)S(1)} %copy.14.short_ref, f32[1,512]{1,0:T(1,128)S(1)} %bitcast.15, bf16[32,256,128]{2,1,0:T(8,128)(2,1)S(1)} %shard_map.82.band_ref, ...), custom_call_target="tpu_custom_call" | custom-call | flops 3849999872 | bytes 2392064 | tf_op jit(solution)/shard_map/pallas_call | solution.py:340
  79.6 0.5 collective-permute-start.26
  80.1 2.1 %collective-permute-done.23.refs_1_ = bf16[192,512]{1,0:T(8,128)(2,1)S(1)} collective-permute-done((bf16[192,512]{1,0:T(8,128)(2,1)S(1)}, bf16[192,512]{1,0:T(8,128)(2,1)S(1)}, u32[]{:S(2)}, u32[]{:S(2)}) %collective-permute-start.23) | collective-permute-done | bytes 196640 | tf_op jit(solution)/shard_map/ppermute | solution.py:19
  82.2 2.1 %shard_map.89.refs_3_ = bf16[1024,128]{1,0:T(8,128)(2,1)S(1)} custom-call(s32[2]{0:T(128)S(1)} %pad_add_fusion.4.where_ref, s32[1168,1]{1,0:T(8,128)S(1)} %copy.13.ids_ref, f32[7,3,512]{2,1,0:T(4,128)S(1)} %copy.14.short_ref, f32[1,512]{1,0:T(1,128)S(1)} %bitcast.16, bf16[32,256,128]{2,1,0:T(8,128)(2,1)S(1)} %shard_map.82.band_ref, ...), custom_call_target="tpu_custom_call" | custom-call | flops 3849999872 | bytes 2392064 | tf_op jit(solution)/shard_map/pallas_call | solution.py:340
  84.5 4.1 %shard_map.90 = (bf16[2,1024,512]{2,1,0:T(8,128)(2,1)S(1)}, bf16[2,256,512]{2,1,0:T(8,128)(2,1)S(1)}) custom-call(s32[5]{0:T(128)S(1)} %stack.52.where_ref, bf16[1024,128]{1,0:T(8,128)(2,1)S(1)} %shard_map.86.refs_0_, bf16[1024,128]{1,0:T(8,128)(2,1)S(1)} %shard_map.87.refs_1_, bf16[1024,128]{1,0:T(8,128)(2,1)S(1)} %shard_map.88.refs_2_, ...), custom_call_target="tpu_custom_call" | custom-call | flops 4400000000 | bytes 4194304 | tf_op jit(solution)/shard_map/pallas_call | solution.py:371
  88.6 2.7 %collective-permute-done.27.refs_1_ = bf16[1024,128]{1,0:T(8,128)(2,1)S(1)} collective-permute-done((bf16[1024,128]{1,0:T(8,128)(2,1)S(1)}, bf16[1024,128]{1,0:T(8,128)(2,1)S(1)}, u32[]{:S(2)}, u32[]{:S(2)}) %collective-permute-start.27) | collective-permute-done | bytes 262176 | tf_op jit(solution)/shard_map/ppermute | solution.py:19
  91.3 1.1 %shard_map.92 = bf16[1024,512]{1,0:T(8,128)(2,1)S(1)} custom-call(bf16[2,1024,512]{2,1,0:T(8,128)(2,1)S(1)} %get-tuple-element.29.most_ref, bf16[2,256,512]{2,1,0:T(8,128)(2,1)S(1)} %get-tuple-element.30.weight_ref, bf16[1024,128]{1,0:T(8,128)(2,1)S(1)} %collective-permute-done.26.refs_0_, bf16[1024,128]{1,0:T(8,128)(2,1)S(1)} %collective-permute-done.27.refs_1_), custom_call_target="tpu_custom_call" | custom-call | flops 1650000000 | bytes 4194304 | tf_op jit(solution)/shard_map/pallas_call | solution.py:408
  92.6 1.8 %shard_map.91.refs_2_ = bf16[1024,512]{1,0:T(8,128)(2,1)S(1)} custom-call(s32[1168,1]{1,0:T(8,128)S(1)} %copy.13.ids_ref, bf16[512,512]{1,0:T(8,128)(2,1)} %table_ref.1), custom_call_target="tpu_custom_call" | custom-call | flops 1100000000 | bytes 1048576 | tf_op jit(solution)/shard_map/pallas_call | solution.py:323
  94.4 0.8 collective-permute-done.28.refs_3_
  95.2 2.4 %shard_map.93 = bf16[1024,512]{1,0:T(8,128)(2,1)} custom-call(bf16[2,1024,512]{2,1,0:T(8,128)(2,1)S(1)} %get-tuple-element.29.most_ref, bf16[2,256,512]{2,1,0:T(8,128)(2,1)S(1)} %get-tuple-element.30.weight_ref, bf16[1024,128]{1,0:T(8,128)(2,1)S(1)} %collective-permute-done.26.refs_0_, bf16[1024,128]{1,0:T(8,128)(2,1)S(1)} %collective-permute-done.27.refs_1_, ...), custom_call_target="tpu_custom_call" | custom-call | flops 1650000000 | bytes 4194304 | tf_op jit(solution)/shard_map/pallas_call | solution.py:409
  (68 shorter events, 1.6 us)
Async XLA Ops:
  0.0 27.2 %collective-permute-start.8 = (bf16[512,512]{1,0:T(8,128)(2,1)}, bf16[512,512]{1,0:T(8,128)(2,1)}, u32[]{:S(2)}, u32[]{:S(2)}) collective-permute-start(bf16[512,512]{1,0:T(8,128)(2,1)} %table_ref.1), channel_id=1, source_target_pairs={{0,2},{1,3},{2,0},{3,1},{4,6},{5,7},{6,4},{7,5},{8,10},{9,11},{10,... | collective-permute-start | bytes 1572872 | tf_op jit(solution)/shard_map/ppermute | solution.py:19
  3.1 1.1 %copy-start.1 = (bf16[256,3,512]{2,0,1:T(8,128)(2,1)S(1)}, bf16[256,3,512]{2,0,1:T(8,128)(2,1)}, u32[]{:S(2)}) copy-start(bf16[256,3,512]{2,0,1:T(8,128)(2,1)} %param.11) | copy-start | bytes 2359300
  4.2 7.3 %copy-start.12 = (f32[7,3,512]{2,0,1:T(8,128)S(1)}, f32[7,3,512]{2,0,1:T(8,128)}, u32[]{:S(2)}) copy-start(f32[7,3,512]{2,0,1:T(8,128)} %param.12) | copy-start | bytes 129028
  4.2 8.1 %copy-start = (bf16[32,128]{1,0:T(8,128)(2,1)S(1)}, bf16[32,128]{1,0:T(8,128)(2,1)}, u32[]{:S(2)}) copy-start(bf16[32,128]{1,0:T(8,128)(2,1)} %filter_ref.1) | copy-start | bytes 24580
  5.3 7.0 %collective-permute-start.12 = (bf16[2,192,256]{2,1,0:T(8,128)(2,1)S(1)}, bf16[2,192,256]{2,1,0:T(8,128)(2,1)S(1)}, u32[]{:S(2)}, u32[]{:S(2)}) collective-permute-start(bf16[2,192,256]{2,1,0:T(8,128)(2,1)S(1)} %get-tuple-element.21), channel_id=1, source_target_pairs={{0,4},{4,0},{8,12},{12,8},{16,20},{20,16},{24,28},{28,24},{1,5},{5... | collective-permute-start | bytes 589832 | tf_op jit(solution)/shard_map/ppermute | solution.py:19
  6.9 13.5 %collective-permute-start.13 = (bf16[2,192,256]{2,1,0:T(8,128)(2,1)S(1)}, bf16[2,192,256]{2,1,0:T(8,128)(2,1)S(1)}, u32[]{:S(2)}, u32[]{:S(2)}) collective-permute-start(bf16[2,192,256]{2,1,0:T(8,128)(2,1)S(1)} %get-tuple-element.22), channel_id=1, source_target_pairs={{0,8},{4,12},{8,0},{12,4},{16,24},{20,28},{24,16},{28,20},{1,9},{5... | collective-permute-start | bytes 589832 | tf_op jit(solution)/shard_map/ppermute | solution.py:19
  8.4 16.1 %collective-permute-start.14 = (bf16[2,192,256]{2,1,0:T(8,128)(2,1)S(1)}, bf16[2,192,256]{2,1,0:T(8,128)(2,1)S(1)}, u32[]{:S(2)}, u32[]{:S(2)}) collective-permute-start(bf16[2,192,256]{2,1,0:T(8,128)(2,1)S(1)} %get-tuple-element.23), channel_id=1, source_target_pairs={{0,12},{4,8},{8,4},{12,0},{16,28},{20,24},{24,20},{28,16},{1,13},{... | collective-permute-start | bytes 589832 | tf_op jit(solution)/shard_map/ppermute | solution.py:19
  8.9 15.7 %collective-permute-start = (bf16[512,256]{1,0:T(8,128)(2,1)}, bf16[512,256]{1,0:T(8,128)(2,1)}, u32[]{:S(2)}, u32[]{:S(2)}) collective-permute-start(bf16[512,256]{1,0:T(8,128)(2,1)} %param.15), channel_id=1, source_target_pairs={{0,16},{4,20},{8,24},{12,28},{16,0},{20,4},{24,8},{28,12},{1,17},{... | collective-permute-start | bytes 786440 | tf_op jit(solution)/shard_map/ppermute | solution.py:19
  12.3 16.7 %collective-permute-start.11 = (bf16[512,512]{1,0:T(8,128)(2,1)}, bf16[512,512]{1,0:T(8,128)(2,1)S(1)}, u32[]{:S(2)}, u32[]{:S(2)}) collective-permute-start(bf16[512,512]{1,0:T(8,128)(2,1)} %table_ref.1), channel_id=1, source_target_pairs={{0,1},{1,0},{2,3},{3,2},{4,5},{5,4},{6,7},{7,6},{8,9},{9,8},{10,11... | collective-permute-start | bytes 1572872 | tf_op jit(solution)/shard_map/ppermute | solution.py:19
  12.7 23.8 %copy-start.13 = (s32[1024]{0:T(1024)S(1)}, s32[1024]{0:T(1024)}, u32[]{:S(2)}) copy-start(s32[1024]{0:T(1024)} %param.8) | copy-start | bytes 12292
  12.7 27.8 %copy-start.10 = (f32[2048]{0:T(1024)S(1)}, f32[2048]{0:T(1024)}, u32[]{:S(2)}) copy-start(f32[2048]{0:T(1024)} %param.10) | copy-start | bytes 24580
  20.3 9.8 %collective-permute-start.4 = (bf16[512,256]{1,0:T(8,128)(2,1)}, bf16[512,256]{1,0:T(8,128)(2,1)S(1)}, u32[]{:S(2)}, u32[]{:S(2)}) collective-permute-start(bf16[512,256]{1,0:T(8,128)(2,1)} %param.15), channel_id=1, source_target_pairs={{0,8},{4,12},{8,0},{12,4},{16,24},{20,28},{24,16},{28,20},{1,9},{5... | collective-permute-start | bytes 786440 | tf_op jit(solution)/shard_map/ppermute | solution.py:19
  24.5 11.9 %collective-permute-start.5 = (bf16[512,256]{1,0:T(8,128)(2,1)}, bf16[512,256]{1,0:T(8,128)(2,1)S(1)}, u32[]{:S(2)}, u32[]{:S(2)}) collective-permute-start(bf16[512,256]{1,0:T(8,128)(2,1)} %collective-permute-done), channel_id=1, source_target_pairs={{0,8},{4,12},{8,0},{12,4},{16,24},{20,28},{24,16},{28,20},{1,9},{5... | collective-permute-start | bytes 786440 | tf_op jit(solution)/shard_map/ppermute | solution.py:19
  27.2 9.3 %collective-permute-start.9 = (bf16[512,512]{1,0:T(8,128)(2,1)}, bf16[512,512]{1,0:T(8,128)(2,1)S(1)}, u32[]{:S(2)}, u32[]{:S(2)}) collective-permute-start(bf16[512,512]{1,0:T(8,128)(2,1)} %collective-permute-done.8.refs_2_), channel_id=1, source_target_pairs={{0,1},{1,0},{2,3},{3,2},{4,5},{5,4},{6,7},{7,6},{8,9},{9,8},{10,11... | collective-permute-start | bytes 1572872 | tf_op jit(solution)/shard_map/ppermute | solution.py:19
  28.4 14.8 %collective-permute-start.1 = (bf16[512,256]{1,0:T(8,128)(2,1)S(1)}, bf16[512,256]{1,0:T(8,128)(2,1)S(1)}, u32[]{:S(2)}, u32[]{:S(2)}) collective-permute-start(bf16[512,256]{1,0:T(8,128)(2,1)S(1)} %get-tuple-element.33), channel_id=1, source_target_pairs={{0,2},{1,3},{2,0},{3,1},{4,6},{5,7},{6,4},{7,5},{8,10},{9,11},{10,... | collective-permute-start | bytes 786440 | tf_op jit(solution)/shard_map/ppermute | solution.py:19
  28.9 24.6 %collective-permute-start.2 = (bf16[512,256]{1,0:T(8,128)(2,1)S(1)}, bf16[512,256]{1,0:T(8,128)(2,1)S(1)}, u32[]{:S(2)}, u32[]{:S(2)}) collective-permute-start(bf16[512,256]{1,0:T(8,128)(2,1)S(1)} %get-tuple-element.34.refs_6_), channel_id=1, source_target_pairs={{0,4},{4,0},{8,12},{12,8},{16,20},{20,16},{24,28},{28,24},{1,5},{5... | collective-permute-start | bytes 786440 | tf_op jit(solution)/shard_map/ppermute | solution.py:19
  30.2 19.6 %collective-permute-start.15 = (bf16[4,192,256]{2,1,0:T(8,128)(2,1)S(1)}, bf16[4,192,256]{2,1,0:T(8,128)(2,1)S(1)}, u32[]{:S(2)}, u32[]{:S(2)}) collective-permute-start(bf16[4,192,256]{2,1,0:T(8,128)(2,1)S(1)} %pad_maximum_fusion), channel_id=1, source_target_pairs={{0,16},{4,20},{8,24},{12,28},{16,0},{20,4},{24,8},{28,12},{1,17},{... | collective-permute-start | bytes 1179656 | tf_op jit(solution)/shard_map/ppermute | solution.py:19
  36.4 18.0 %collective-permute-start.7 = (bf16[512,256]{1,0:T(8,128)(2,1)S(1)}, bf16[512,256]{1,0:T(8,128)(2,1)S(1)}, u32[]{:S(2)}, u32[]{:S(2)}) collective-permute-start(bf16[512,256]{1,0:T(8,128)(2,1)S(1)} %get-tuple-element.32.refs_10_), channel_id=1, source_target_pairs={{0,4},{4,0},{8,12},{12,8},{16,20},{20,16},{24,28},{28,24},{1,5},{5... | collective-permute-start | bytes 786440 | tf_op jit(solution)/shard_map/ppermute | solution.py:19
  36.6 6.7 %collective-permute-start.10 = (s32[144]{0:T(256)S(1)}, s32[144]{0:T(256)S(1)}, u32[]{:S(2)}, u32[]{:S(2)}) collective-permute-start(s32[144]{0:T(256)S(1)} %slice.15), channel_id=1, source_target_pairs={{0,4},{4,8},{8,12},{12,16},{16,20},{20,24},{24,28},{1,5},{5,9},{9,... | collective-permute-start | bytes 1736 | tf_op jit(solution)/shard_map/ppermute | solution.py:288
  43.2 8.9 %copy-start.2 = (bf16[512,256]{1,0:T(8,128)(2,1)}, bf16[512,256]{1,0:T(8,128)(2,1)S(1)}, u32[]{:S(2)}) copy-start(bf16[512,256]{1,0:T(8,128)(2,1)S(1)} %collective-permute-done.1.refs_7_) | copy-start | bytes 786436
  43.2 12.7 %collective-permute-start.6 = (bf16[512,256]{1,0:T(8,128)(2,1)S(1)}, bf16[512,256]{1,0:T(8,128)(2,1)}, u32[]{:S(2)}, u32[]{:S(2)}) collective-permute-start(bf16[512,256]{1,0:T(8,128)(2,1)S(1)} %get-tuple-element.31), channel_id=1, source_target_pairs={{0,2},{1,3},{2,0},{3,1},{4,6},{5,7},{6,4},{7,5},{8,10},{9,11},{10,... | collective-permute-start | bytes 786440 | tf_op jit(solution)/shard_map/ppermute | solution.py:19
  43.3 11.9 %collective-permute-start.3 = (bf16[512,256]{1,0:T(8,128)(2,1)S(1)}, bf16[512,256]{1,0:T(8,128)(2,1)S(1)}, u32[]{:S(2)}, u32[]{:S(2)}) collective-permute-start(bf16[512,256]{1,0:T(8,128)(2,1)S(1)} %collective-permute-done.1.refs_7_), channel_id=1, source_target_pairs={{0,4},{4,0},{8,12},{12,8},{16,20},{20,16},{24,28},{28,24},{1,5},{5... | collective-permute-start | bytes 786440 | tf_op jit(solution)/shard_map/ppermute | solution.py:19
  44.1 19.0 %copy-start.11 = (f32[512]{0:T(512)S(1)}, f32[512]{0:T(512)}, u32[]{:S(2)}) copy-start(f32[512]{0:T(512)} %param.14) | copy-start | bytes 6148
  52.0 11.1 %collective-permute-start.16 = (bf16[192,512]{1,0:T(8,128)(2,1)}, bf16[192,512]{1,0:T(8,128)(2,1)}, u32[]{:S(2)}, u32[]{:S(2)}) collective-permute-start(bf16[192,512]{1,0:T(8,128)(2,1)} %shard_map.85.refs_0_), channel_id=1, source_target_pairs={{0,4},{4,0},{8,12},{12,8},{16,20},{20,16},{24,28},{28,24},{1,5},{5... | collective-permute-start | bytes 589832 | tf_op jit(solution)/shard_map/ppermute | solution.py:19
  53.6 0.7 copy-start.4
  54.3 8.7 %collective-permute-start.17 = (bf16[192,512]{1,0:T(8,128)(2,1)}, bf16[192,512]{1,0:T(8,128)(2,1)}, u32[]{:S(2)}, u32[]{:S(2)}) collective-permute-start(bf16[192,512]{1,0:T(8,128)(2,1)} %shard_map.85.refs_0_), channel_id=1, source_target_pairs={{0,8},{4,12},{8,0},{12,4},{16,24},{20,28},{24,16},{28,20},{1,9},{5... | collective-permute-start | bytes 589832 | tf_op jit(solution)/shard_map/ppermute | solution.py:19
  54.4 0.7 copy-start.6
  55.1 0.7 copy-start.8
  56.1 11.5 %collective-permute-start.20 = (bf16[192,512]{1,0:T(8,128)(2,1)}, bf16[192,512]{1,0:T(8,128)(2,1)S(1)}, u32[]{:S(2)}, u32[]{:S(2)}) collective-permute-start(bf16[192,512]{1,0:T(8,128)(2,1)} %shard_map.85.refs_0_), channel_id=1, source_target_pairs={{0,16},{4,20},{8,24},{12,28},{16,0},{20,4},{24,8},{28,12},{1,17},{... | collective-permute-start | bytes 589832 | tf_op jit(solution)/shard_map/ppermute | solution.py:19
  60.3 24.2 %collective-permute-start.25 = (bf16[512,256]{1,0:T(8,128)(2,1)}, bf16[512,256]{1,0:T(8,128)(2,1)S(1)}, u32[]{:S(2)}, u32[]{:S(2)}) collective-permute-start(bf16[512,256]{1,0:T(8,128)(2,1)} %collective-permute-done.6.refs_11_), channel_id=1, source_target_pairs={{0,4},{4,0},{8,12},{12,8},{16,20},{20,16},{24,28},{28,24},{1,5},{5... | collective-permute-start | bytes 786440 | tf_op jit(solution)/shard_map/ppermute | solution.py:19
  63.0 8.2 %collective-permute-start.18 = (bf16[192,512]{1,0:T(8,128)(2,1)}, bf16[192,512]{1,0:T(8,128)(2,1)S(1)}, u32[]{:S(2)}, u32[]{:S(2)}) collective-permute-start(bf16[192,512]{1,0:T(8,128)(2,1)} %collective-permute-done.17.refs_0_), channel_id=1, source_target_pairs={{0,4},{4,0},{8,12},{12,8},{16,20},{20,16},{24,28},{28,24},{1,5},{5... | collective-permute-start | bytes 589832 | tf_op jit(solution)/shard_map/ppermute | solution.py:19
  67.6 8.9 %collective-permute-start.21 = (bf16[192,512]{1,0:T(8,128)(2,1)S(1)}, bf16[192,512]{1,0:T(8,128)(2,1)S(1)}, u32[]{:S(2)}, u32[]{:S(2)}) collective-permute-start(bf16[192,512]{1,0:T(8,128)(2,1)S(1)} %collective-permute-done.20.refs_0_), channel_id=1, source_target_pairs={{0,4},{4,0},{8,12},{12,8},{16,20},{20,16},{24,28},{28,24},{1,5},{5... | collective-permute-start | bytes 589832 | tf_op jit(solution)/shard_map/ppermute | solution.py:19
  68.2 11.9 %collective-permute-start.22 = (bf16[192,512]{1,0:T(8,128)(2,1)S(1)}, bf16[192,512]{1,0:T(8,128)(2,1)S(1)}, u32[]{:S(2)}, u32[]{:S(2)}) collective-permute-start(bf16[192,512]{1,0:T(8,128)(2,1)S(1)} %collective-permute-done.20.refs_0_), channel_id=1, source_target_pairs={{0,8},{4,12},{8,0},{12,4},{16,24},{20,28},{24,16},{28,20},{1,9},{5... | collective-permute-start | bytes 589832 | tf_op jit(solution)/shard_map/ppermute | solution.py:19
  68.2 9.2 %collective-permute-start.19 = (bf16[1024,128]{1,0:T(8,128)(2,1)S(1)}, bf16[1024,128]{1,0:T(8,128)(2,1)S(1)}, u32[]{:S(2)}, u32[]{:S(2)}) collective-permute-start(bf16[1024,128]{1,0:T(8,128)(2,1)S(1)} %shard_map.86.refs_0_), channel_id=1, source_target_pairs={{0,2},{1,3},{2,0},{3,1},{4,6},{5,7},{6,4},{7,5},{8,10},{9,11},{10,... | collective-permute-start | bytes 786440 | tf_op jit(solution)/shard_map/ppermute | solution.py:19
  74.2 10.3 %collective-permute-start.24 = (bf16[1024,128]{1,0:T(8,128)(2,1)S(1)}, bf16[1024,128]{1,0:T(8,128)(2,1)S(1)}, u32[]{:S(2)}, u32[]{:S(2)}) collective-permute-start(bf16[1024,128]{1,0:T(8,128)(2,1)S(1)} %shard_map.87.refs_1_), channel_id=1, source_target_pairs={{0,2},{1,3},{2,0},{3,1},{4,6},{5,7},{6,4},{7,5},{8,10},{9,11},{10,... | collective-permute-start | bytes 786440 | tf_op jit(solution)/shard_map/ppermute | solution.py:19
  76.6 5.7 %collective-permute-start.23 = (bf16[192,512]{1,0:T(8,128)(2,1)S(1)}, bf16[192,512]{1,0:T(8,128)(2,1)S(1)}, u32[]{:S(2)}, u32[]{:S(2)}) collective-permute-start(bf16[192,512]{1,0:T(8,128)(2,1)S(1)} %collective-permute-done.21.refs_1_), channel_id=1, source_target_pairs={{0,8},{4,12},{8,0},{12,4},{16,24},{20,28},{24,16},{28,20},{1,9},{5... | collective-permute-start | bytes 589832 | tf_op jit(solution)/shard_map/ppermute | solution.py:19
  79.6 5.0 %copy-start.3 = (bf16[512,256]{1,0:T(8,128)(2,1)S(1)}, bf16[512,256]{1,0:T(8,128)(2,1)}, u32[]{:S(2)}) copy-start(bf16[512,256]{1,0:T(8,128)(2,1)} %copy-done.2) | copy-start | bytes 786436
  79.6 4.9 %copy-start.5 = (bf16[512,256]{1,0:T(8,128)(2,1)S(1)}, bf16[512,256]{1,0:T(8,128)(2,1)}, u32[]{:S(2)}) copy-start(bf16[512,256]{1,0:T(8,128)(2,1)} %copy-done.4) | copy-start | bytes 786436
  79.6 4.9 %copy-start.7 = (bf16[512,256]{1,0:T(8,128)(2,1)S(1)}, bf16[512,256]{1,0:T(8,128)(2,1)}, u32[]{:S(2)}) copy-start(bf16[512,256]{1,0:T(8,128)(2,1)} %copy-done.6) | copy-start | bytes 786436
  79.6 4.9 %copy-start.9 = (bf16[512,256]{1,0:T(8,128)(2,1)S(1)}, bf16[512,256]{1,0:T(8,128)(2,1)}, u32[]{:S(2)}) copy-start(bf16[512,256]{1,0:T(8,128)(2,1)} %copy-done.8) | copy-start | bytes 786436
  79.6 9.0 %collective-permute-start.26 = (bf16[1024,128]{1,0:T(8,128)(2,1)S(1)}, bf16[1024,128]{1,0:T(8,128)(2,1)S(1)}, u32[]{:S(2)}, u32[]{:S(2)}) collective-permute-start(bf16[1024,128]{1,0:T(8,128)(2,1)S(1)} %shard_map.88.refs_2_), channel_id=1, source_target_pairs={{0,2},{1,3},{2,0},{3,1},{4,6},{5,7},{6,4},{7,5},{8,10},{9,11},{10,... | collective-permute-start | bytes 786440 | tf_op jit(solution)/shard_map/ppermute | solution.py:19
  84.4 7.0 %collective-permute-start.27 = (bf16[1024,128]{1,0:T(8,128)(2,1)S(1)}, bf16[1024,128]{1,0:T(8,128)(2,1)S(1)}, u32[]{:S(2)}, u32[]{:S(2)}) collective-permute-start(bf16[1024,128]{1,0:T(8,128)(2,1)S(1)} %shard_map.89.refs_3_), channel_id=1, source_target_pairs={{0,2},{1,3},{2,0},{3,1},{4,6},{5,7},{6,4},{7,5},{8,10},{9,11},{10,... | collective-permute-start | bytes 786440 | tf_op jit(solution)/shard_map/ppermute | solution.py:19
  92.5 2.7 %collective-permute-start.28 = (bf16[1024,512]{1,0:T(8,128)(2,1)S(1)}, bf16[1024,512]{1,0:T(8,128)(2,1)S(1)}, u32[]{:S(2)}, u32[]{:S(2)}) collective-permute-start(bf16[1024,512]{1,0:T(8,128)(2,1)S(1)} %shard_map.92), channel_id=1, source_target_pairs={{0,1},{1,0},{2,3},{3,2},{4,5},{5,4},{6,7},{7,6},{8,9},{9,8},{10,11... | collective-permute-start | bytes 3145736 | tf_op jit(solution)/shard_map/ppermute | solution.py:19

commit v4 on v3

--- a/solution.py
+++ b/solution.py
@@ -69,15 +69,14 @@
     ).astype(BF)
 
 
-def band_kernel(filter_ref, out_ref):
-    groups, taps = filter_ref.shape
+def bands(line):
+    taps = line.shape[1]
     row = lax.broadcasted_iota(jnp.int32, (taps, taps), 0)
     col = lax.broadcasted_iota(jnp.int32, (taps, taps), 1)
-    for g in range(groups):
-        line = jnp.broadcast_to(filter_ref[g : g + 1, :].astype(F32), (taps, taps))
-        ring = pltpu.roll(line, 0, 1, stride=1, stride_axis=0)
-        out_ref[g, :taps, :] = jnp.where(col < row, ring, 0.0).astype(BF)
-        out_ref[g, taps:, :] = jnp.where(col >= row, ring, 0.0).astype(BF)
+    ring = pltpu.roll(jnp.broadcast_to(line.astype(F32), (taps, taps)), 0, 1, stride=1, stride_axis=0)
+    return jnp.concatenate(
+        [jnp.where(col < row, ring, 0.0), jnp.where(col >= row, ring, 0.0)], axis=0
+    ).astype(BF)
 
 
 def norm_kernel(where_ref, gain_ref, *refs):
@@ -118,13 +117,13 @@
 
 
 def mixer_kernel(
-    group_size, where_ref, ids_ref, short_ref, skip_ref, band_ref, *refs
+    group_size, where_ref, ids_ref, short_ref, skip_ref, filter_ref, *refs
 ):
     pieces = refs[:-6]
     out_ref, rows_ref, proj_ref, product_ref, turned_ref, conv_ref = refs[-6:]
     tokens, width = out_ref.shape
     short_taps = short_ref.shape[0]
-    taps = band_ref.shape[2]
+    taps = filter_ref.shape[1]
     length, vocab = ids_ref.shape[0], rows_ref.shape[1]
     halo = length - tokens
     piece = width // len(pieces)
@@ -162,7 +161,9 @@
         stacked = jnp.concatenate(
             [turned_ref[rows, b * taps : (b + 2) * taps] for b in range(blocks)], axis=0
         )
-        mixed = jnp.dot(stacked, band_ref[g], preferred_element_type=F32)
+        mixed = jnp.dot(
+            stacked, bands(filter_ref[g : g + 1, :]), preferred_element_type=F32
+        )
         for b in range(blocks):
             conv_ref[rows, b * taps : (b + 1) * taps] = mixed[b * group_size : (b + 1) * group_size]
     for b in range(blocks):
@@ -174,13 +175,16 @@
 
 def most_kernel(chunks, late, where_ref, *refs):
     count = 2 * chunks - late
-    gates, weights, (out_ref, last_ref, lhs_ref, rhs_ref) = refs[:count], refs[count:-4], refs[-4:]
+    gates, weights, (out_ref, last_ref, lhs_ref, rhs_ref, sems) = refs[:count], refs[count:-5], refs[-5:]
     tokens, lane = gates[0].shape
     width = chunks * lane
     top, _, cols = rhs_ref.shape
+    copies = []
     for index, weight in enumerate(weights):
         offset, side = index // 2, index % 2
-        rhs_ref[offset ^ where_ref[4], side * width : (side + 1) * width, :] = weight[...]
+        place = rhs_ref.at[offset ^ where_ref[4], pl.ds(side * width, width)]
+        copies.append(pltpu.make_async_copy(weight, place, sems.at[index]))
+        copies[-1].start()
     for index in range(2 * chunks):
         side, m = index // chunks, index % chunks
         begin = pl.multiple_of(side * width + (where_ref[2] ^ m) * lane, lane)
@@ -188,6 +192,8 @@
             lhs_ref[:, pl.ds(begin, lane)] = gates[index][...]
         else:
             lhs_ref[:, pl.ds(begin, lane)] = jnp.zeros((tokens, lane), BF)
+    for copy in copies:
+        copy.wait()
     rows = min(tokens, 256)
     for half in range(2):
         for b in range(top // 2):
@@ -275,15 +281,11 @@
     parts = [over(part, offset) if offset else part for offset, part in enumerate(parts)]
 
     table_row = swap(embed_table, "tp", 2)
-    table_core = swap(embed_table, "tp", 1)
+    table_core = swap(after(embed_table, far[0]), "tp", 1)
     table_both = swap(table_row, "tp", 1)
 
     crossing = after(jnp.stack([part[1] for part in parts]), far[0], table_row, table_core)
     crossing = over(crossing, top)
-
-    bands = call(
-        band_kernel, jax.ShapeDtypeStruct((groups, 2 * taps, taps), BF), 1, cost_us(0.5), groups * taps
-    )(long_filter)
 
     tail = lax.ppermute(after(token_ids, table_both)[tokens - halo :], "seq", [(i, i + 1) for i in range(n * minor - 1)])
     tail = jnp.where(device == 0, -1, tail)
@@ -302,13 +304,6 @@
         scratch_shapes=[pltpu.VMEM((n, vocab, depth), BF), pltpu.SemaphoreType.DMA],
     )(where, norm_gain.reshape(m, 1, width), embed_table, table_core, table_row, table_both)
 
-    halves = []
-    for one, two in zip(near, far, strict=True):
-        kept = jnp.where(same_side, one, two)
-        given = jnp.where(same_side, two, one)
-        given = swap(given, "tp", 2)
-        halves += [kept, given, over(kept, 1), over(given, 1)]
-
     parts[0] = after(parts[0], ids)
     projected = call(
         project_kernel,
@@ -323,6 +318,15 @@
     embedded = call(
         embed_kernel, jax.ShapeDtypeStruct((tokens, width), BF), 2, cost_us(1.0), 2 * tokens * width
     )(ids, embed_table)
+    halves = []
+    for index, (one, two) in enumerate(zip(near, far, strict=True)):
+        if index:
+            one, two = after(one, projected), after(two, projected)
+        kept = jnp.where(same_side, one, two)
+        given = jnp.where(same_side, two, one)
+        given = swap(given, "tp", 2)
+        halves += [kept, given, over(kept, 1), over(given, 1)]
+
     halves[-1] = over(after(halves[-3], projected), 1)
     starts = [projected, over(projected, 2), over(projected, top)]
     gates, row_gates, besides = [], [], []
@@ -336,7 +340,7 @@
         if index == 2:
             at = after(at, row_gates[0])
         if index == 0:
-            at = after(at, *halves[:-1])
+            at = after(at, *halves[:6])
         gate = pl.pallas_call(
             functools.partial(mixer_kernel, width // groups),
             grid_spec=pltpu.PrefetchScalarGridSpec(
@@ -346,7 +350,7 @@
                     pl.BlockSpec((length, 1), lambda i, s: (0, 0)),
                     pl.BlockSpec((short_taps, 3, lane), lambda i, s: (0, 0, s[1])),
                     pl.BlockSpec((1, lane), lambda i, s: (0, s[1])),
-                    pl.BlockSpec((lane * groups // width, 2 * taps, taps), lambda i, s: (s[1], 0, 0)),
+                    pl.BlockSpec((lane * groups // width, taps), lambda i, s: (s[1], 0)),
                 ]
                 + [pl.BlockSpec((3 * piece, vocab), lambda i, s: (0, 0))] * len(pieces),
                 out_specs=pl.BlockSpec((tokens, lane), lambda i, s: (0, 0)),
@@ -363,7 +367,7 @@
             cost_estimate=pl.CostEstimate(
                 flops=cost_us(3.5), bytes_accessed=4 * vocab * length, transcendentals=0
             ),
-        )(at, ids, short_filter, long_skip[None, :], bands, *pieces)
+        )(at, ids, short_filter, long_skip[None, :], long_filter, *pieces)
         gates.append(gate)
         row_gates.append(swap(gate, "tp", 2))
 
@@ -378,10 +382,13 @@
         cost_us(4.0),
         8 * tokens * width,
         room=24,
-        in_specs=[SCALARS] + [WHOLE] * (2 * chunks - late + 2 * top),
+        in_specs=[SCALARS]
+        + [WHOLE] * (2 * chunks - late)
+        + [pl.BlockSpec(memory_space=pltpu.HBM)] * (2 * top),
         scratch_shapes=[
             pltpu.VMEM((tokens, 2 * width), BF),
             pltpu.VMEM((top, 2 * width, width * 2 // top), BF),
+            pltpu.SemaphoreType.DMA((2 * top,)),
         ],
     )(where, *gates, *row_gates[:-late], *halves)
 

time: 98 us -> 94.3 us (0.962)
  Pallas kernels: 26.3 us -> 22.4 us
  starting transfers between devices: 31.9 us -> 34.3 us
  local copies, waits for them, and re-layouts: 3.81 us -> 1.63 us
    ppermute x28, starting transfers between devices: 28 us -> 30.5 us  [swap(): return lax.ppermute(block, axis, [(i, i ^ offset) for i in range(count)])]
    unnamed x29 -> x15, local copies, waits for them, and re-layouts: 3.37 us -> 1.19 us
    pallas_call x4, Pallas kernels: 10.5 us -> 8.74 us  [body(): pl.pallas_call(functools.partial(mixer_kernel, width // groups), grid_spe...]
    pallas_call x1, Pallas kernels: 1.81 us -> 0.77 us  [body(): call(embed_kernel, jax.ShapeDtypeStruct((tokens, width), BF), 2, cost_us(...]
  transfers between devices with their start and end apart: 29 -> 29, of which waited for: 13 -> 11; matrix products, arithmetic and copies ran while one was open for 2% -> 2% of each run, Pallas kernels for 23% -> 20%
where the time goes in v4:
time: 94.3 us; the launch traced here: 94.1 us
  starting transfers between devices  34.3 us (36%)
  waiting for transfers between devices  33.8 us (36%)
  Pallas kernels  22.4 us (24%)
  local copies, waits for them, and re-layouts  1.63 us (2%)
  other arithmetic  1.54 us (2%)
    ppermute x28, waiting for transfers between devices, swap(): return lax.ppermute(block, axis, [(i, i ^ offset) for i in range(count)])  33.8 us
    ppermute x28, starting transfers between devices, swap(): return lax.ppermute(block, axis, [(i, i ^ offset) for i in range(count)])  30.5 us
    pallas_call x4, Pallas kernels, body(): pl.pallas_call(functools.partial(mixer_kernel, width // groups), grid_spe...  8.74 us
    pallas_call x1, Pallas kernels, body(): call(functools.partial(most_kernel, chunks, late), [jax.ShapeDtypeStruct(...  4.04 us
    ppermute x1, starting transfers between devices, body(): lax.ppermute(after(token_ids, table_both)[tokens - halo:], 'seq', [(i, i...  3.82 us
    pallas_call x1, Pallas kernels, body(): stepped(final_kernel, 0, 2)(most, last, *row_gates[-late:], embedded, sent)  2.42 us
    pallas_call x1, Pallas kernels, body(): call(norm_kernel, jax.ShapeDtypeStruct((n, vocab, depth), BF), 6, cost_us...  1.97 us
  transfers between devices with their start and end apart: 29, of which 11 were waited for; matrix products, arithmetic and copies ran while one was open for 2% of the time, Pallas kernels for 20%

profile of v4, /device:TPU:0, one launch (start us, length us, event | category | flops | bytes accessed | tf_op | source)
XLA Modules:
  0.0 94.1 jit_solution(15971718089732900323)
XLA Ops:
  0.0 3.0 %collective-permute-start.6 = (bf16[512,512]{1,0:T(8,128)(2,1)}, bf16[512,512]{1,0:T(8,128)(2,1)S(1)}, u32[]{:S(2)}, u32[]{:S(2)}) collective-permute-start(bf16[512,512]{1,0:T(8,128)(2,1)} %table_ref.1), channel_id=1, source_target_pairs={{0,2},{1,3},{2,0},{3,1},{4,6},{5,7},{6,4},{7,5},{8,10},{9,11},{10,... | collective-permute-start | bytes 1572872 | tf_op jit(solution)/shard_map/ppermute | solution.py:19
  3.0 2.6 %collective-permute-start = (bf16[512,256]{1,0:T(8,128)(2,1)}, bf16[512,256]{1,0:T(8,128)(2,1)}, u32[]{:S(2)}, u32[]{:S(2)}) collective-permute-start(bf16[512,256]{1,0:T(8,128)(2,1)} %param.15), channel_id=1, source_target_pairs={{0,16},{4,20},{8,24},{12,28},{16,0},{20,4},{24,8},{28,12},{1,17},{... | collective-permute-start | bytes 786440 | tf_op jit(solution)/shard_map/ppermute | solution.py:19
  5.6 1.1 %copy-done = bf16[256,3,512]{2,0,1:T(8,128)(2,1)S(1)} copy-done((bf16[256,3,512]{2,0,1:T(8,128)(2,1)S(1)}, bf16[256,3,512]{2,0,1:T(8,128)(2,1)}, u32[]{:S(2)}) %copy-start) | copy-done | bytes 786456
  6.8 1.8 %shard_map.83 = (bf16[2,192,256]{2,1,0:T(8,128)(2,1)S(1)}, bf16[2,192,256]{2,1,0:T(8,128)(2,1)}, bf16[2,192,256]{2,1,0:T(8,128)(2,1)}, bf16[2,192,256]{2,1,0:T(8,128)(2,1)S(1)}) custom-call(s32[5]{0:T(128)S(1)} %stack.52.where_ref, bf16[3,256,512]{2,1,0:T(8,128)(2,1)S(1)} %bitcast.11), custom_call_target="tpu_custom_call" | custom-call | flops 1100000000 | bytes 1572864 | tf_op jit(solution)/shard_map/pallas_call | solution.py:268
  8.6 1.6 %collective-permute-start.8 = (bf16[2,192,256]{2,1,0:T(8,128)(2,1)}, bf16[2,192,256]{2,1,0:T(8,128)(2,1)S(1)}, u32[]{:S(2)}, u32[]{:S(2)}) collective-permute-start(bf16[2,192,256]{2,1,0:T(8,128)(2,1)} %get-tuple-element.23), channel_id=1, source_target_pairs={{0,4},{4,0},{8,12},{12,8},{16,20},{20,16},{24,28},{28,24},{1,5},{5... | collective-permute-start | bytes 589832 | tf_op jit(solution)/shard_map/ppermute | solution.py:19
  10.2 1.6 %collective-permute-start.9 = (bf16[2,192,256]{2,1,0:T(8,128)(2,1)}, bf16[2,192,256]{2,1,0:T(8,128)(2,1)S(1)}, u32[]{:S(2)}, u32[]{:S(2)}) collective-permute-start(bf16[2,192,256]{2,1,0:T(8,128)(2,1)} %get-tuple-element.24), channel_id=1, source_target_pairs={{0,8},{4,12},{8,0},{12,4},{16,24},{20,28},{24,16},{28,20},{1,9},{5... | collective-permute-start | bytes 589832 | tf_op jit(solution)/shard_map/ppermute | solution.py:19
  11.8 0.4 collective-permute-start.10
  12.2 5.5 %collective-permute-done = bf16[512,256]{1,0:T(8,128)(2,1)} collective-permute-done((bf16[512,256]{1,0:T(8,128)(2,1)}, bf16[512,256]{1,0:T(8,128)(2,1)}, u32[]{:S(2)}, u32[]{:S(2)}) %collective-permute-start) | collective-permute-done | bytes 262176 | tf_op jit(solution)/shard_map/ppermute | solution.py:19
  17.7 0.5 collective-permute-start.7
  18.3 0.6 collective-permute-start.4
  18.9 2.8 %collective-permute-done.9.refs_2_ = bf16[2,192,256]{2,1,0:T(8,128)(2,1)S(1)} collective-permute-done((bf16[2,192,256]{2,1,0:T(8,128)(2,1)}, bf16[2,192,256]{2,1,0:T(8,128)(2,1)S(1)}, u32[]{:S(2)}, u32[]{:S(2)}) %collective-permute-start.9) | collective-permute-done | bytes 196640 | tf_op jit(solution)/shard_map/ppermute | solution.py:19
  21.8 4.5 %collective-permute-done.10.refs_3_ = bf16[2,192,256]{2,1,0:T(8,128)(2,1)S(1)} collective-permute-done((bf16[2,192,256]{2,1,0:T(8,128)(2,1)S(1)}, bf16[2,192,256]{2,1,0:T(8,128)(2,1)S(1)}, u32[]{:S(2)}, u32[]{:S(2)}) %collective-permute-start.10) | collective-permute-done | bytes 196640 | tf_op jit(solution)/shard_map/ppermute | solution.py:19
  26.2 1.1 %broadcast_select_fusion.2 = (bf16[512,256]{1,0:T(8,128)(2,1)S(1)}, bf16[512,256]{1,0:T(8,128)(2,1)S(1)}) fusion(bf16[512,256]{1,0:T(8,128)(2,1)} %collective-permute-done, bf16[512,256]{1,0:T(8,128)(2,1)} %param.15, pred[]{:T(512)S(6)} %eq.6), kind=kLoop, calls=%fused_computation.3 | loop fusion | flops 262144 | bytes 1048577 | tf_op jit(solution)/shard_map/jit(_where)/select_n | solution.py:326
  27.3 0.6 collective-permute-start.1
  27.9 1.2 %collective-permute-start.2 = (bf16[512,256]{1,0:T(8,128)(2,1)S(1)}, bf16[512,256]{1,0:T(8,128)(2,1)}, u32[]{:S(2)}, u32[]{:S(2)}) collective-permute-start(bf16[512,256]{1,0:T(8,128)(2,1)S(1)} %get-tuple-element.40.refs_6_), channel_id=1, source_target_pairs={{0,4},{4,0},{8,12},{12,8},{16,20},{20,16},{24,28},{28,24},{1,5},{5... | collective-permute-start | bytes 786440 | tf_op jit(solution)/shard_map/ppermute | solution.py:19
  29.2 0.1 collective-permute-start.11
  29.4 3.8 %collective-permute-start.12 = (s32[144]{0:T(256)S(1)}, s32[144]{0:T(256)S(1)}, u32[]{:S(2)}, u32[]{:S(2)}) collective-permute-start(s32[144]{0:T(256)S(1)} %slice.19), channel_id=1, source_target_pairs={{0,4},{4,8},{8,12},{12,16},{16,20},{20,24},{24,28},{1,5},{5,9},{9,... | collective-permute-start | bytes 1736 | tf_op jit(solution)/shard_map/ppermute | solution.py:290
  33.2 2.0 %shard_map.82.normed_ref = bf16[8,512,256]{2,1,0:T(8,128)(2,1)S(1)} custom-call(s32[5]{0:T(128)S(1)} %stack.52.where_ref, f32[4,1,512]{2,1,0:T(1,128)S(1)} %bitcast.12, bf16[512,512]{1,0:T(8,128)(2,1)S(1)} %copy-done.1, bf16[512,512]{1,0:T(8,128)(2,1)S(1)} %collective-permute-done.5.refs_1_, bf16[512,512]{1,0:T(8,128)(2,1)S(1)} %collective-permute-done.6.refs_2_, ...), custom_call_target="tpu_custom_call" | custom-call | flops 1650000000 | bytes 4194304 | tf_op jit(solution)/shard_map/pallas_call | solution.py:296
  35.2 2.1 %collective-permute-start.13 = (bf16[512,256]{1,0:T(8,128)(2,1)}, bf16[512,256]{1,0:T(8,128)(2,1)S(1)}, u32[]{:S(2)}, u32[]{:S(2)}) collective-permute-start(bf16[512,256]{1,0:T(8,128)(2,1)} %collective-permute-done), channel_id=1, source_target_pairs={{0,8},{4,12},{8,0},{12,4},{16,24},{20,28},{24,16},{28,20},{1,9},{5... | collective-permute-start | bytes 786440 | tf_op jit(solution)/shard_map/ppermute | solution.py:19
  37.3 1.4 %collective-permute-start.3 = (bf16[512,256]{1,0:T(8,128)(2,1)S(1)}, bf16[512,256]{1,0:T(8,128)(2,1)S(1)}, u32[]{:S(2)}, u32[]{:S(2)}) collective-permute-start(bf16[512,256]{1,0:T(8,128)(2,1)S(1)} %collective-permute-done.1.refs_7_), channel_id=1, source_target_pairs={{0,4},{4,0},{8,12},{12,8},{16,20},{20,16},{24,28},{28,24},{1,5},{5... | collective-permute-start | bytes 786440 | tf_op jit(solution)/shard_map/ppermute | solution.py:19
  38.9 7.0 %collective-permute-done.11.crossing_ref = bf16[4,192,256]{2,1,0:T(8,128)(2,1)S(1)} collective-permute-done((bf16[4,192,256]{2,1,0:T(8,128)(2,1)S(1)}, bf16[4,192,256]{2,1,0:T(8,128)(2,1)S(1)}, u32[]{:S(2)}, u32[]{:S(2)}) %collective-permute-start.11) | collective-permute-done | bytes 393248 | tf_op jit(solution)/shard_map/ppermute | solution.py:19
  45.9 1.5 %shard_map.84.refs_0_ = bf16[192,512]{1,0:T(8,128)(2,1)S(1)} custom-call(s32[5]{0:T(128)S(1)} %stack.52.where_ref, bf16[8,512,256]{2,1,0:T(8,128)(2,1)S(1)} %shard_map.82.normed_ref, bf16[4,192,256]{2,1,0:T(8,128)(2,1)S(1)} %collective-permute-done.11.crossing_ref, bf16[2,192,256]{2,1,0:T(8,128)(2,1)S(1)} %get-tuple-element.28.refs_0_, ...), custom_call_target="tpu_custom_call" | custom-call | flops 11000000512 | bytes 2883584 | tf_op jit(solution)/shard_map/pallas_call | solution.py:308
  47.6 1.6 %collective-permute-start.14 = (bf16[512,256]{1,0:T(8,128)(2,1)S(1)}, bf16[512,256]{1,0:T(8,128)(2,1)S(1)}, u32[]{:S(2)}, u32[]{:S(2)}) collective-permute-start(bf16[512,256]{1,0:T(8,128)(2,1)S(1)} %get-tuple-element.37), channel_id=1, source_target_pairs={{0,2},{1,3},{2,0},{3,1},{4,6},{5,7},{6,4},{7,5},{8,10},{9,11},{10,... | collective-permute-start | bytes 786440 | tf_op jit(solution)/shard_map/ppermute | solution.py:19
  49.3 2.5 %collective-permute-start.15 = (bf16[192,512]{1,0:T(8,128)(2,1)S(1)}, bf16[192,512]{1,0:T(8,128)(2,1)S(1)}, u32[]{:S(2)}, u32[]{:S(2)}) collective-permute-start(bf16[192,512]{1,0:T(8,128)(2,1)S(1)} %shard_map.84.refs_0_), channel_id=1, source_target_pairs={{0,4},{4,0},{8,12},{12,8},{16,20},{20,16},{24,28},{28,24},{1,5},{5... | collective-permute-start | bytes 589832 | tf_op jit(solution)/shard_map/ppermute | solution.py:19
  51.9 0.2 copy.13.ids_ref
  52.2 2.0 %collective-permute-start.19 = (bf16[192,512]{1,0:T(8,128)(2,1)S(1)}, bf16[192,512]{1,0:T(8,128)(2,1)S(1)}, u32[]{:S(2)}, u32[]{:S(2)}) collective-permute-start(bf16[192,512]{1,0:T(8,128)(2,1)S(1)} %shard_map.84.refs_0_), channel_id=1, source_target_pairs={{0,16},{4,20},{8,24},{12,28},{16,0},{20,4},{24,8},{28,12},{1,17},{... | collective-permute-start | bytes 589832 | tf_op jit(solution)/shard_map/ppermute | solution.py:19
  54.2 0.8 collective-permute-start.24
  55.0 4.8 %collective-permute-done.16.refs_0_ = bf16[192,512]{1,0:T(8,128)(2,1)S(1)} collective-permute-done((bf16[192,512]{1,0:T(8,128)(2,1)S(1)}, bf16[192,512]{1,0:T(8,128)(2,1)S(1)}, u32[]{:S(2)}, u32[]{:S(2)}) %collective-permute-start.16) | collective-permute-done | bytes 196640 | tf_op jit(solution)/shard_map/ppermute | solution.py:19
  59.8 0.7 collective-permute-start.17
  60.5 2.2 %shard_map.85.refs_0_ = bf16[1024,128]{1,0:T(8,128)(2,1)S(1)} custom-call(s32[2]{0:T(128)S(1)} %pad_add_fusion.1.where_ref, s32[1168,1]{1,0:T(8,128)S(1)} %copy.13.ids_ref, f32[7,3,512]{2,1,0:T(4,128)S(1)} %copy.14.short_ref, f32[1,512]{1,0:T(1,128)S(1)} %bitcast.13, bf16[32,128]{1,0:T(8,128)(2,1)S(1)} %copy-done.3, bf16[192,512]{1,0:T(8,128)(2,1)S(1)} %shard_map.84.refs_0_, ...), custom_call_target="tpu_custom_call" | custom-call | flops 3849999872 | bytes 2392064 | tf_op jit(solution)/shard_map/pallas_call | solution.py:344
  62.7 1.4 %collective-permute-start.20 = (bf16[192,512]{1,0:T(8,128)(2,1)S(1)}, bf16[192,512]{1,0:T(8,128)(2,1)S(1)}, u32[]{:S(2)}, u32[]{:S(2)}) collective-permute-start(bf16[192,512]{1,0:T(8,128)(2,1)S(1)} %collective-permute-done.19.refs_0_), channel_id=1, source_target_pairs={{0,4},{4,0},{8,12},{12,8},{16,20},{20,16},{24,28},{28,24},{1,5},{5... | collective-permute-start | bytes 589832 | tf_op jit(solution)/shard_map/ppermute | solution.py:19
  64.1 0.6 collective-permute-start.18
  64.7 2.9 %collective-permute-done.17.refs_1_ = bf16[192,512]{1,0:T(8,128)(2,1)S(1)} collective-permute-done((bf16[192,512]{1,0:T(8,128)(2,1)S(1)}, bf16[192,512]{1,0:T(8,128)(2,1)S(1)}, u32[]{:S(2)}, u32[]{:S(2)}) %collective-permute-start.17) | collective-permute-done | bytes 196640 | tf_op jit(solution)/shard_map/ppermute | solution.py:19
  67.6 1.0 %collective-permute-start.25 = (bf16[512,256]{1,0:T(8,128)(2,1)S(1)}, bf16[512,256]{1,0:T(8,128)(2,1)S(1)}, u32[]{:S(2)}, u32[]{:S(2)}) collective-permute-start(bf16[512,256]{1,0:T(8,128)(2,1)S(1)} %collective-permute-done.14.refs_11_), channel_id=1, source_target_pairs={{0,4},{4,0},{8,12},{12,8},{16,20},{20,16},{24,28},{28,24},{1,5},{5... | collective-permute-start | bytes 786440 | tf_op jit(solution)/shard_map/ppermute | solution.py:19
  68.6 2.2 %shard_map.86.refs_1_ = bf16[1024,128]{1,0:T(8,128)(2,1)S(1)} custom-call(s32[2]{0:T(128)S(1)} %pad_add_fusion.2.where_ref, s32[1168,1]{1,0:T(8,128)S(1)} %copy.13.ids_ref, f32[7,3,512]{2,1,0:T(4,128)S(1)} %copy.14.short_ref, f32[1,512]{1,0:T(1,128)S(1)} %bitcast.14, bf16[32,128]{1,0:T(8,128)(2,1)S(1)} %copy-done.3, ...), custom_call_target="tpu_custom_call" | custom-call | flops 3849999872 | bytes 2392064 | tf_op jit(solution)/shard_map/pallas_call | solution.py:344
  70.8 1.0 %collective-permute-done.20.refs_1_ = bf16[192,512]{1,0:T(8,128)(2,1)S(1)} collective-permute-done((bf16[192,512]{1,0:T(8,128)(2,1)S(1)}, bf16[192,512]{1,0:T(8,128)(2,1)S(1)}, u32[]{:S(2)}, u32[]{:S(2)}) %collective-permute-start.20) | collective-permute-done | bytes 196640 | tf_op jit(solution)/shard_map/ppermute | solution.py:19
  71.8 0.6 collective-permute-start.23
  72.5 2.2 %collective-permute-start.22 = (bf16[192,512]{1,0:T(8,128)(2,1)S(1)}, bf16[192,512]{1,0:T(8,128)(2,1)S(1)}, u32[]{:S(2)}, u32[]{:S(2)}) collective-permute-start(bf16[192,512]{1,0:T(8,128)(2,1)S(1)} %collective-permute-done.20.refs_1_), channel_id=1, source_target_pairs={{0,8},{4,12},{8,0},{12,4},{16,24},{20,28},{24,16},{28,20},{1,9},{5... | collective-permute-start | bytes 589832 | tf_op jit(solution)/shard_map/ppermute | solution.py:19
  74.6 2.2 %shard_map.87.refs_2_ = bf16[1024,128]{1,0:T(8,128)(2,1)S(1)} custom-call(s32[2]{0:T(128)S(1)} %pad_add_fusion.3.where_ref, s32[1168,1]{1,0:T(8,128)S(1)} %copy.13.ids_ref, f32[7,3,512]{2,1,0:T(4,128)S(1)} %copy.14.short_ref, f32[1,512]{1,0:T(1,128)S(1)} %bitcast.15, bf16[32,128]{1,0:T(8,128)(2,1)S(1)} %copy-done.3, ...), custom_call_target="tpu_custom_call" | custom-call | flops 3849999872 | bytes 2392064 | tf_op jit(solution)/shard_map/pallas_call | solution.py:344
  76.9 1.4 %collective-permute-done.22.refs_1_ = bf16[192,512]{1,0:T(8,128)(2,1)S(1)} collective-permute-done((bf16[192,512]{1,0:T(8,128)(2,1)S(1)}, bf16[192,512]{1,0:T(8,128)(2,1)S(1)}, u32[]{:S(2)}, u32[]{:S(2)}) %collective-permute-start.22) | collective-permute-done | bytes 196640 | tf_op jit(solution)/shard_map/ppermute | solution.py:19
  78.3 2.2 %shard_map.88.refs_3_ = bf16[1024,128]{1,0:T(8,128)(2,1)S(1)} custom-call(s32[2]{0:T(128)S(1)} %pad_add_fusion.4.where_ref, s32[1168,1]{1,0:T(8,128)S(1)} %copy.13.ids_ref, f32[7,3,512]{2,1,0:T(4,128)S(1)} %copy.14.short_ref, f32[1,512]{1,0:T(1,128)S(1)} %bitcast.16, bf16[32,128]{1,0:T(8,128)(2,1)S(1)} %copy-done.3, ...), custom_call_target="tpu_custom_call" | custom-call | flops 3849999872 | bytes 2392064 | tf_op jit(solution)/shard_map/pallas_call | solution.py:344
  80.5 1.3 %collective-permute-start.27 = (bf16[1024,128]{1,0:T(8,128)(2,1)S(1)}, bf16[1024,128]{1,0:T(8,128)(2,1)S(1)}, u32[]{:S(2)}, u32[]{:S(2)}) collective-permute-start(bf16[1024,128]{1,0:T(8,128)(2,1)S(1)} %shard_map.88.refs_3_), channel_id=1, source_target_pairs={{0,2},{1,3},{2,0},{3,1},{4,6},{5,7},{6,4},{7,5},{8,10},{9,11},{10,... | collective-permute-start | bytes 786440 | tf_op jit(solution)/shard_map/ppermute | solution.py:19
  81.8 4.0 %shard_map.89 = (bf16[2,1024,512]{2,1,0:T(8,128)(2,1)S(1)}, bf16[2,256,512]{2,1,0:T(8,128)(2,1)S(1)}) custom-call(s32[5]{0:T(128)S(1)} %stack.52.where_ref, bf16[1024,128]{1,0:T(8,128)(2,1)S(1)} %shard_map.85.refs_0_, bf16[1024,128]{1,0:T(8,128)(2,1)S(1)} %shard_map.86.refs_1_, bf16[1024,128]{1,0:T(8,128)(2,1)S(1)} %shard_map.87.refs_2_, ...), custom_call_target="tpu_custom_call" | custom-call | flops 4400000000 | bytes 4194304 | tf_op jit(solution)/shard_map/pallas_call | solution.py:375
  85.9 1.9 %collective-permute-done.27.refs_1_ = bf16[1024,128]{1,0:T(8,128)(2,1)S(1)} collective-permute-done((bf16[1024,128]{1,0:T(8,128)(2,1)S(1)}, bf16[1024,128]{1,0:T(8,128)(2,1)S(1)}, u32[]{:S(2)}, u32[]{:S(2)}) %collective-permute-start.27) | collective-permute-done | bytes 262176 | tf_op jit(solution)/shard_map/ppermute | solution.py:19
  87.8 1.1 %shard_map.91 = bf16[1024,512]{1,0:T(8,128)(2,1)S(1)} custom-call(bf16[2,1024,512]{2,1,0:T(8,128)(2,1)S(1)} %get-tuple-element.35.most_ref, bf16[2,256,512]{2,1,0:T(8,128)(2,1)S(1)} %get-tuple-element.36.weight_ref, bf16[1024,128]{1,0:T(8,128)(2,1)S(1)} %collective-permute-done.26.refs_0_, bf16[1024,128]{1,0:T(8,128)(2,1)S(1)} %collective-permute-done.27.refs_1_), custom_call_target="tpu_custom_call" | custom-call | flops 1650000000 | bytes 4194304 | tf_op jit(solution)/shard_map/pallas_call | solution.py:415
  89.0 0.8 shard_map.90.refs_2_
  89.8 1.9 %collective-permute-done.28.refs_3_ = bf16[1024,512]{1,0:T(8,128)(2,1)S(1)} collective-permute-done((bf16[1024,512]{1,0:T(8,128)(2,1)S(1)}, bf16[1024,512]{1,0:T(8,128)(2,1)S(1)}, u32[]{:S(2)}, u32[]{:S(2)}) %collective-permute-start.28) | collective-permute-done | bytes 1048608 | tf_op jit(solution)/shard_map/ppermute | solution.py:19
  91.6 2.4 %shard_map.92 = bf16[1024,512]{1,0:T(8,128)(2,1)} custom-call(bf16[2,1024,512]{2,1,0:T(8,128)(2,1)S(1)} %get-tuple-element.35.most_ref, bf16[2,256,512]{2,1,0:T(8,128)(2,1)S(1)} %get-tuple-element.36.weight_ref, bf16[1024,128]{1,0:T(8,128)(2,1)S(1)} %collective-permute-done.26.refs_0_, bf16[1024,128]{1,0:T(8,128)(2,1)S(1)} %collective-permute-done.27.refs_1_, ...), custom_call_target="tpu_custom_call" | custom-call | flops 1650000000 | bytes 4194304 | tf_op jit(solution)/shard_map/pallas_call | solution.py:416
  (53 shorter events, 1.1 us)
Async XLA Ops:
  0.0 17.7 %collective-permute-start.6 = (bf16[512,512]{1,0:T(8,128)(2,1)}, bf16[512,512]{1,0:T(8,128)(2,1)S(1)}, u32[]{:S(2)}, u32[]{:S(2)}) collective-permute-start(bf16[512,512]{1,0:T(8,128)(2,1)} %table_ref.1), channel_id=1, source_target_pairs={{0,2},{1,3},{2,0},{3,1},{4,6},{5,7},{6,4},{7,5},{8,10},{9,11},{10,... | collective-permute-start | bytes 1572872 | tf_op jit(solution)/shard_map/ppermute | solution.py:19
  3.0 14.7 %collective-permute-start = (bf16[512,256]{1,0:T(8,128)(2,1)}, bf16[512,256]{1,0:T(8,128)(2,1)}, u32[]{:S(2)}, u32[]{:S(2)}) collective-permute-start(bf16[512,256]{1,0:T(8,128)(2,1)} %param.15), channel_id=1, source_target_pairs={{0,16},{4,20},{8,24},{12,28},{16,0},{20,4},{24,8},{28,12},{1,17},{... | collective-permute-start | bytes 786440 | tf_op jit(solution)/shard_map/ppermute | solution.py:19
  5.6 1.1 %copy-start = (bf16[256,3,512]{2,0,1:T(8,128)(2,1)S(1)}, bf16[256,3,512]{2,0,1:T(8,128)(2,1)}, u32[]{:S(2)}) copy-start(bf16[256,3,512]{2,0,1:T(8,128)(2,1)} %param.11) | copy-start | bytes 2359300
  6.8 10.9 %copy-start.1 = (bf16[512,512]{1,0:T(8,128)(2,1)S(1)}, bf16[512,512]{1,0:T(8,128)(2,1)}, u32[]{:S(2)}) copy-start(bf16[512,512]{1,0:T(8,128)(2,1)} %table_ref.1) | copy-start | bytes 1572868
  8.6 20.7 %copy-start.6 = (s32[1024]{0:T(1024)S(1)}, s32[1024]{0:T(1024)}, u32[]{:S(2)}) copy-start(s32[1024]{0:T(1024)} %param.8) | copy-start | bytes 12292
  8.6 24.6 %copy-start.2 = (f32[2048]{0:T(1024)S(1)}, f32[2048]{0:T(1024)}, u32[]{:S(2)}) copy-start(f32[2048]{0:T(1024)} %param.10) | copy-start | bytes 24580
  8.6 9.6 %collective-permute-start.8 = (bf16[2,192,256]{2,1,0:T(8,128)(2,1)}, bf16[2,192,256]{2,1,0:T(8,128)(2,1)S(1)}, u32[]{:S(2)}, u32[]{:S(2)}) collective-permute-start(bf16[2,192,256]{2,1,0:T(8,128)(2,1)} %get-tuple-element.23), channel_id=1, source_target_pairs={{0,4},{4,0},{8,12},{12,8},{16,20},{20,16},{24,28},{28,24},{1,5},{5... | collective-permute-start | bytes 589832 | tf_op jit(solution)/shard_map/ppermute | solution.py:19
  10.2 11.5 %collective-permute-start.9 = (bf16[2,192,256]{2,1,0:T(8,128)(2,1)}, bf16[2,192,256]{2,1,0:T(8,128)(2,1)S(1)}, u32[]{:S(2)}, u32[]{:S(2)}) collective-permute-start(bf16[2,192,256]{2,1,0:T(8,128)(2,1)} %get-tuple-element.24), channel_id=1, source_target_pairs={{0,8},{4,12},{8,0},{12,4},{16,24},{20,28},{24,16},{28,20},{1,9},{5... | collective-permute-start | bytes 589832 | tf_op jit(solution)/shard_map/ppermute | solution.py:19
  11.8 14.4 %collective-permute-start.10 = (bf16[2,192,256]{2,1,0:T(8,128)(2,1)S(1)}, bf16[2,192,256]{2,1,0:T(8,128)(2,1)S(1)}, u32[]{:S(2)}, u32[]{:S(2)}) collective-permute-start(bf16[2,192,256]{2,1,0:T(8,128)(2,1)S(1)} %get-tuple-element.25), channel_id=1, source_target_pairs={{0,12},{4,8},{8,4},{12,0},{16,28},{20,24},{24,20},{28,16},{1,13},{... | collective-permute-start | bytes 589832 | tf_op jit(solution)/shard_map/ppermute | solution.py:19
  17.7 11.5 %collective-permute-start.5 = (bf16[512,512]{1,0:T(8,128)(2,1)S(1)}, bf16[512,512]{1,0:T(8,128)(2,1)S(1)}, u32[]{:S(2)}, u32[]{:S(2)}) collective-permute-start(bf16[512,512]{1,0:T(8,128)(2,1)S(1)} %copy-done.1), channel_id=1, source_target_pairs={{0,1},{1,0},{2,3},{3,2},{4,5},{5,4},{6,7},{7,6},{8,9},{9,8},{10,11... | collective-permute-start | bytes 1572872 | tf_op jit(solution)/shard_map/ppermute | solution.py:19
  17.7 11.6 %collective-permute-start.7 = (bf16[512,512]{1,0:T(8,128)(2,1)S(1)}, bf16[512,512]{1,0:T(8,128)(2,1)S(1)}, u32[]{:S(2)}, u32[]{:S(2)}) collective-permute-start(bf16[512,512]{1,0:T(8,128)(2,1)S(1)} %collective-permute-done.6.refs_2_), channel_id=1, source_target_pairs={{0,1},{1,0},{2,3},{3,2},{4,5},{5,4},{6,7},{7,6},{8,9},{9,8},{10,11... | collective-permute-start | bytes 1572872 | tf_op jit(solution)/shard_map/ppermute | solution.py:19
  18.3 29.1 %collective-permute-start.4 = (bf16[512,256]{1,0:T(8,128)(2,1)}, bf16[512,256]{1,0:T(8,128)(2,1)S(1)}, u32[]{:S(2)}, u32[]{:S(2)}) collective-permute-start(bf16[512,256]{1,0:T(8,128)(2,1)} %param.15), channel_id=1, source_target_pairs={{0,8},{4,12},{8,0},{12,4},{16,24},{20,28},{24,16},{28,20},{1,9},{5... | collective-permute-start | bytes 786440 | tf_op jit(solution)/shard_map/ppermute | solution.py:19
  27.3 7.9 %collective-permute-start.1 = (bf16[512,256]{1,0:T(8,128)(2,1)S(1)}, bf16[512,256]{1,0:T(8,128)(2,1)S(1)}, u32[]{:S(2)}, u32[]{:S(2)}) collective-permute-start(bf16[512,256]{1,0:T(8,128)(2,1)S(1)} %get-tuple-element.39), channel_id=1, source_target_pairs={{0,2},{1,3},{2,0},{3,1},{4,6},{5,7},{6,4},{7,5},{8,10},{9,11},{10,... | collective-permute-start | bytes 786440 | tf_op jit(solution)/shard_map/ppermute | solution.py:19
  27.9 24.3 %collective-permute-start.2 = (bf16[512,256]{1,0:T(8,128)(2,1)S(1)}, bf16[512,256]{1,0:T(8,128)(2,1)}, u32[]{:S(2)}, u32[]{:S(2)}) collective-permute-start(bf16[512,256]{1,0:T(8,128)(2,1)S(1)} %get-tuple-element.40.refs_6_), channel_id=1, source_target_pairs={{0,4},{4,0},{8,12},{12,8},{16,20},{20,16},{24,28},{28,24},{1,5},{5... | collective-permute-start | bytes 786440 | tf_op jit(solution)/shard_map/ppermute | solution.py:19
  29.2 16.7 %collective-permute-start.11 = (bf16[4,192,256]{2,1,0:T(8,128)(2,1)S(1)}, bf16[4,192,256]{2,1,0:T(8,128)(2,1)S(1)}, u32[]{:S(2)}, u32[]{:S(2)}) collective-permute-start(bf16[4,192,256]{2,1,0:T(8,128)(2,1)S(1)} %pad_maximum_fusion), channel_id=1, source_target_pairs={{0,16},{4,20},{8,24},{12,28},{16,0},{20,4},{24,8},{28,12},{1,17},{... | collective-permute-start | bytes 1179656 | tf_op jit(solution)/shard_map/ppermute | solution.py:19
  29.4 7.9 %collective-permute-start.12 = (s32[144]{0:T(256)S(1)}, s32[144]{0:T(256)S(1)}, u32[]{:S(2)}, u32[]{:S(2)}) collective-permute-start(s32[144]{0:T(256)S(1)} %slice.19), channel_id=1, source_target_pairs={{0,4},{4,8},{8,12},{12,16},{16,20},{20,24},{24,28},{1,5},{5,9},{9,... | collective-permute-start | bytes 1736 | tf_op jit(solution)/shard_map/ppermute | solution.py:290
  35.2 12.3 %collective-permute-start.13 = (bf16[512,256]{1,0:T(8,128)(2,1)}, bf16[512,256]{1,0:T(8,128)(2,1)S(1)}, u32[]{:S(2)}, u32[]{:S(2)}) collective-permute-start(bf16[512,256]{1,0:T(8,128)(2,1)} %collective-permute-done), channel_id=1, source_target_pairs={{0,8},{4,12},{8,0},{12,4},{16,24},{20,28},{24,16},{28,20},{1,9},{5... | collective-permute-start | bytes 786440 | tf_op jit(solution)/shard_map/ppermute | solution.py:19
  37.3 16.9 %collective-permute-start.3 = (bf16[512,256]{1,0:T(8,128)(2,1)S(1)}, bf16[512,256]{1,0:T(8,128)(2,1)S(1)}, u32[]{:S(2)}, u32[]{:S(2)}) collective-permute-start(bf16[512,256]{1,0:T(8,128)(2,1)S(1)} %collective-permute-done.1.refs_7_), channel_id=1, source_target_pairs={{0,4},{4,0},{8,12},{12,8},{16,20},{20,16},{24,28},{28,24},{1,5},{5... | collective-permute-start | bytes 786440 | tf_op jit(solution)/shard_map/ppermute | solution.py:19
  38.8 10.4 %copy-start.5 = (f32[7,3,512]{2,0,1:T(8,128)S(1)}, f32[7,3,512]{2,0,1:T(8,128)}, u32[]{:S(2)}) copy-start(f32[7,3,512]{2,0,1:T(8,128)} %param.12) | copy-start | bytes 129028
  38.8 21.6 %copy-start.3 = (bf16[32,128]{1,0:T(8,128)(2,1)S(1)}, bf16[32,128]{1,0:T(8,128)(2,1)}, u32[]{:S(2)}) copy-start(bf16[32,128]{1,0:T(8,128)(2,1)} %filter_ref.7) | copy-start | bytes 24580
  38.8 21.6 %copy-start.4 = (f32[512]{0:T(512)S(1)}, f32[512]{0:T(512)}, u32[]{:S(2)}) copy-start(f32[512]{0:T(512)} %param.14) | copy-start | bytes 6148
  47.6 12.9 %collective-permute-start.14 = (bf16[512,256]{1,0:T(8,128)(2,1)S(1)}, bf16[512,256]{1,0:T(8,128)(2,1)S(1)}, u32[]{:S(2)}, u32[]{:S(2)}) collective-permute-start(bf16[512,256]{1,0:T(8,128)(2,1)S(1)} %get-tuple-element.37), channel_id=1, source_target_pairs={{0,2},{1,3},{2,0},{3,1},{4,6},{5,7},{6,4},{7,5},{8,10},{9,11},{10,... | collective-permute-start | bytes 786440 | tf_op jit(solution)/shard_map/ppermute | solution.py:19
  49.3 11.1 %collective-permute-start.15 = (bf16[192,512]{1,0:T(8,128)(2,1)S(1)}, bf16[192,512]{1,0:T(8,128)(2,1)S(1)}, u32[]{:S(2)}, u32[]{:S(2)}) collective-permute-start(bf16[192,512]{1,0:T(8,128)(2,1)S(1)} %shard_map.84.refs_0_), channel_id=1, source_target_pairs={{0,4},{4,0},{8,12},{12,8},{16,20},{20,16},{24,28},{28,24},{1,5},{5... | collective-permute-start | bytes 589832 | tf_op jit(solution)/shard_map/ppermute | solution.py:19
  51.8 8.0 %collective-permute-start.16 = (bf16[192,512]{1,0:T(8,128)(2,1)S(1)}, bf16[192,512]{1,0:T(8,128)(2,1)S(1)}, u32[]{:S(2)}, u32[]{:S(2)}) collective-permute-start(bf16[192,512]{1,0:T(8,128)(2,1)S(1)} %shard_map.84.refs_0_), channel_id=1, source_target_pairs={{0,8},{4,12},{8,0},{12,4},{16,24},{20,28},{24,16},{28,20},{1,9},{5... | collective-permute-start | bytes 589832 | tf_op jit(solution)/shard_map/ppermute | solution.py:19
  52.2 10.5 %collective-permute-start.19 = (bf16[192,512]{1,0:T(8,128)(2,1)S(1)}, bf16[192,512]{1,0:T(8,128)(2,1)S(1)}, u32[]{:S(2)}, u32[]{:S(2)}) collective-permute-start(bf16[192,512]{1,0:T(8,128)(2,1)S(1)} %shard_map.84.refs_0_), channel_id=1, source_target_pairs={{0,16},{4,20},{8,24},{12,28},{16,0},{20,4},{24,8},{28,12},{1,17},{... | collective-permute-start | bytes 589832 | tf_op jit(solution)/shard_map/ppermute | solution.py:19
  54.2 27.6 %collective-permute-start.24 = (bf16[512,256]{1,0:T(8,128)(2,1)S(1)}, bf16[512,256]{1,0:T(8,128)(2,1)S(1)}, u32[]{:S(2)}, u32[]{:S(2)}) collective-permute-start(bf16[512,256]{1,0:T(8,128)(2,1)S(1)} %get-tuple-element.38.refs_10_), channel_id=1, source_target_pairs={{0,4},{4,0},{8,12},{12,8},{16,20},{20,16},{24,28},{28,24},{1,5},{5... | collective-permute-start | bytes 786440 | tf_op jit(solution)/shard_map/ppermute | solution.py:19
  59.8 7.8 %collective-permute-start.17 = (bf16[192,512]{1,0:T(8,128)(2,1)S(1)}, bf16[192,512]{1,0:T(8,128)(2,1)S(1)}, u32[]{:S(2)}, u32[]{:S(2)}) collective-permute-start(bf16[192,512]{1,0:T(8,128)(2,1)S(1)} %collective-permute-done.16.refs_0_), channel_id=1, source_target_pairs={{0,4},{4,0},{8,12},{12,8},{16,20},{20,16},{24,28},{28,24},{1,5},{5... | collective-permute-start | bytes 589832 | tf_op jit(solution)/shard_map/ppermute | solution.py:19
  62.7 9.2 %collective-permute-start.20 = (bf16[192,512]{1,0:T(8,128)(2,1)S(1)}, bf16[192,512]{1,0:T(8,128)(2,1)S(1)}, u32[]{:S(2)}, u32[]{:S(2)}) collective-permute-start(bf16[192,512]{1,0:T(8,128)(2,1)S(1)} %collective-permute-done.19.refs_0_), channel_id=1, source_target_pairs={{0,4},{4,0},{8,12},{12,8},{16,20},{20,16},{24,28},{28,24},{1,5},{5... | collective-permute-start | bytes 589832 | tf_op jit(solution)/shard_map/ppermute | solution.py:19
  64.1 12.7 %collective-permute-start.21 = (bf16[192,512]{1,0:T(8,128)(2,1)S(1)}, bf16[192,512]{1,0:T(8,128)(2,1)S(1)}, u32[]{:S(2)}, u32[]{:S(2)}) collective-permute-start(bf16[192,512]{1,0:T(8,128)(2,1)S(1)} %collective-permute-done.19.refs_0_), channel_id=1, source_target_pairs={{0,8},{4,12},{8,0},{12,4},{16,24},{20,28},{24,16},{28,20},{1,9},{5... | collective-permute-start | bytes 589832 | tf_op jit(solution)/shard_map/ppermute | solution.py:19
  64.1 8.3 %collective-permute-start.18 = (bf16[1024,128]{1,0:T(8,128)(2,1)S(1)}, bf16[1024,128]{1,0:T(8,128)(2,1)S(1)}, u32[]{:S(2)}, u32[]{:S(2)}) collective-permute-start(bf16[1024,128]{1,0:T(8,128)(2,1)S(1)} %shard_map.85.refs_0_), channel_id=1, source_target_pairs={{0,2},{1,3},{2,0},{3,1},{4,6},{5,7},{6,4},{7,5},{8,10},{9,11},{10,... | collective-permute-start | bytes 786440 | tf_op jit(solution)/shard_map/ppermute | solution.py:19
  67.6 14.2 %collective-permute-start.25 = (bf16[512,256]{1,0:T(8,128)(2,1)S(1)}, bf16[512,256]{1,0:T(8,128)(2,1)S(1)}, u32[]{:S(2)}, u32[]{:S(2)}) collective-permute-start(bf16[512,256]{1,0:T(8,128)(2,1)S(1)} %collective-permute-done.14.refs_11_), channel_id=1, source_target_pairs={{0,4},{4,0},{8,12},{12,8},{16,20},{20,16},{24,28},{28,24},{1,5},{5... | collective-permute-start | bytes 786440 | tf_op jit(solution)/shard_map/ppermute | solution.py:19
  71.8 10.0 %collective-permute-start.23 = (bf16[1024,128]{1,0:T(8,128)(2,1)S(1)}, bf16[1024,128]{1,0:T(8,128)(2,1)S(1)}, u32[]{:S(2)}, u32[]{:S(2)}) collective-permute-start(bf16[1024,128]{1,0:T(8,128)(2,1)S(1)} %shard_map.86.refs_1_), channel_id=1, source_target_pairs={{0,2},{1,3},{2,0},{3,1},{4,6},{5,7},{6,4},{7,5},{8,10},{9,11},{10,... | collective-permute-start | bytes 786440 | tf_op jit(solution)/shard_map/ppermute | solution.py:19
  72.5 5.8 %collective-permute-start.22 = (bf16[192,512]{1,0:T(8,128)(2,1)S(1)}, bf16[192,512]{1,0:T(8,128)(2,1)S(1)}, u32[]{:S(2)}, u32[]{:S(2)}) collective-permute-start(bf16[192,512]{1,0:T(8,128)(2,1)S(1)} %collective-permute-done.20.refs_1_), channel_id=1, source_target_pairs={{0,8},{4,12},{8,0},{12,4},{16,24},{20,28},{24,16},{28,20},{1,9},{5... | collective-permute-start | bytes 589832 | tf_op jit(solution)/shard_map/ppermute | solution.py:19
  76.8 9.0 %collective-permute-start.26 = (bf16[1024,128]{1,0:T(8,128)(2,1)S(1)}, bf16[1024,128]{1,0:T(8,128)(2,1)S(1)}, u32[]{:S(2)}, u32[]{:S(2)}) collective-permute-start(bf16[1024,128]{1,0:T(8,128)(2,1)S(1)} %shard_map.87.refs_2_), channel_id=1, source_target_pairs={{0,2},{1,3},{2,0},{3,1},{4,6},{5,7},{6,4},{7,5},{8,10},{9,11},{10,... | collective-permute-start | bytes 786440 | tf_op jit(solution)/shard_map/ppermute | solution.py:19
  80.5 7.3 %collective-permute-start.27 = (bf16[1024,128]{1,0:T(8,128)(2,1)S(1)}, bf16[1024,128]{1,0:T(8,128)(2,1)S(1)}, u32[]{:S(2)}, u32[]{:S(2)}) collective-permute-start(bf16[1024,128]{1,0:T(8,128)(2,1)S(1)} %shard_map.88.refs_3_), channel_id=1, source_target_pairs={{0,2},{1,3},{2,0},{3,1},{4,6},{5,7},{6,4},{7,5},{8,10},{9,11},{10,... | collective-permute-start | bytes 786440 | tf_op jit(solution)/shard_map/ppermute | solution.py:19
  88.9 2.7 %collective-permute-start.28 = (bf16[1024,512]{1,0:T(8,128)(2,1)S(1)}, bf16[1024,512]{1,0:T(8,128)(2,1)S(1)}, u32[]{:S(2)}, u32[]{:S(2)}) collective-permute-start(bf16[1024,512]{1,0:T(8,128)(2,1)S(1)} %shard_map.91), channel_id=1, source_target_pairs={{0,1},{1,0},{2,3},{3,2},{4,5},{5,4},{6,7},{7,6},{8,9},{9,8},{10,11... | collective-permute-start | bytes 3145736 | tf_op jit(solution)/shard_map/ppermute | solution.py:19

commit v5 on v4

--- a/solution.py
+++ b/solution.py
@@ -333,12 +333,15 @@
     for index in range(chunks):
         if index == 1:
             starts[2] = after(starts[2], gates[0])
+            starts[1] = after(starts[1], gates[0])
             starts.append(over(starts[2], 2))
         pieces = [starts[index], over(starts[index], 1) if index < 3 else over(besides[2], 2)]
         besides.append(pieces[1])
         at = jnp.stack([seq, chunk_at ^ index]).astype(jnp.int32)
         if index == 2:
             at = after(at, row_gates[0])
+        if index == 1:
+            at = after(at, *halves[:7])
         if index == 0:
             at = after(at, *halves[:6])
         gate = pl.pallas_call(
@@ -392,7 +395,7 @@
         ],
     )(where, *gates, *row_gates[:-late], *halves)
 
-    rows = tokens // 4
+    rows = tokens // 2
 
     def stepped(kernel, half, more):
         return pl.pallas_call(

time: 94.3 us -> 93 us (0.986)
  Pallas kernels: 22.4 us -> 21.4 us
  transfers between devices with their start and end apart: 29 -> 29, of which waited for: 11 -> 13; matrix products, arithmetic and copies ran while one was open for 2% -> 2% of each run, Pallas kernels for 20% -> 20%
where the time goes in v5:
time: 93 us; the launch traced here: 92.8 us
  waiting for transfers between devices  34 us (37%)
  starting transfers between devices  33.9 us (36%)
  Pallas kernels  21.4 us (23%)
  local copies, waits for them, and re-layouts  1.63 us (2%)
  other arithmetic  1.54 us (2%)
    ppermute x28, waiting for transfers between devices, swap(): return lax.ppermute(block, axis, [(i, i ^ offset) for i in range(count)])  34 us
    ppermute x28, starting transfers between devices, swap(): return lax.ppermute(block, axis, [(i, i ^ offset) for i in range(count)])  30.2 us
    pallas_call x4, Pallas kernels, body(): pl.pallas_call(functools.partial(mixer_kernel, width // groups), grid_spe...  8.72 us
    pallas_call x1, Pallas kernels, body(): call(functools.partial(most_kernel, chunks, late), [jax.ShapeDtypeStruct(...  3.97 us
    ppermute x1, starting transfers between devices, body(): lax.ppermute(after(token_ids, table_both)[tokens - halo:], 'seq', [(i, i...  3.8 us
    pallas_call x1, Pallas kernels, body(): call(norm_kernel, jax.ShapeDtypeStruct((n, vocab, depth), BF), 6, cost_us...  1.96 us
  transfers between devices with their start and end apart: 29, of which 13 were waited for; matrix products, arithmetic and copies ran while one was open for 2% of the time, Pallas kernels for 20%

profile of v5, /device:TPU:0, one launch (start us, length us, event | category | flops | bytes accessed | tf_op | source)
XLA Modules:
  0.0 92.8 jit_solution(4270333346887638170)
XLA Ops:
  0.0 3.0 %collective-permute-start.6 = (bf16[512,512]{1,0:T(8,128)(2,1)}, bf16[512,512]{1,0:T(8,128)(2,1)S(1)}, u32[]{:S(2)}, u32[]{:S(2)}) collective-permute-start(bf16[512,512]{1,0:T(8,128)(2,1)} %table_ref.1), channel_id=1, source_target_pairs={{0,2},{1,3},{2,0},{3,1},{4,6},{5,7},{6,4},{7,5},{8,10},{9,11},{10,... | collective-permute-start | bytes 1572872 | tf_op jit(solution)/shard_map/ppermute | solution.py:19
  3.0 2.6 %collective-permute-start = (bf16[512,256]{1,0:T(8,128)(2,1)}, bf16[512,256]{1,0:T(8,128)(2,1)}, u32[]{:S(2)}, u32[]{:S(2)}) collective-permute-start(bf16[512,256]{1,0:T(8,128)(2,1)} %param.15), channel_id=1, source_target_pairs={{0,16},{4,20},{8,24},{12,28},{16,0},{20,4},{24,8},{28,12},{1,17},{... | collective-permute-start | bytes 786440 | tf_op jit(solution)/shard_map/ppermute | solution.py:19
  5.6 1.1 %copy-done = bf16[256,3,512]{2,0,1:T(8,128)(2,1)S(1)} copy-done((bf16[256,3,512]{2,0,1:T(8,128)(2,1)S(1)}, bf16[256,3,512]{2,0,1:T(8,128)(2,1)}, u32[]{:S(2)}) %copy-start) | copy-done | bytes 786456
  6.8 1.8 %shard_map.83 = (bf16[2,192,256]{2,1,0:T(8,128)(2,1)S(1)}, bf16[2,192,256]{2,1,0:T(8,128)(2,1)}, bf16[2,192,256]{2,1,0:T(8,128)(2,1)}, bf16[2,192,256]{2,1,0:T(8,128)(2,1)S(1)}) custom-call(s32[5]{0:T(128)S(1)} %stack.52.where_ref, bf16[3,256,512]{2,1,0:T(8,128)(2,1)S(1)} %bitcast.11), custom_call_target="tpu_custom_call" | custom-call | flops 1100000000 | bytes 1572864 | tf_op jit(solution)/shard_map/pallas_call | solution.py:268
  8.6 1.6 %collective-permute-start.8 = (bf16[2,192,256]{2,1,0:T(8,128)(2,1)}, bf16[2,192,256]{2,1,0:T(8,128)(2,1)S(1)}, u32[]{:S(2)}, u32[]{:S(2)}) collective-permute-start(bf16[2,192,256]{2,1,0:T(8,128)(2,1)} %get-tuple-element.25), channel_id=1, source_target_pairs={{0,4},{4,0},{8,12},{12,8},{16,20},{20,16},{24,28},{28,24},{1,5},{5... | collective-permute-start | bytes 589832 | tf_op jit(solution)/shard_map/ppermute | solution.py:19
  10.2 1.6 %collective-permute-start.9 = (bf16[2,192,256]{2,1,0:T(8,128)(2,1)}, bf16[2,192,256]{2,1,0:T(8,128)(2,1)S(1)}, u32[]{:S(2)}, u32[]{:S(2)}) collective-permute-start(bf16[2,192,256]{2,1,0:T(8,128)(2,1)} %get-tuple-element.26), channel_id=1, source_target_pairs={{0,8},{4,12},{8,0},{12,4},{16,24},{20,28},{24,16},{28,20},{1,9},{5... | collective-permute-start | bytes 589832 | tf_op jit(solution)/shard_map/ppermute | solution.py:19
  11.8 0.4 collective-permute-start.10
  12.2 5.5 %collective-permute-done = bf16[512,256]{1,0:T(8,128)(2,1)} collective-permute-done((bf16[512,256]{1,0:T(8,128)(2,1)}, bf16[512,256]{1,0:T(8,128)(2,1)}, u32[]{:S(2)}, u32[]{:S(2)}) %collective-permute-start) | collective-permute-done | bytes 262176 | tf_op jit(solution)/shard_map/ppermute | solution.py:19
  17.7 0.5 collective-permute-start.7
  18.2 0.7 collective-permute-start.4
  18.9 2.9 %collective-permute-done.9.refs_2_ = bf16[2,192,256]{2,1,0:T(8,128)(2,1)S(1)} collective-permute-done((bf16[2,192,256]{2,1,0:T(8,128)(2,1)}, bf16[2,192,256]{2,1,0:T(8,128)(2,1)S(1)}, u32[]{:S(2)}, u32[]{:S(2)}) %collective-permute-start.9) | collective-permute-done | bytes 196640 | tf_op jit(solution)/shard_map/ppermute | solution.py:19
  21.8 4.5 %collective-permute-done.10.refs_3_ = bf16[2,192,256]{2,1,0:T(8,128)(2,1)S(1)} collective-permute-done((bf16[2,192,256]{2,1,0:T(8,128)(2,1)S(1)}, bf16[2,192,256]{2,1,0:T(8,128)(2,1)S(1)}, u32[]{:S(2)}, u32[]{:S(2)}) %collective-permute-start.10) | collective-permute-done | bytes 196640 | tf_op jit(solution)/shard_map/ppermute | solution.py:19
  26.2 1.1 %broadcast_select_fusion.2 = (bf16[512,256]{1,0:T(8,128)(2,1)S(1)}, bf16[512,256]{1,0:T(8,128)(2,1)S(1)}) fusion(bf16[512,256]{1,0:T(8,128)(2,1)} %collective-permute-done, bf16[512,256]{1,0:T(8,128)(2,1)} %param.15, pred[]{:T(512)S(6)} %eq.6), kind=kLoop, calls=%fused_computation.3 | loop fusion | flops 262144 | bytes 1048577 | tf_op jit(solution)/shard_map/jit(_where)/select_n | solution.py:326
  27.3 0.6 collective-permute-start.1
  27.9 1.2 %collective-permute-start.2 = (bf16[512,256]{1,0:T(8,128)(2,1)S(1)}, bf16[512,256]{1,0:T(8,128)(2,1)}, u32[]{:S(2)}, u32[]{:S(2)}) collective-permute-start(bf16[512,256]{1,0:T(8,128)(2,1)S(1)} %get-tuple-element.44.refs_6_), channel_id=1, source_target_pairs={{0,4},{4,0},{8,12},{12,8},{16,20},{20,16},{24,28},{28,24},{1,5},{5... | collective-permute-start | bytes 786440 | tf_op jit(solution)/shard_map/ppermute | solution.py:19
  29.4 3.8 %collective-permute-start.12 = (s32[144]{0:T(256)S(1)}, s32[144]{0:T(256)S(1)}, u32[]{:S(2)}, u32[]{:S(2)}) collective-permute-start(s32[144]{0:T(256)S(1)} %slice.19), channel_id=1, source_target_pairs={{0,4},{4,8},{8,12},{12,16},{16,20},{20,24},{24,28},{1,5},{5,9},{9,... | collective-permute-start | bytes 1736 | tf_op jit(solution)/shard_map/ppermute | solution.py:290
  33.2 2.0 %shard_map.82.normed_ref = bf16[8,512,256]{2,1,0:T(8,128)(2,1)S(1)} custom-call(s32[5]{0:T(128)S(1)} %stack.52.where_ref, f32[4,1,512]{2,1,0:T(1,128)S(1)} %bitcast.12, bf16[512,512]{1,0:T(8,128)(2,1)S(1)} %copy-done.1, bf16[512,512]{1,0:T(8,128)(2,1)S(1)} %collective-permute-done.5.refs_1_, bf16[512,512]{1,0:T(8,128)(2,1)S(1)} %collective-permute-done.6.refs_2_, ...), custom_call_target="tpu_custom_call" | custom-call | flops 1650000000 | bytes 4194304 | tf_op jit(solution)/shard_map/pallas_call | solution.py:296
  35.2 2.1 %collective-permute-start.13 = (bf16[512,256]{1,0:T(8,128)(2,1)}, bf16[512,256]{1,0:T(8,128)(2,1)S(1)}, u32[]{:S(2)}, u32[]{:S(2)}) collective-permute-start(bf16[512,256]{1,0:T(8,128)(2,1)} %collective-permute-done), channel_id=1, source_target_pairs={{0,8},{4,12},{8,0},{12,4},{16,24},{20,28},{24,16},{28,20},{1,9},{5... | collective-permute-start | bytes 786440 | tf_op jit(solution)/shard_map/ppermute | solution.py:19
  37.3 1.4 %collective-permute-start.3 = (bf16[512,256]{1,0:T(8,128)(2,1)S(1)}, bf16[512,256]{1,0:T(8,128)(2,1)S(1)}, u32[]{:S(2)}, u32[]{:S(2)}) collective-permute-start(bf16[512,256]{1,0:T(8,128)(2,1)S(1)} %collective-permute-done.1.refs_7_), channel_id=1, source_target_pairs={{0,4},{4,0},{8,12},{12,8},{16,20},{20,16},{24,28},{28,24},{1,5},{5... | collective-permute-start | bytes 786440 | tf_op jit(solution)/shard_map/ppermute | solution.py:19
  38.8 7.0 %collective-permute-done.11.crossing_ref = bf16[4,192,256]{2,1,0:T(8,128)(2,1)S(1)} collective-permute-done((bf16[4,192,256]{2,1,0:T(8,128)(2,1)S(1)}, bf16[4,192,256]{2,1,0:T(8,128)(2,1)S(1)}, u32[]{:S(2)}, u32[]{:S(2)}) %collective-permute-start.11) | collective-permute-done | bytes 393248 | tf_op jit(solution)/shard_map/ppermute | solution.py:19
  45.9 1.5 %shard_map.84.refs_0_ = bf16[192,512]{1,0:T(8,128)(2,1)S(1)} custom-call(s32[5]{0:T(128)S(1)} %stack.52.where_ref, bf16[8,512,256]{2,1,0:T(8,128)(2,1)S(1)} %shard_map.82.normed_ref, bf16[4,192,256]{2,1,0:T(8,128)(2,1)S(1)} %collective-permute-done.11.crossing_ref, bf16[2,192,256]{2,1,0:T(8,128)(2,1)S(1)} %get-tuple-element.30.refs_0_, ...), custom_call_target="tpu_custom_call" | custom-call | flops 11000000512 | bytes 2883584 | tf_op jit(solution)/shard_map/pallas_call | solution.py:308
  47.6 1.6 %collective-permute-start.14 = (bf16[512,256]{1,0:T(8,128)(2,1)S(1)}, bf16[512,256]{1,0:T(8,128)(2,1)S(1)}, u32[]{:S(2)}, u32[]{:S(2)}) collective-permute-start(bf16[512,256]{1,0:T(8,128)(2,1)S(1)} %get-tuple-element.41), channel_id=1, source_target_pairs={{0,2},{1,3},{2,0},{3,1},{4,6},{5,7},{6,4},{7,5},{8,10},{9,11},{10,... | collective-permute-start | bytes 786440 | tf_op jit(solution)/shard_map/ppermute | solution.py:19
  49.2 2.4 %collective-permute-start.15 = (bf16[192,512]{1,0:T(8,128)(2,1)S(1)}, bf16[192,512]{1,0:T(8,128)(2,1)S(1)}, u32[]{:S(2)}, u32[]{:S(2)}) collective-permute-start(bf16[192,512]{1,0:T(8,128)(2,1)S(1)} %shard_map.84.refs_0_), channel_id=1, source_target_pairs={{0,4},{4,0},{8,12},{12,8},{16,20},{20,16},{24,28},{28,24},{1,5},{5... | collective-permute-start | bytes 589832 | tf_op jit(solution)/shard_map/ppermute | solution.py:19
  52.1 1.0 %collective-permute-start.20 = (bf16[192,512]{1,0:T(8,128)(2,1)S(1)}, bf16[192,512]{1,0:T(8,128)(2,1)S(1)}, u32[]{:S(2)}, u32[]{:S(2)}) collective-permute-start(bf16[192,512]{1,0:T(8,128)(2,1)S(1)} %shard_map.84.refs_0_), channel_id=1, source_target_pairs={{0,16},{4,20},{8,24},{12,28},{16,0},{20,4},{24,8},{28,12},{1,17},{... | collective-permute-start | bytes 589832 | tf_op jit(solution)/shard_map/ppermute | solution.py:19
  53.1 1.0 %collective-permute-start.17 = (bf16[192,512]{1,0:T(8,128)(2,1)S(1)}, bf16[192,512]{1,0:T(8,128)(2,1)S(1)}, u32[]{:S(2)}, u32[]{:S(2)}) collective-permute-start(bf16[192,512]{1,0:T(8,128)(2,1)S(1)} %shard_map.84.refs_0_), channel_id=1, source_target_pairs={{0,8},{4,12},{8,0},{12,4},{16,24},{20,28},{24,16},{28,20},{1,9},{5... | collective-permute-start | bytes 589832 | tf_op jit(solution)/shard_map/ppermute | solution.py:19
  54.1 0.8 collective-permute-start.16
  55.2 1.0 %collective-permute-done.15.refs_1_ = bf16[192,512]{1,0:T(8,128)(2,1)S(1)} collective-permute-done((bf16[192,512]{1,0:T(8,128)(2,1)S(1)}, bf16[192,512]{1,0:T(8,128)(2,1)S(1)}, u32[]{:S(2)}, u32[]{:S(2)}) %collective-permute-start.15) | collective-permute-done | bytes 196640 | tf_op jit(solution)/shard_map/ppermute | solution.py:19
  56.3 2.2 %shard_map.85.refs_0_ = bf16[1024,128]{1,0:T(8,128)(2,1)S(1)} custom-call(s32[2]{0:T(128)S(1)} %pad_add_fusion.1.where_ref, s32[1168,1]{1,0:T(8,128)S(1)} %copy.13.ids_ref, f32[7,3,512]{2,1,0:T(4,128)S(1)} %copy.14.short_ref, f32[1,512]{1,0:T(1,128)S(1)} %bitcast.13, bf16[32,128]{1,0:T(8,128)(2,1)S(1)} %copy-done.3, bf16[192,512]{1,0:T(8,128)(2,1)S(1)} %shard_map.84.refs_0_, ...), custom_call_target="tpu_custom_call" | custom-call | flops 3849999872 | bytes 2392064 | tf_op jit(solution)/shard_map/pallas_call | solution.py:347
  58.5 3.4 %collective-permute-done.17.refs_0_ = bf16[192,512]{1,0:T(8,128)(2,1)S(1)} collective-permute-done((bf16[192,512]{1,0:T(8,128)(2,1)S(1)}, bf16[192,512]{1,0:T(8,128)(2,1)S(1)}, u32[]{:S(2)}, u32[]{:S(2)}) %collective-permute-start.17) | collective-permute-done | bytes 196640 | tf_op jit(solution)/shard_map/ppermute | solution.py:19
  61.9 0.7 collective-permute-start.18
  62.8 1.3 %collective-permute-start.21 = (bf16[192,512]{1,0:T(8,128)(2,1)S(1)}, bf16[192,512]{1,0:T(8,128)(2,1)S(1)}, u32[]{:S(2)}, u32[]{:S(2)}) collective-permute-start(bf16[192,512]{1,0:T(8,128)(2,1)S(1)} %collective-permute-done.20.refs_0_), channel_id=1, source_target_pairs={{0,4},{4,0},{8,12},{12,8},{16,20},{20,16},{24,28},{28,24},{1,5},{5... | collective-permute-start | bytes 589832 | tf_op jit(solution)/shard_map/ppermute | solution.py:19
  64.1 0.4 collective-permute-start.22
  64.4 0.4 collective-permute-start.19
  64.8 0.5 collective-permute-start.25
  65.4 4.3 %collective-permute-done.18.refs_1_ = bf16[192,512]{1,0:T(8,128)(2,1)S(1)} collective-permute-done((bf16[192,512]{1,0:T(8,128)(2,1)S(1)}, bf16[192,512]{1,0:T(8,128)(2,1)S(1)}, u32[]{:S(2)}, u32[]{:S(2)}) %collective-permute-start.18) | collective-permute-done | bytes 196640 | tf_op jit(solution)/shard_map/ppermute | solution.py:19
  69.7 2.2 %shard_map.86.refs_1_ = bf16[1024,128]{1,0:T(8,128)(2,1)S(1)} custom-call(s32[2]{0:T(128)S(1)} %pad_add_fusion.2.where_ref, s32[1168,1]{1,0:T(8,128)S(1)} %copy.13.ids_ref, f32[7,3,512]{2,1,0:T(4,128)S(1)} %copy.14.short_ref, f32[1,512]{1,0:T(1,128)S(1)} %bitcast.14, bf16[32,128]{1,0:T(8,128)(2,1)S(1)} %copy-done.3, ...), custom_call_target="tpu_custom_call" | custom-call | flops 3849999872 | bytes 2392064 | tf_op jit(solution)/shard_map/pallas_call | solution.py:347
  72.2 1.1 %collective-permute-start.23 = (bf16[192,512]{1,0:T(8,128)(2,1)S(1)}, bf16[192,512]{1,0:T(8,128)(2,1)S(1)}, u32[]{:S(2)}, u32[]{:S(2)}) collective-permute-start(bf16[192,512]{1,0:T(8,128)(2,1)S(1)} %collective-permute-done.21.refs_1_), channel_id=1, source_target_pairs={{0,8},{4,12},{8,0},{12,4},{16,24},{20,28},{24,16},{28,20},{1,9},{5... | collective-permute-start | bytes 589832 | tf_op jit(solution)/shard_map/ppermute | solution.py:19
  73.6 2.2 %shard_map.87.refs_2_ = bf16[1024,128]{1,0:T(8,128)(2,1)S(1)} custom-call(s32[2]{0:T(128)S(1)} %pad_add_fusion.3.where_ref, s32[1168,1]{1,0:T(8,128)S(1)} %copy.13.ids_ref, f32[7,3,512]{2,1,0:T(4,128)S(1)} %copy.14.short_ref, f32[1,512]{1,0:T(1,128)S(1)} %bitcast.15, bf16[32,128]{1,0:T(8,128)(2,1)S(1)} %copy-done.3, ...), custom_call_target="tpu_custom_call" | custom-call | flops 3849999872 | bytes 2392064 | tf_op jit(solution)/shard_map/pallas_call | solution.py:347
  75.8 0.8 collective-permute-start.26
  76.6 1.3 %collective-permute-done.23.refs_1_ = bf16[192,512]{1,0:T(8,128)(2,1)S(1)} collective-permute-done((bf16[192,512]{1,0:T(8,128)(2,1)S(1)}, bf16[192,512]{1,0:T(8,128)(2,1)S(1)}, u32[]{:S(2)}, u32[]{:S(2)}) %collective-permute-start.23) | collective-permute-done | bytes 196640 | tf_op jit(solution)/shard_map/ppermute | solution.py:19
  77.9 2.2 %shard_map.88.refs_3_ = bf16[1024,128]{1,0:T(8,128)(2,1)S(1)} custom-call(s32[2]{0:T(128)S(1)} %pad_add_fusion.4.where_ref, s32[1168,1]{1,0:T(8,128)S(1)} %copy.13.ids_ref, f32[7,3,512]{2,1,0:T(4,128)S(1)} %copy.14.short_ref, f32[1,512]{1,0:T(1,128)S(1)} %bitcast.16, bf16[32,128]{1,0:T(8,128)(2,1)S(1)} %copy-done.3, ...), custom_call_target="tpu_custom_call" | custom-call | flops 3849999872 | bytes 2392064 | tf_op jit(solution)/shard_map/pallas_call | solution.py:347
  80.1 1.8 %collective-permute-start.27 = (bf16[1024,128]{1,0:T(8,128)(2,1)S(1)}, bf16[1024,128]{1,0:T(8,128)(2,1)S(1)}, u32[]{:S(2)}, u32[]{:S(2)}) collective-permute-start(bf16[1024,128]{1,0:T(8,128)(2,1)S(1)} %shard_map.88.refs_3_), channel_id=1, source_target_pairs={{0,2},{1,3},{2,0},{3,1},{4,6},{5,7},{6,4},{7,5},{8,10},{9,11},{10,... | collective-permute-start | bytes 786440 | tf_op jit(solution)/shard_map/ppermute | solution.py:19
  81.9 4.0 %shard_map.89 = (bf16[2,1024,512]{2,1,0:T(8,128)(2,1)S(1)}, bf16[2,256,512]{2,1,0:T(8,128)(2,1)S(1)}) custom-call(s32[5]{0:T(128)S(1)} %stack.52.where_ref, bf16[1024,128]{1,0:T(8,128)(2,1)S(1)} %shard_map.85.refs_0_, bf16[1024,128]{1,0:T(8,128)(2,1)S(1)} %shard_map.86.refs_1_, bf16[1024,128]{1,0:T(8,128)(2,1)S(1)} %shard_map.87.refs_2_, ...), custom_call_target="tpu_custom_call" | custom-call | flops 4400000000 | bytes 4194304 | tf_op jit(solution)/shard_map/pallas_call | solution.py:378
  85.9 1.5 %collective-permute-done.27.refs_1_ = bf16[1024,128]{1,0:T(8,128)(2,1)S(1)} collective-permute-done((bf16[1024,128]{1,0:T(8,128)(2,1)S(1)}, bf16[1024,128]{1,0:T(8,128)(2,1)S(1)}, u32[]{:S(2)}, u32[]{:S(2)}) %collective-permute-start.27) | collective-permute-done | bytes 262176 | tf_op jit(solution)/shard_map/ppermute | solution.py:19
  87.4 0.8 shard_map.91
  88.3 0.8 shard_map.90.refs_2_
  89.1 1.9 %collective-permute-done.28.refs_3_ = bf16[1024,512]{1,0:T(8,128)(2,1)S(1)} collective-permute-done((bf16[1024,512]{1,0:T(8,128)(2,1)S(1)}, bf16[1024,512]{1,0:T(8,128)(2,1)S(1)}, u32[]{:S(2)}, u32[]{:S(2)}) %collective-permute-start.28) | collective-permute-done | bytes 1048608 | tf_op jit(solution)/shard_map/ppermute | solution.py:19
  91.0 1.8 %shard_map.92 = bf16[1024,512]{1,0:T(8,128)(2,1)} custom-call(bf16[2,1024,512]{2,1,0:T(8,128)(2,1)S(1)} %get-tuple-element.39.most_ref, bf16[2,256,512]{2,1,0:T(8,128)(2,1)S(1)} %get-tuple-element.40.weight_ref, bf16[1024,128]{1,0:T(8,128)(2,1)S(1)} %collective-permute-done.26.refs_0_, bf16[1024,128]{1,0:T(8,128)(2,1)S(1)} %collective-permute-done.27.refs_1_, ...), custom_call_target="tpu_custom_call" | custom-call | flops 1650000000 | bytes 4194304 | tf_op jit(solution)/shard_map/pallas_call | solution.py:419
  (53 shorter events, 2.3 us)
Async XLA Ops:
  0.0 17.7 %collective-permute-start.6 = (bf16[512,512]{1,0:T(8,128)(2,1)}, bf16[512,512]{1,0:T(8,128)(2,1)S(1)}, u32[]{:S(2)}, u32[]{:S(2)}) collective-permute-start(bf16[512,512]{1,0:T(8,128)(2,1)} %table_ref.1), channel_id=1, source_target_pairs={{0,2},{1,3},{2,0},{3,1},{4,6},{5,7},{6,4},{7,5},{8,10},{9,11},{10,... | collective-permute-start | bytes 1572872 | tf_op jit(solution)/shard_map/ppermute | solution.py:19
  3.0 14.7 %collective-permute-start = (bf16[512,256]{1,0:T(8,128)(2,1)}, bf16[512,256]{1,0:T(8,128)(2,1)}, u32[]{:S(2)}, u32[]{:S(2)}) collective-permute-start(bf16[512,256]{1,0:T(8,128)(2,1)} %param.15), channel_id=1, source_target_pairs={{0,16},{4,20},{8,24},{12,28},{16,0},{20,4},{24,8},{28,12},{1,17},{... | collective-permute-start | bytes 786440 | tf_op jit(solution)/shard_map/ppermute | solution.py:19
  5.6 1.1 %copy-start = (bf16[256,3,512]{2,0,1:T(8,128)(2,1)S(1)}, bf16[256,3,512]{2,0,1:T(8,128)(2,1)}, u32[]{:S(2)}) copy-start(bf16[256,3,512]{2,0,1:T(8,128)(2,1)} %param.11) | copy-start | bytes 2359300
  6.8 10.9 %copy-start.1 = (bf16[512,512]{1,0:T(8,128)(2,1)S(1)}, bf16[512,512]{1,0:T(8,128)(2,1)}, u32[]{:S(2)}) copy-start(bf16[512,512]{1,0:T(8,128)(2,1)} %table_ref.1) | copy-start | bytes 1572868
  8.6 20.7 %copy-start.6 = (s32[1024]{0:T(1024)S(1)}, s32[1024]{0:T(1024)}, u32[]{:S(2)}) copy-start(s32[1024]{0:T(1024)} %param.8) | copy-start | bytes 12292
  8.6 24.6 %copy-start.2 = (f32[2048]{0:T(1024)S(1)}, f32[2048]{0:T(1024)}, u32[]{:S(2)}) copy-start(f32[2048]{0:T(1024)} %param.10) | copy-start | bytes 24580
  8.6 9.6 %collective-permute-start.8 = (bf16[2,192,256]{2,1,0:T(8,128)(2,1)}, bf16[2,192,256]{2,1,0:T(8,128)(2,1)S(1)}, u32[]{:S(2)}, u32[]{:S(2)}) collective-permute-start(bf16[2,192,256]{2,1,0:T(8,128)(2,1)} %get-tuple-element.25), channel_id=1, source_target_pairs={{0,4},{4,0},{8,12},{12,8},{16,20},{20,16},{24,28},{28,24},{1,5},{5... | collective-permute-start | bytes 589832 | tf_op jit(solution)/shard_map/ppermute | solution.py:19
  10.2 11.5 %collective-permute-start.9 = (bf16[2,192,256]{2,1,0:T(8,128)(2,1)}, bf16[2,192,256]{2,1,0:T(8,128)(2,1)S(1)}, u32[]{:S(2)}, u32[]{:S(2)}) collective-permute-start(bf16[2,192,256]{2,1,0:T(8,128)(2,1)} %get-tuple-element.26), channel_id=1, source_target_pairs={{0,8},{4,12},{8,0},{12,4},{16,24},{20,28},{24,16},{28,20},{1,9},{5... | collective-permute-start | bytes 589832 | tf_op jit(solution)/shard_map/ppermute | solution.py:19
  11.8 14.4 %collective-permute-start.10 = (bf16[2,192,256]{2,1,0:T(8,128)(2,1)S(1)}, bf16[2,192,256]{2,1,0:T(8,128)(2,1)S(1)}, u32[]{:S(2)}, u32[]{:S(2)}) collective-permute-start(bf16[2,192,256]{2,1,0:T(8,128)(2,1)S(1)} %get-tuple-element.27), channel_id=1, source_target_pairs={{0,12},{4,8},{8,4},{12,0},{16,28},{20,24},{24,20},{28,16},{1,13},{... | collective-permute-start | bytes 589832 | tf_op jit(solution)/shard_map/ppermute | solution.py:19
  17.7 11.5 %collective-permute-start.5 = (bf16[512,512]{1,0:T(8,128)(2,1)S(1)}, bf16[512,512]{1,0:T(8,128)(2,1)S(1)}, u32[]{:S(2)}, u32[]{:S(2)}) collective-permute-start(bf16[512,512]{1,0:T(8,128)(2,1)S(1)} %copy-done.1), channel_id=1, source_target_pairs={{0,1},{1,0},{2,3},{3,2},{4,5},{5,4},{6,7},{7,6},{8,9},{9,8},{10,11... | collective-permute-start | bytes 1572872 | tf_op jit(solution)/shard_map/ppermute | solution.py:19
  17.7 11.6 %collective-permute-start.7 = (bf16[512,512]{1,0:T(8,128)(2,1)S(1)}, bf16[512,512]{1,0:T(8,128)(2,1)S(1)}, u32[]{:S(2)}, u32[]{:S(2)}) collective-permute-start(bf16[512,512]{1,0:T(8,128)(2,1)S(1)} %collective-permute-done.6.refs_2_), channel_id=1, source_target_pairs={{0,1},{1,0},{2,3},{3,2},{4,5},{5,4},{6,7},{7,6},{8,9},{9,8},{10,11... | collective-permute-start | bytes 1572872 | tf_op jit(solution)/shard_map/ppermute | solution.py:19
  18.2 29.2 %collective-permute-start.4 = (bf16[512,256]{1,0:T(8,128)(2,1)}, bf16[512,256]{1,0:T(8,128)(2,1)S(1)}, u32[]{:S(2)}, u32[]{:S(2)}) collective-permute-start(bf16[512,256]{1,0:T(8,128)(2,1)} %param.15), channel_id=1, source_target_pairs={{0,8},{4,12},{8,0},{12,4},{16,24},{20,28},{24,16},{28,20},{1,9},{5... | collective-permute-start | bytes 786440 | tf_op jit(solution)/shard_map/ppermute | solution.py:19
  27.3 7.9 %collective-permute-start.1 = (bf16[512,256]{1,0:T(8,128)(2,1)S(1)}, bf16[512,256]{1,0:T(8,128)(2,1)S(1)}, u32[]{:S(2)}, u32[]{:S(2)}) collective-permute-start(bf16[512,256]{1,0:T(8,128)(2,1)S(1)} %get-tuple-element.43), channel_id=1, source_target_pairs={{0,2},{1,3},{2,0},{3,1},{4,6},{5,7},{6,4},{7,5},{8,10},{9,11},{10,... | collective-permute-start | bytes 786440 | tf_op jit(solution)/shard_map/ppermute | solution.py:19
  27.9 25.1 %collective-permute-start.2 = (bf16[512,256]{1,0:T(8,128)(2,1)S(1)}, bf16[512,256]{1,0:T(8,128)(2,1)}, u32[]{:S(2)}, u32[]{:S(2)}) collective-permute-start(bf16[512,256]{1,0:T(8,128)(2,1)S(1)} %get-tuple-element.44.refs_6_), channel_id=1, source_target_pairs={{0,4},{4,0},{8,12},{12,8},{16,20},{20,16},{24,28},{28,24},{1,5},{5... | collective-permute-start | bytes 786440 | tf_op jit(solution)/shard_map/ppermute | solution.py:19
  29.2 16.7 %collective-permute-start.11 = (bf16[4,192,256]{2,1,0:T(8,128)(2,1)S(1)}, bf16[4,192,256]{2,1,0:T(8,128)(2,1)S(1)}, u32[]{:S(2)}, u32[]{:S(2)}) collective-permute-start(bf16[4,192,256]{2,1,0:T(8,128)(2,1)S(1)} %pad_maximum_fusion), channel_id=1, source_target_pairs={{0,16},{4,20},{8,24},{12,28},{16,0},{20,4},{24,8},{28,12},{1,17},{... | collective-permute-start | bytes 1179656 | tf_op jit(solution)/shard_map/ppermute | solution.py:19
  29.4 7.9 %collective-permute-start.12 = (s32[144]{0:T(256)S(1)}, s32[144]{0:T(256)S(1)}, u32[]{:S(2)}, u32[]{:S(2)}) collective-permute-start(s32[144]{0:T(256)S(1)} %slice.19), channel_id=1, source_target_pairs={{0,4},{4,8},{8,12},{12,16},{16,20},{20,24},{24,28},{1,5},{5,9},{9,... | collective-permute-start | bytes 1736 | tf_op jit(solution)/shard_map/ppermute | solution.py:290
  35.2 12.4 %collective-permute-start.13 = (bf16[512,256]{1,0:T(8,128)(2,1)}, bf16[512,256]{1,0:T(8,128)(2,1)S(1)}, u32[]{:S(2)}, u32[]{:S(2)}) collective-permute-start(bf16[512,256]{1,0:T(8,128)(2,1)} %collective-permute-done), channel_id=1, source_target_pairs={{0,8},{4,12},{8,0},{12,4},{16,24},{20,28},{24,16},{28,20},{1,9},{5... | collective-permute-start | bytes 786440 | tf_op jit(solution)/shard_map/ppermute | solution.py:19
  37.3 16.8 %collective-permute-start.3 = (bf16[512,256]{1,0:T(8,128)(2,1)S(1)}, bf16[512,256]{1,0:T(8,128)(2,1)S(1)}, u32[]{:S(2)}, u32[]{:S(2)}) collective-permute-start(bf16[512,256]{1,0:T(8,128)(2,1)S(1)} %collective-permute-done.1.refs_7_), channel_id=1, source_target_pairs={{0,4},{4,0},{8,12},{12,8},{16,20},{20,16},{24,28},{28,24},{1,5},{5... | collective-permute-start | bytes 786440 | tf_op jit(solution)/shard_map/ppermute | solution.py:19
  38.8 10.4 %copy-start.5 = (f32[7,3,512]{2,0,1:T(8,128)S(1)}, f32[7,3,512]{2,0,1:T(8,128)}, u32[]{:S(2)}) copy-start(f32[7,3,512]{2,0,1:T(8,128)} %param.12) | copy-start | bytes 129028
  38.8 17.5 %copy-start.3 = (bf16[32,128]{1,0:T(8,128)(2,1)S(1)}, bf16[32,128]{1,0:T(8,128)(2,1)}, u32[]{:S(2)}) copy-start(bf16[32,128]{1,0:T(8,128)(2,1)} %filter_ref.7) | copy-start | bytes 24580
  38.8 17.5 %copy-start.4 = (f32[512]{0:T(512)S(1)}, f32[512]{0:T(512)}, u32[]{:S(2)}) copy-start(f32[512]{0:T(512)} %param.14) | copy-start | bytes 6148
  47.6 7.6 %collective-permute-start.14 = (bf16[512,256]{1,0:T(8,128)(2,1)S(1)}, bf16[512,256]{1,0:T(8,128)(2,1)S(1)}, u32[]{:S(2)}, u32[]{:S(2)}) collective-permute-start(bf16[512,256]{1,0:T(8,128)(2,1)S(1)} %get-tuple-element.41), channel_id=1, source_target_pairs={{0,2},{1,3},{2,0},{3,1},{4,6},{5,7},{6,4},{7,5},{8,10},{9,11},{10,... | collective-permute-start | bytes 786440 | tf_op jit(solution)/shard_map/ppermute | solution.py:19
  49.2 7.0 %collective-permute-start.15 = (bf16[192,512]{1,0:T(8,128)(2,1)S(1)}, bf16[192,512]{1,0:T(8,128)(2,1)S(1)}, u32[]{:S(2)}, u32[]{:S(2)}) collective-permute-start(bf16[192,512]{1,0:T(8,128)(2,1)S(1)} %shard_map.84.refs_0_), channel_id=1, source_target_pairs={{0,4},{4,0},{8,12},{12,8},{16,20},{20,16},{24,28},{28,24},{1,5},{5... | collective-permute-start | bytes 589832 | tf_op jit(solution)/shard_map/ppermute | solution.py:19
  52.1 10.7 %collective-permute-start.20 = (bf16[192,512]{1,0:T(8,128)(2,1)S(1)}, bf16[192,512]{1,0:T(8,128)(2,1)S(1)}, u32[]{:S(2)}, u32[]{:S(2)}) collective-permute-start(bf16[192,512]{1,0:T(8,128)(2,1)S(1)} %shard_map.84.refs_0_), channel_id=1, source_target_pairs={{0,16},{4,20},{8,24},{12,28},{16,0},{20,4},{24,8},{28,12},{1,17},{... | collective-permute-start | bytes 589832 | tf_op jit(solution)/shard_map/ppermute | solution.py:19
  53.1 8.8 %collective-permute-start.17 = (bf16[192,512]{1,0:T(8,128)(2,1)S(1)}, bf16[192,512]{1,0:T(8,128)(2,1)S(1)}, u32[]{:S(2)}, u32[]{:S(2)}) collective-permute-start(bf16[192,512]{1,0:T(8,128)(2,1)S(1)} %shard_map.84.refs_0_), channel_id=1, source_target_pairs={{0,8},{4,12},{8,0},{12,4},{16,24},{20,28},{24,16},{28,20},{1,9},{5... | collective-permute-start | bytes 589832 | tf_op jit(solution)/shard_map/ppermute | solution.py:19
  54.1 10.7 %collective-permute-start.16 = (bf16[512,256]{1,0:T(8,128)(2,1)S(1)}, bf16[512,256]{1,0:T(8,128)(2,1)S(1)}, u32[]{:S(2)}, u32[]{:S(2)}) collective-permute-start(bf16[512,256]{1,0:T(8,128)(2,1)S(1)} %get-tuple-element.42.refs_10_), channel_id=1, source_target_pairs={{0,4},{4,0},{8,12},{12,8},{16,20},{20,16},{24,28},{28,24},{1,5},{5... | collective-permute-start | bytes 786440 | tf_op jit(solution)/shard_map/ppermute | solution.py:19
  61.9 7.8 %collective-permute-start.18 = (bf16[192,512]{1,0:T(8,128)(2,1)S(1)}, bf16[192,512]{1,0:T(8,128)(2,1)S(1)}, u32[]{:S(2)}, u32[]{:S(2)}) collective-permute-start(bf16[192,512]{1,0:T(8,128)(2,1)S(1)} %collective-permute-done.17.refs_0_), channel_id=1, source_target_pairs={{0,4},{4,0},{8,12},{12,8},{16,20},{20,16},{24,28},{28,24},{1,5},{5... | collective-permute-start | bytes 589832 | tf_op jit(solution)/shard_map/ppermute | solution.py:19
  62.8 9.5 %collective-permute-start.21 = (bf16[192,512]{1,0:T(8,128)(2,1)S(1)}, bf16[192,512]{1,0:T(8,128)(2,1)S(1)}, u32[]{:S(2)}, u32[]{:S(2)}) collective-permute-start(bf16[192,512]{1,0:T(8,128)(2,1)S(1)} %collective-permute-done.20.refs_0_), channel_id=1, source_target_pairs={{0,4},{4,0},{8,12},{12,8},{16,20},{20,16},{24,28},{28,24},{1,5},{5... | collective-permute-start | bytes 589832 | tf_op jit(solution)/shard_map/ppermute | solution.py:19
  64.1 12.6 %collective-permute-start.22 = (bf16[192,512]{1,0:T(8,128)(2,1)S(1)}, bf16[192,512]{1,0:T(8,128)(2,1)S(1)}, u32[]{:S(2)}, u32[]{:S(2)}) collective-permute-start(bf16[192,512]{1,0:T(8,128)(2,1)S(1)} %collective-permute-done.20.refs_0_), channel_id=1, source_target_pairs={{0,8},{4,12},{8,0},{12,4},{16,24},{20,28},{24,16},{28,20},{1,9},{5... | collective-permute-start | bytes 589832 | tf_op jit(solution)/shard_map/ppermute | solution.py:19
  64.4 9.2 %collective-permute-start.19 = (bf16[1024,128]{1,0:T(8,128)(2,1)S(1)}, bf16[1024,128]{1,0:T(8,128)(2,1)S(1)}, u32[]{:S(2)}, u32[]{:S(2)}) collective-permute-start(bf16[1024,128]{1,0:T(8,128)(2,1)S(1)} %shard_map.85.refs_0_), channel_id=1, source_target_pairs={{0,2},{1,3},{2,0},{3,1},{4,6},{5,7},{6,4},{7,5},{8,10},{9,11},{10,... | collective-permute-start | bytes 786440 | tf_op jit(solution)/shard_map/ppermute | solution.py:19
  64.8 17.1 %collective-permute-start.25 = (bf16[512,256]{1,0:T(8,128)(2,1)S(1)}, bf16[512,256]{1,0:T(8,128)(2,1)S(1)}, u32[]{:S(2)}, u32[]{:S(2)}) collective-permute-start(bf16[512,256]{1,0:T(8,128)(2,1)S(1)} %collective-permute-done.14.refs_11_), channel_id=1, source_target_pairs={{0,4},{4,0},{8,12},{12,8},{16,20},{20,16},{24,28},{28,24},{1,5},{5... | collective-permute-start | bytes 786440 | tf_op jit(solution)/shard_map/ppermute | solution.py:19
  71.9 10.0 %collective-permute-start.24 = (bf16[1024,128]{1,0:T(8,128)(2,1)S(1)}, bf16[1024,128]{1,0:T(8,128)(2,1)S(1)}, u32[]{:S(2)}, u32[]{:S(2)}) collective-permute-start(bf16[1024,128]{1,0:T(8,128)(2,1)S(1)} %shard_map.86.refs_1_), channel_id=1, source_target_pairs={{0,2},{1,3},{2,0},{3,1},{4,6},{5,7},{6,4},{7,5},{8,10},{9,11},{10,... | collective-permute-start | bytes 786440 | tf_op jit(solution)/shard_map/ppermute | solution.py:19
  72.2 5.7 %collective-permute-start.23 = (bf16[192,512]{1,0:T(8,128)(2,1)S(1)}, bf16[192,512]{1,0:T(8,128)(2,1)S(1)}, u32[]{:S(2)}, u32[]{:S(2)}) collective-permute-start(bf16[192,512]{1,0:T(8,128)(2,1)S(1)} %collective-permute-done.21.refs_1_), channel_id=1, source_target_pairs={{0,8},{4,12},{8,0},{12,4},{16,24},{20,28},{24,16},{28,20},{1,9},{5... | collective-permute-start | bytes 589832 | tf_op jit(solution)/shard_map/ppermute | solution.py:19
  75.8 10.1 %collective-permute-start.26 = (bf16[1024,128]{1,0:T(8,128)(2,1)S(1)}, bf16[1024,128]{1,0:T(8,128)(2,1)S(1)}, u32[]{:S(2)}, u32[]{:S(2)}) collective-permute-start(bf16[1024,128]{1,0:T(8,128)(2,1)S(1)} %shard_map.87.refs_2_), channel_id=1, source_target_pairs={{0,2},{1,3},{2,0},{3,1},{4,6},{5,7},{6,4},{7,5},{8,10},{9,11},{10,... | collective-permute-start | bytes 786440 | tf_op jit(solution)/shard_map/ppermute | solution.py:19
  80.1 7.3 %collective-permute-start.27 = (bf16[1024,128]{1,0:T(8,128)(2,1)S(1)}, bf16[1024,128]{1,0:T(8,128)(2,1)S(1)}, u32[]{:S(2)}, u32[]{:S(2)}) collective-permute-start(bf16[1024,128]{1,0:T(8,128)(2,1)S(1)} %shard_map.88.refs_3_), channel_id=1, source_target_pairs={{0,2},{1,3},{2,0},{3,1},{4,6},{5,7},{6,4},{7,5},{8,10},{9,11},{10,... | collective-permute-start | bytes 786440 | tf_op jit(solution)/shard_map/ppermute | solution.py:19
  88.2 2.7 %collective-permute-start.28 = (bf16[1024,512]{1,0:T(8,128)(2,1)S(1)}, bf16[1024,512]{1,0:T(8,128)(2,1)S(1)}, u32[]{:S(2)}, u32[]{:S(2)}) collective-permute-start(bf16[1024,512]{1,0:T(8,128)(2,1)S(1)} %shard_map.91), channel_id=1, source_target_pairs={{0,1},{1,0},{2,3},{3,2},{4,5},{5,4},{6,7},{7,6},{8,9},{9,8},{10,11... | collective-permute-start | bytes 3145736 | tf_op jit(solution)/shard_map/ppermute | solution.py:19

commit v6 on v5

--- a/solution.py
+++ b/solution.py
@@ -395,7 +395,7 @@
         ],
     )(where, *gates, *row_gates[:-late], *halves)
 
-    rows = tokens // 2
+    rows = tokens
 
     def stepped(kernel, half, more):
         return pl.pallas_call(
@@ -409,7 +409,7 @@
             + [pl.BlockSpec((rows, width), lambda i: (i, 0))] * more,
             out_specs=pl.BlockSpec((rows, width), lambda i: (i, 0)),
             out_shape=jax.ShapeDtypeStruct((tokens, width), BF),
-            compiler_params=pltpu.CompilerParams(vmem_limit_bytes=12 * MIB),
+            compiler_params=pltpu.CompilerParams(vmem_limit_bytes=40 * MIB),
             cost_estimate=pl.CostEstimate(
                 flops=cost_us(1.5), bytes_accessed=8 * tokens * width, transcendentals=0
             ),

time: 93 us -> 92.7 us (level)
  no operation moved by 1% of the time
where the time goes in v6:
time: 92.7 us; the launch traced here: 92.4 us
  starting transfers between devices  34 us (37%)
  waiting for transfers between devices  33.9 us (37%)
  Pallas kernels  21.1 us (23%)
  local copies, waits for them, and re-layouts  1.63 us (2%)
  other arithmetic  1.54 us (2%)
    ppermute x28, waiting for transfers between devices, swap(): return lax.ppermute(block, axis, [(i, i ^ offset) for i in range(count)])  33.9 us
    ppermute x28, starting transfers between devices, swap(): return lax.ppermute(block, axis, [(i, i ^ offset) for i in range(count)])  30.2 us
    pallas_call x4, Pallas kernels, body(): pl.pallas_call(functools.partial(mixer_kernel, width // groups), grid_spe...  8.72 us
    pallas_call x1, Pallas kernels, body(): call(functools.partial(most_kernel, chunks, late), [jax.ShapeDtypeStruct(...  3.97 us
    ppermute x1, starting transfers between devices, body(): lax.ppermute(after(token_ids, table_both)[tokens - halo:], 'seq', [(i, i...  3.8 us
  transfers between devices with their start and end apart: 29, of which 13 were waited for; matrix products, arithmetic and copies ran while one was open for 2% of the time, Pallas kernels for 20%

profile of v6, /device:TPU:0, one launch (start us, length us, event | category | flops | bytes accessed | tf_op | source)
XLA Modules:
  0.0 92.4 jit_solution(3945978652337759177)
XLA Ops:
  0.0 3.0 %collective-permute-start.6 = (bf16[512,512]{1,0:T(8,128)(2,1)}, bf16[512,512]{1,0:T(8,128)(2,1)S(1)}, u32[]{:S(2)}, u32[]{:S(2)}) collective-permute-start(bf16[512,512]{1,0:T(8,128)(2,1)} %table_ref.1), channel_id=1, source_target_pairs={{0,2},{1,3},{2,0},{3,1},{4,6},{5,7},{6,4},{7,5},{8,10},{9,11},{10,... | collective-permute-start | bytes 1572872 | tf_op jit(solution)/shard_map/ppermute | solution.py:19
  3.0 2.6 %collective-permute-start = (bf16[512,256]{1,0:T(8,128)(2,1)}, bf16[512,256]{1,0:T(8,128)(2,1)}, u32[]{:S(2)}, u32[]{:S(2)}) collective-permute-start(bf16[512,256]{1,0:T(8,128)(2,1)} %param.15), channel_id=1, source_target_pairs={{0,16},{4,20},{8,24},{12,28},{16,0},{20,4},{24,8},{28,12},{1,17},{... | collective-permute-start | bytes 786440 | tf_op jit(solution)/shard_map/ppermute | solution.py:19
  5.6 1.1 %copy-done = bf16[256,3,512]{2,0,1:T(8,128)(2,1)S(1)} copy-done((bf16[256,3,512]{2,0,1:T(8,128)(2,1)S(1)}, bf16[256,3,512]{2,0,1:T(8,128)(2,1)}, u32[]{:S(2)}) %copy-start) | copy-done | bytes 786456
  6.8 1.8 %shard_map.83 = (bf16[2,192,256]{2,1,0:T(8,128)(2,1)S(1)}, bf16[2,192,256]{2,1,0:T(8,128)(2,1)}, bf16[2,192,256]{2,1,0:T(8,128)(2,1)}, bf16[2,192,256]{2,1,0:T(8,128)(2,1)S(1)}) custom-call(s32[5]{0:T(128)S(1)} %stack.52.where_ref, bf16[3,256,512]{2,1,0:T(8,128)(2,1)S(1)} %bitcast.11), custom_call_target="tpu_custom_call" | custom-call | flops 1100000000 | bytes 1572864 | tf_op jit(solution)/shard_map/pallas_call | solution.py:268
  8.6 1.6 %collective-permute-start.8 = (bf16[2,192,256]{2,1,0:T(8,128)(2,1)}, bf16[2,192,256]{2,1,0:T(8,128)(2,1)S(1)}, u32[]{:S(2)}, u32[]{:S(2)}) collective-permute-start(bf16[2,192,256]{2,1,0:T(8,128)(2,1)} %get-tuple-element.25), channel_id=1, source_target_pairs={{0,4},{4,0},{8,12},{12,8},{16,20},{20,16},{24,28},{28,24},{1,5},{5... | collective-permute-start | bytes 589832 | tf_op jit(solution)/shard_map/ppermute | solution.py:19
  10.2 1.6 %collective-permute-start.9 = (bf16[2,192,256]{2,1,0:T(8,128)(2,1)}, bf16[2,192,256]{2,1,0:T(8,128)(2,1)S(1)}, u32[]{:S(2)}, u32[]{:S(2)}) collective-permute-start(bf16[2,192,256]{2,1,0:T(8,128)(2,1)} %get-tuple-element.26), channel_id=1, source_target_pairs={{0,8},{4,12},{8,0},{12,4},{16,24},{20,28},{24,16},{28,20},{1,9},{5... | collective-permute-start | bytes 589832 | tf_op jit(solution)/shard_map/ppermute | solution.py:19
  11.8 0.4 collective-permute-start.10
  12.2 5.5 %collective-permute-done = bf16[512,256]{1,0:T(8,128)(2,1)} collective-permute-done((bf16[512,256]{1,0:T(8,128)(2,1)}, bf16[512,256]{1,0:T(8,128)(2,1)}, u32[]{:S(2)}, u32[]{:S(2)}) %collective-permute-start) | collective-permute-done | bytes 262176 | tf_op jit(solution)/shard_map/ppermute | solution.py:19
  17.7 0.5 collective-permute-start.7
  18.2 0.7 collective-permute-start.4
  18.9 2.9 %collective-permute-done.9.refs_2_ = bf16[2,192,256]{2,1,0:T(8,128)(2,1)S(1)} collective-permute-done((bf16[2,192,256]{2,1,0:T(8,128)(2,1)}, bf16[2,192,256]{2,1,0:T(8,128)(2,1)S(1)}, u32[]{:S(2)}, u32[]{:S(2)}) %collective-permute-start.9) | collective-permute-done | bytes 196640 | tf_op jit(solution)/shard_map/ppermute | solution.py:19
  21.8 4.5 %collective-permute-done.10.refs_3_ = bf16[2,192,256]{2,1,0:T(8,128)(2,1)S(1)} collective-permute-done((bf16[2,192,256]{2,1,0:T(8,128)(2,1)S(1)}, bf16[2,192,256]{2,1,0:T(8,128)(2,1)S(1)}, u32[]{:S(2)}, u32[]{:S(2)}) %collective-permute-start.10) | collective-permute-done | bytes 196640 | tf_op jit(solution)/shard_map/ppermute | solution.py:19
  26.2 1.1 %broadcast_select_fusion.2 = (bf16[512,256]{1,0:T(8,128)(2,1)S(1)}, bf16[512,256]{1,0:T(8,128)(2,1)S(1)}) fusion(bf16[512,256]{1,0:T(8,128)(2,1)} %collective-permute-done, bf16[512,256]{1,0:T(8,128)(2,1)} %param.15, pred[]{:T(512)S(6)} %eq.6), kind=kLoop, calls=%fused_computation.3 | loop fusion | flops 262144 | bytes 1048577 | tf_op jit(solution)/shard_map/jit(_where)/select_n | solution.py:326
  27.3 0.6 collective-permute-start.1
  27.9 1.2 %collective-permute-start.2 = (bf16[512,256]{1,0:T(8,128)(2,1)S(1)}, bf16[512,256]{1,0:T(8,128)(2,1)}, u32[]{:S(2)}, u32[]{:S(2)}) collective-permute-start(bf16[512,256]{1,0:T(8,128)(2,1)S(1)} %get-tuple-element.44.refs_6_), channel_id=1, source_target_pairs={{0,4},{4,0},{8,12},{12,8},{16,20},{20,16},{24,28},{28,24},{1,5},{5... | collective-permute-start | bytes 786440 | tf_op jit(solution)/shard_map/ppermute | solution.py:19
  29.4 3.8 %collective-permute-start.12 = (s32[144]{0:T(256)S(1)}, s32[144]{0:T(256)S(1)}, u32[]{:S(2)}, u32[]{:S(2)}) collective-permute-start(s32[144]{0:T(256)S(1)} %slice.19), channel_id=1, source_target_pairs={{0,4},{4,8},{8,12},{12,16},{16,20},{20,24},{24,28},{1,5},{5,9},{9,... | collective-permute-start | bytes 1736 | tf_op jit(solution)/shard_map/ppermute | solution.py:290
  33.2 1.8 %shard_map.82.normed_ref = bf16[8,512,256]{2,1,0:T(8,128)(2,1)S(1)} custom-call(s32[5]{0:T(128)S(1)} %stack.52.where_ref, f32[4,1,512]{2,1,0:T(1,128)S(1)} %bitcast.12, bf16[512,512]{1,0:T(8,128)(2,1)S(1)} %copy-done.1, bf16[512,512]{1,0:T(8,128)(2,1)S(1)} %collective-permute-done.5.refs_1_, bf16[512,512]{1,0:T(8,128)(2,1)S(1)} %collective-permute-done.6.refs_2_, ...), custom_call_target="tpu_custom_call" | custom-call | flops 1650000000 | bytes 4194304 | tf_op jit(solution)/shard_map/pallas_call | solution.py:296
  35.0 2.1 %collective-permute-start.13 = (bf16[512,256]{1,0:T(8,128)(2,1)}, bf16[512,256]{1,0:T(8,128)(2,1)S(1)}, u32[]{:S(2)}, u32[]{:S(2)}) collective-permute-start(bf16[512,256]{1,0:T(8,128)(2,1)} %collective-permute-done), channel_id=1, source_target_pairs={{0,8},{4,12},{8,0},{12,4},{16,24},{20,28},{24,16},{28,20},{1,9},{5... | collective-permute-start | bytes 786440 | tf_op jit(solution)/shard_map/ppermute | solution.py:19
  37.1 1.4 %collective-permute-start.3 = (bf16[512,256]{1,0:T(8,128)(2,1)S(1)}, bf16[512,256]{1,0:T(8,128)(2,1)S(1)}, u32[]{:S(2)}, u32[]{:S(2)}) collective-permute-start(bf16[512,256]{1,0:T(8,128)(2,1)S(1)} %collective-permute-done.1.refs_7_), channel_id=1, source_target_pairs={{0,4},{4,0},{8,12},{12,8},{16,20},{20,16},{24,28},{28,24},{1,5},{5... | collective-permute-start | bytes 786440 | tf_op jit(solution)/shard_map/ppermute | solution.py:19
  38.7 7.2 %collective-permute-done.11.crossing_ref = bf16[4,192,256]{2,1,0:T(8,128)(2,1)S(1)} collective-permute-done((bf16[4,192,256]{2,1,0:T(8,128)(2,1)S(1)}, bf16[4,192,256]{2,1,0:T(8,128)(2,1)S(1)}, u32[]{:S(2)}, u32[]{:S(2)}) %collective-permute-start.11) | collective-permute-done | bytes 393248 | tf_op jit(solution)/shard_map/ppermute | solution.py:19
  45.9 1.5 %shard_map.84.refs_0_ = bf16[192,512]{1,0:T(8,128)(2,1)S(1)} custom-call(s32[5]{0:T(128)S(1)} %stack.52.where_ref, bf16[8,512,256]{2,1,0:T(8,128)(2,1)S(1)} %shard_map.82.normed_ref, bf16[4,192,256]{2,1,0:T(8,128)(2,1)S(1)} %collective-permute-done.11.crossing_ref, bf16[2,192,256]{2,1,0:T(8,128)(2,1)S(1)} %get-tuple-element.30.refs_0_, ...), custom_call_target="tpu_custom_call" | custom-call | flops 11000000512 | bytes 2883584 | tf_op jit(solution)/shard_map/pallas_call | solution.py:308
  47.5 1.6 %collective-permute-start.14 = (bf16[512,256]{1,0:T(8,128)(2,1)S(1)}, bf16[512,256]{1,0:T(8,128)(2,1)S(1)}, u32[]{:S(2)}, u32[]{:S(2)}) collective-permute-start(bf16[512,256]{1,0:T(8,128)(2,1)S(1)} %get-tuple-element.41), channel_id=1, source_target_pairs={{0,2},{1,3},{2,0},{3,1},{4,6},{5,7},{6,4},{7,5},{8,10},{9,11},{10,... | collective-permute-start | bytes 786440 | tf_op jit(solution)/shard_map/ppermute | solution.py:19
  49.1 2.4 %collective-permute-start.15 = (bf16[192,512]{1,0:T(8,128)(2,1)S(1)}, bf16[192,512]{1,0:T(8,128)(2,1)S(1)}, u32[]{:S(2)}, u32[]{:S(2)}) collective-permute-start(bf16[192,512]{1,0:T(8,128)(2,1)S(1)} %shard_map.84.refs_0_), channel_id=1, source_target_pairs={{0,4},{4,0},{8,12},{12,8},{16,20},{20,16},{24,28},{28,24},{1,5},{5... | collective-permute-start | bytes 589832 | tf_op jit(solution)/shard_map/ppermute | solution.py:19
  51.9 1.1 %collective-permute-start.20 = (bf16[192,512]{1,0:T(8,128)(2,1)S(1)}, bf16[192,512]{1,0:T(8,128)(2,1)S(1)}, u32[]{:S(2)}, u32[]{:S(2)}) collective-permute-start(bf16[192,512]{1,0:T(8,128)(2,1)S(1)} %shard_map.84.refs_0_), channel_id=1, source_target_pairs={{0,16},{4,20},{8,24},{12,28},{16,0},{20,4},{24,8},{28,12},{1,17},{... | collective-permute-start | bytes 589832 | tf_op jit(solution)/shard_map/ppermute | solution.py:19
  53.1 0.9 collective-permute-start.17
  53.9 0.8 collective-permute-start.16
  54.7 0.5 collective-permute-done.14.refs_11_
  55.2 0.7 collective-permute-done.15.refs_1_
  55.9 2.2 %shard_map.85.refs_0_ = bf16[1024,128]{1,0:T(8,128)(2,1)S(1)} custom-call(s32[2]{0:T(128)S(1)} %pad_add_fusion.1.where_ref, s32[1168,1]{1,0:T(8,128)S(1)} %copy.13.ids_ref, f32[7,3,512]{2,1,0:T(4,128)S(1)} %copy.14.short_ref, f32[1,512]{1,0:T(1,128)S(1)} %bitcast.13, bf16[32,128]{1,0:T(8,128)(2,1)S(1)} %copy-done.3, bf16[192,512]{1,0:T(8,128)(2,1)S(1)} %shard_map.84.refs_0_, ...), custom_call_target="tpu_custom_call" | custom-call | flops 3849999872 | bytes 2392064 | tf_op jit(solution)/shard_map/pallas_call | solution.py:347
  58.1 3.8 %collective-permute-done.17.refs_0_ = bf16[192,512]{1,0:T(8,128)(2,1)S(1)} collective-permute-done((bf16[192,512]{1,0:T(8,128)(2,1)S(1)}, bf16[192,512]{1,0:T(8,128)(2,1)S(1)}, u32[]{:S(2)}, u32[]{:S(2)}) %collective-permute-start.17) | collective-permute-done | bytes 196640 | tf_op jit(solution)/shard_map/ppermute | solution.py:19
  61.9 0.8 collective-permute-start.18
  62.8 1.3 %collective-permute-start.21 = (bf16[192,512]{1,0:T(8,128)(2,1)S(1)}, bf16[192,512]{1,0:T(8,128)(2,1)S(1)}, u32[]{:S(2)}, u32[]{:S(2)}) collective-permute-start(bf16[192,512]{1,0:T(8,128)(2,1)S(1)} %collective-permute-done.20.refs_0_), channel_id=1, source_target_pairs={{0,4},{4,0},{8,12},{12,8},{16,20},{20,16},{24,28},{28,24},{1,5},{5... | collective-permute-start | bytes 589832 | tf_op jit(solution)/shard_map/ppermute | solution.py:19
  64.4 0.4 collective-permute-start.19
  64.8 0.5 collective-permute-start.25
  65.4 4.3 %collective-permute-done.18.refs_1_ = bf16[192,512]{1,0:T(8,128)(2,1)S(1)} collective-permute-done((bf16[192,512]{1,0:T(8,128)(2,1)S(1)}, bf16[192,512]{1,0:T(8,128)(2,1)S(1)}, u32[]{:S(2)}, u32[]{:S(2)}) %collective-permute-start.18) | collective-permute-done | bytes 196640 | tf_op jit(solution)/shard_map/ppermute | solution.py:19
  69.7 2.2 %shard_map.86.refs_1_ = bf16[1024,128]{1,0:T(8,128)(2,1)S(1)} custom-call(s32[2]{0:T(128)S(1)} %pad_add_fusion.2.where_ref, s32[1168,1]{1,0:T(8,128)S(1)} %copy.13.ids_ref, f32[7,3,512]{2,1,0:T(4,128)S(1)} %copy.14.short_ref, f32[1,512]{1,0:T(1,128)S(1)} %bitcast.14, bf16[32,128]{1,0:T(8,128)(2,1)S(1)} %copy-done.3, ...), custom_call_target="tpu_custom_call" | custom-call | flops 3849999872 | bytes 2392064 | tf_op jit(solution)/shard_map/pallas_call | solution.py:347
  72.1 1.2 %collective-permute-start.23 = (bf16[192,512]{1,0:T(8,128)(2,1)S(1)}, bf16[192,512]{1,0:T(8,128)(2,1)S(1)}, u32[]{:S(2)}, u32[]{:S(2)}) collective-permute-start(bf16[192,512]{1,0:T(8,128)(2,1)S(1)} %collective-permute-done.21.refs_1_), channel_id=1, source_target_pairs={{0,8},{4,12},{8,0},{12,4},{16,24},{20,28},{24,16},{28,20},{1,9},{5... | collective-permute-start | bytes 589832 | tf_op jit(solution)/shard_map/ppermute | solution.py:19
  73.5 2.2 %shard_map.87.refs_2_ = bf16[1024,128]{1,0:T(8,128)(2,1)S(1)} custom-call(s32[2]{0:T(128)S(1)} %pad_add_fusion.3.where_ref, s32[1168,1]{1,0:T(8,128)S(1)} %copy.13.ids_ref, f32[7,3,512]{2,1,0:T(4,128)S(1)} %copy.14.short_ref, f32[1,512]{1,0:T(1,128)S(1)} %bitcast.15, bf16[32,128]{1,0:T(8,128)(2,1)S(1)} %copy-done.3, ...), custom_call_target="tpu_custom_call" | custom-call | flops 3849999872 | bytes 2392064 | tf_op jit(solution)/shard_map/pallas_call | solution.py:347
  75.7 0.9 collective-permute-start.26
  76.6 1.2 %collective-permute-done.23.refs_1_ = bf16[192,512]{1,0:T(8,128)(2,1)S(1)} collective-permute-done((bf16[192,512]{1,0:T(8,128)(2,1)S(1)}, bf16[192,512]{1,0:T(8,128)(2,1)S(1)}, u32[]{:S(2)}, u32[]{:S(2)}) %collective-permute-start.23) | collective-permute-done | bytes 196640 | tf_op jit(solution)/shard_map/ppermute | solution.py:19
  77.8 2.2 %shard_map.88.refs_3_ = bf16[1024,128]{1,0:T(8,128)(2,1)S(1)} custom-call(s32[2]{0:T(128)S(1)} %pad_add_fusion.4.where_ref, s32[1168,1]{1,0:T(8,128)S(1)} %copy.13.ids_ref, f32[7,3,512]{2,1,0:T(4,128)S(1)} %copy.14.short_ref, f32[1,512]{1,0:T(1,128)S(1)} %bitcast.16, bf16[32,128]{1,0:T(8,128)(2,1)S(1)} %copy-done.3, ...), custom_call_target="tpu_custom_call" | custom-call | flops 3849999872 | bytes 2392064 | tf_op jit(solution)/shard_map/pallas_call | solution.py:347
  80.0 1.9 %collective-permute-start.27 = (bf16[1024,128]{1,0:T(8,128)(2,1)S(1)}, bf16[1024,128]{1,0:T(8,128)(2,1)S(1)}, u32[]{:S(2)}, u32[]{:S(2)}) collective-permute-start(bf16[1024,128]{1,0:T(8,128)(2,1)S(1)} %shard_map.88.refs_3_), channel_id=1, source_target_pairs={{0,2},{1,3},{2,0},{3,1},{4,6},{5,7},{6,4},{7,5},{8,10},{9,11},{10,... | collective-permute-start | bytes 786440 | tf_op jit(solution)/shard_map/ppermute | solution.py:19
  81.9 4.0 %shard_map.89 = (bf16[2,1024,512]{2,1,0:T(8,128)(2,1)S(1)}, bf16[2,256,512]{2,1,0:T(8,128)(2,1)S(1)}) custom-call(s32[5]{0:T(128)S(1)} %stack.52.where_ref, bf16[1024,128]{1,0:T(8,128)(2,1)S(1)} %shard_map.85.refs_0_, bf16[1024,128]{1,0:T(8,128)(2,1)S(1)} %shard_map.86.refs_1_, bf16[1024,128]{1,0:T(8,128)(2,1)S(1)} %shard_map.87.refs_2_, ...), custom_call_target="tpu_custom_call" | custom-call | flops 4400000000 | bytes 4194304 | tf_op jit(solution)/shard_map/pallas_call | solution.py:378
  85.9 1.3 %collective-permute-done.27.refs_1_ = bf16[1024,128]{1,0:T(8,128)(2,1)S(1)} collective-permute-done((bf16[1024,128]{1,0:T(8,128)(2,1)S(1)}, bf16[1024,128]{1,0:T(8,128)(2,1)S(1)}, u32[]{:S(2)}, u32[]{:S(2)}) %collective-permute-start.27) | collective-permute-done | bytes 262176 | tf_op jit(solution)/shard_map/ppermute | solution.py:19
  87.2 0.7 shard_map.91
  88.0 0.8 shard_map.90.refs_2_
  88.7 1.9 %collective-permute-done.28.refs_3_ = bf16[1024,512]{1,0:T(8,128)(2,1)S(1)} collective-permute-done((bf16[1024,512]{1,0:T(8,128)(2,1)S(1)}, bf16[1024,512]{1,0:T(8,128)(2,1)S(1)}, u32[]{:S(2)}, u32[]{:S(2)}) %collective-permute-start.28) | collective-permute-done | bytes 1048608 | tf_op jit(solution)/shard_map/ppermute | solution.py:19
  90.6 1.8 %shard_map.92 = bf16[1024,512]{1,0:T(8,128)(2,1)} custom-call(bf16[2,1024,512]{2,1,0:T(8,128)(2,1)S(1)} %get-tuple-element.39.most_ref, bf16[2,256,512]{2,1,0:T(8,128)(2,1)S(1)} %get-tuple-element.40.weight_ref, bf16[1024,128]{1,0:T(8,128)(2,1)S(1)} %collective-permute-done.26.refs_0_, bf16[1024,128]{1,0:T(8,128)(2,1)S(1)} %collective-permute-done.27.refs_1_, ...), custom_call_target="tpu_custom_call" | custom-call | flops 1650000000 | bytes 4194304 | tf_op jit(solution)/shard_map/pallas_call | solution.py:419
  (53 shorter events, 2.0 us)
Async XLA Ops:
  0.0 17.7 %collective-permute-start.6 = (bf16[512,512]{1,0:T(8,128)(2,1)}, bf16[512,512]{1,0:T(8,128)(2,1)S(1)}, u32[]{:S(2)}, u32[]{:S(2)}) collective-permute-start(bf16[512,512]{1,0:T(8,128)(2,1)} %table_ref.1), channel_id=1, source_target_pairs={{0,2},{1,3},{2,0},{3,1},{4,6},{5,7},{6,4},{7,5},{8,10},{9,11},{10,... | collective-permute-start | bytes 1572872 | tf_op jit(solution)/shard_map/ppermute | solution.py:19
  3.0 14.7 %collective-permute-start = (bf16[512,256]{1,0:T(8,128)(2,1)}, bf16[512,256]{1,0:T(8,128)(2,1)}, u32[]{:S(2)}, u32[]{:S(2)}) collective-permute-start(bf16[512,256]{1,0:T(8,128)(2,1)} %param.15), channel_id=1, source_target_pairs={{0,16},{4,20},{8,24},{12,28},{16,0},{20,4},{24,8},{28,12},{1,17},{... | collective-permute-start | bytes 786440 | tf_op jit(solution)/shard_map/ppermute | solution.py:19
  5.6 1.1 %copy-start = (bf16[256,3,512]{2,0,1:T(8,128)(2,1)S(1)}, bf16[256,3,512]{2,0,1:T(8,128)(2,1)}, u32[]{:S(2)}) copy-start(bf16[256,3,512]{2,0,1:T(8,128)(2,1)} %param.11) | copy-start | bytes 2359300
  6.8 10.9 %copy-start.1 = (bf16[512,512]{1,0:T(8,128)(2,1)S(1)}, bf16[512,512]{1,0:T(8,128)(2,1)}, u32[]{:S(2)}) copy-start(bf16[512,512]{1,0:T(8,128)(2,1)} %table_ref.1) | copy-start | bytes 1572868
  8.6 20.7 %copy-start.6 = (s32[1024]{0:T(1024)S(1)}, s32[1024]{0:T(1024)}, u32[]{:S(2)}) copy-start(s32[1024]{0:T(1024)} %param.8) | copy-start | bytes 12292
  8.6 24.6 %copy-start.2 = (f32[2048]{0:T(1024)S(1)}, f32[2048]{0:T(1024)}, u32[]{:S(2)}) copy-start(f32[2048]{0:T(1024)} %param.10) | copy-start | bytes 24580
  8.6 9.6 %collective-permute-start.8 = (bf16[2,192,256]{2,1,0:T(8,128)(2,1)}, bf16[2,192,256]{2,1,0:T(8,128)(2,1)S(1)}, u32[]{:S(2)}, u32[]{:S(2)}) collective-permute-start(bf16[2,192,256]{2,1,0:T(8,128)(2,1)} %get-tuple-element.25), channel_id=1, source_target_pairs={{0,4},{4,0},{8,12},{12,8},{16,20},{20,16},{24,28},{28,24},{1,5},{5... | collective-permute-start | bytes 589832 | tf_op jit(solution)/shard_map/ppermute | solution.py:19
  10.2 11.5 %collective-permute-start.9 = (bf16[2,192,256]{2,1,0:T(8,128)(2,1)}, bf16[2,192,256]{2,1,0:T(8,128)(2,1)S(1)}, u32[]{:S(2)}, u32[]{:S(2)}) collective-permute-start(bf16[2,192,256]{2,1,0:T(8,128)(2,1)} %get-tuple-element.26), channel_id=1, source_target_pairs={{0,8},{4,12},{8,0},{12,4},{16,24},{20,28},{24,16},{28,20},{1,9},{5... | collective-permute-start | bytes 589832 | tf_op jit(solution)/shard_map/ppermute | solution.py:19
  11.8 14.4 %collective-permute-start.10 = (bf16[2,192,256]{2,1,0:T(8,128)(2,1)S(1)}, bf16[2,192,256]{2,1,0:T(8,128)(2,1)S(1)}, u32[]{:S(2)}, u32[]{:S(2)}) collective-permute-start(bf16[2,192,256]{2,1,0:T(8,128)(2,1)S(1)} %get-tuple-element.27), channel_id=1, source_target_pairs={{0,12},{4,8},{8,4},{12,0},{16,28},{20,24},{24,20},{28,16},{1,13},{... | collective-permute-start | bytes 589832 | tf_op jit(solution)/shard_map/ppermute | solution.py:19
  17.7 11.5 %collective-permute-start.5 = (bf16[512,512]{1,0:T(8,128)(2,1)S(1)}, bf16[512,512]{1,0:T(8,128)(2,1)S(1)}, u32[]{:S(2)}, u32[]{:S(2)}) collective-permute-start(bf16[512,512]{1,0:T(8,128)(2,1)S(1)} %copy-done.1), channel_id=1, source_target_pairs={{0,1},{1,0},{2,3},{3,2},{4,5},{5,4},{6,7},{7,6},{8,9},{9,8},{10,11... | collective-permute-start | bytes 1572872 | tf_op jit(solution)/shard_map/ppermute | solution.py:19
  17.7 11.6 %collective-permute-start.7 = (bf16[512,512]{1,0:T(8,128)(2,1)S(1)}, bf16[512,512]{1,0:T(8,128)(2,1)S(1)}, u32[]{:S(2)}, u32[]{:S(2)}) collective-permute-start(bf16[512,512]{1,0:T(8,128)(2,1)S(1)} %collective-permute-done.6.refs_2_), channel_id=1, source_target_pairs={{0,1},{1,0},{2,3},{3,2},{4,5},{5,4},{6,7},{7,6},{8,9},{9,8},{10,11... | collective-permute-start | bytes 1572872 | tf_op jit(solution)/shard_map/ppermute | solution.py:19
  18.2 29.2 %collective-permute-start.4 = (bf16[512,256]{1,0:T(8,128)(2,1)}, bf16[512,256]{1,0:T(8,128)(2,1)S(1)}, u32[]{:S(2)}, u32[]{:S(2)}) collective-permute-start(bf16[512,256]{1,0:T(8,128)(2,1)} %param.15), channel_id=1, source_target_pairs={{0,8},{4,12},{8,0},{12,4},{16,24},{20,28},{24,16},{28,20},{1,9},{5... | collective-permute-start | bytes 786440 | tf_op jit(solution)/shard_map/ppermute | solution.py:19
  27.3 7.7 %collective-permute-start.1 = (bf16[512,256]{1,0:T(8,128)(2,1)S(1)}, bf16[512,256]{1,0:T(8,128)(2,1)S(1)}, u32[]{:S(2)}, u32[]{:S(2)}) collective-permute-start(bf16[512,256]{1,0:T(8,128)(2,1)S(1)} %get-tuple-element.43), channel_id=1, source_target_pairs={{0,2},{1,3},{2,0},{3,1},{4,6},{5,7},{6,4},{7,5},{8,10},{9,11},{10,... | collective-permute-start | bytes 786440 | tf_op jit(solution)/shard_map/ppermute | solution.py:19
  27.9 25.1 %collective-permute-start.2 = (bf16[512,256]{1,0:T(8,128)(2,1)S(1)}, bf16[512,256]{1,0:T(8,128)(2,1)}, u32[]{:S(2)}, u32[]{:S(2)}) collective-permute-start(bf16[512,256]{1,0:T(8,128)(2,1)S(1)} %get-tuple-element.44.refs_6_), channel_id=1, source_target_pairs={{0,4},{4,0},{8,12},{12,8},{16,20},{20,16},{24,28},{28,24},{1,5},{5... | collective-permute-start | bytes 786440 | tf_op jit(solution)/shard_map/ppermute | solution.py:19
  29.2 16.7 %collective-permute-start.11 = (bf16[4,192,256]{2,1,0:T(8,128)(2,1)S(1)}, bf16[4,192,256]{2,1,0:T(8,128)(2,1)S(1)}, u32[]{:S(2)}, u32[]{:S(2)}) collective-permute-start(bf16[4,192,256]{2,1,0:T(8,128)(2,1)S(1)} %pad_maximum_fusion), channel_id=1, source_target_pairs={{0,16},{4,20},{8,24},{12,28},{16,0},{20,4},{24,8},{28,12},{1,17},{... | collective-permute-start | bytes 1179656 | tf_op jit(solution)/shard_map/ppermute | solution.py:19
  29.4 7.7 %collective-permute-start.12 = (s32[144]{0:T(256)S(1)}, s32[144]{0:T(256)S(1)}, u32[]{:S(2)}, u32[]{:S(2)}) collective-permute-start(s32[144]{0:T(256)S(1)} %slice.19), channel_id=1, source_target_pairs={{0,4},{4,8},{8,12},{12,16},{16,20},{20,24},{24,28},{1,5},{5,9},{9,... | collective-permute-start | bytes 1736 | tf_op jit(solution)/shard_map/ppermute | solution.py:290
  35.0 12.4 %collective-permute-start.13 = (bf16[512,256]{1,0:T(8,128)(2,1)}, bf16[512,256]{1,0:T(8,128)(2,1)S(1)}, u32[]{:S(2)}, u32[]{:S(2)}) collective-permute-start(bf16[512,256]{1,0:T(8,128)(2,1)} %collective-permute-done), channel_id=1, source_target_pairs={{0,8},{4,12},{8,0},{12,4},{16,24},{20,28},{24,16},{28,20},{1,9},{5... | collective-permute-start | bytes 786440 | tf_op jit(solution)/shard_map/ppermute | solution.py:19
  37.1 16.8 %collective-permute-start.3 = (bf16[512,256]{1,0:T(8,128)(2,1)S(1)}, bf16[512,256]{1,0:T(8,128)(2,1)S(1)}, u32[]{:S(2)}, u32[]{:S(2)}) collective-permute-start(bf16[512,256]{1,0:T(8,128)(2,1)S(1)} %collective-permute-done.1.refs_7_), channel_id=1, source_target_pairs={{0,4},{4,0},{8,12},{12,8},{16,20},{20,16},{24,28},{28,24},{1,5},{5... | collective-permute-start | bytes 786440 | tf_op jit(solution)/shard_map/ppermute | solution.py:19
  38.6 10.4 %copy-start.5 = (f32[7,3,512]{2,0,1:T(8,128)S(1)}, f32[7,3,512]{2,0,1:T(8,128)}, u32[]{:S(2)}) copy-start(f32[7,3,512]{2,0,1:T(8,128)} %param.12) | copy-start | bytes 129028
  38.6 17.3 %copy-start.3 = (bf16[32,128]{1,0:T(8,128)(2,1)S(1)}, bf16[32,128]{1,0:T(8,128)(2,1)}, u32[]{:S(2)}) copy-start(bf16[32,128]{1,0:T(8,128)(2,1)} %filter_ref.7) | copy-start | bytes 24580
  38.7 17.3 %copy-start.4 = (f32[512]{0:T(512)S(1)}, f32[512]{0:T(512)}, u32[]{:S(2)}) copy-start(f32[512]{0:T(512)} %param.14) | copy-start | bytes 6148
  47.5 7.8 %collective-permute-start.14 = (bf16[512,256]{1,0:T(8,128)(2,1)S(1)}, bf16[512,256]{1,0:T(8,128)(2,1)S(1)}, u32[]{:S(2)}, u32[]{:S(2)}) collective-permute-start(bf16[512,256]{1,0:T(8,128)(2,1)S(1)} %get-tuple-element.41), channel_id=1, source_target_pairs={{0,2},{1,3},{2,0},{3,1},{4,6},{5,7},{6,4},{7,5},{8,10},{9,11},{10,... | collective-permute-start | bytes 786440 | tf_op jit(solution)/shard_map/ppermute | solution.py:19
  49.1 6.8 %collective-permute-start.15 = (bf16[192,512]{1,0:T(8,128)(2,1)S(1)}, bf16[192,512]{1,0:T(8,128)(2,1)S(1)}, u32[]{:S(2)}, u32[]{:S(2)}) collective-permute-start(bf16[192,512]{1,0:T(8,128)(2,1)S(1)} %shard_map.84.refs_0_), channel_id=1, source_target_pairs={{0,4},{4,0},{8,12},{12,8},{16,20},{20,16},{24,28},{28,24},{1,5},{5... | collective-permute-start | bytes 589832 | tf_op jit(solution)/shard_map/ppermute | solution.py:19
  51.9 10.9 %collective-permute-start.20 = (bf16[192,512]{1,0:T(8,128)(2,1)S(1)}, bf16[192,512]{1,0:T(8,128)(2,1)S(1)}, u32[]{:S(2)}, u32[]{:S(2)}) collective-permute-start(bf16[192,512]{1,0:T(8,128)(2,1)S(1)} %shard_map.84.refs_0_), channel_id=1, source_target_pairs={{0,16},{4,20},{8,24},{12,28},{16,0},{20,4},{24,8},{28,12},{1,17},{... | collective-permute-start | bytes 589832 | tf_op jit(solution)/shard_map/ppermute | solution.py:19
  53.1 8.8 %collective-permute-start.17 = (bf16[192,512]{1,0:T(8,128)(2,1)S(1)}, bf16[192,512]{1,0:T(8,128)(2,1)S(1)}, u32[]{:S(2)}, u32[]{:S(2)}) collective-permute-start(bf16[192,512]{1,0:T(8,128)(2,1)S(1)} %shard_map.84.refs_0_), channel_id=1, source_target_pairs={{0,8},{4,12},{8,0},{12,4},{16,24},{20,28},{24,16},{28,20},{1,9},{5... | collective-permute-start | bytes 589832 | tf_op jit(solution)/shard_map/ppermute | solution.py:19
  53.9 10.9 %collective-permute-start.16 = (bf16[512,256]{1,0:T(8,128)(2,1)S(1)}, bf16[512,256]{1,0:T(8,128)(2,1)S(1)}, u32[]{:S(2)}, u32[]{:S(2)}) collective-permute-start(bf16[512,256]{1,0:T(8,128)(2,1)S(1)} %get-tuple-element.42.refs_10_), channel_id=1, source_target_pairs={{0,4},{4,0},{8,12},{12,8},{16,20},{20,16},{24,28},{28,24},{1,5},{5... | collective-permute-start | bytes 786440 | tf_op jit(solution)/shard_map/ppermute | solution.py:19
  61.9 7.8 %collective-permute-start.18 = (bf16[192,512]{1,0:T(8,128)(2,1)S(1)}, bf16[192,512]{1,0:T(8,128)(2,1)S(1)}, u32[]{:S(2)}, u32[]{:S(2)}) collective-permute-start(bf16[192,512]{1,0:T(8,128)(2,1)S(1)} %collective-permute-done.17.refs_0_), channel_id=1, source_target_pairs={{0,4},{4,0},{8,12},{12,8},{16,20},{20,16},{24,28},{28,24},{1,5},{5... | collective-permute-start | bytes 589832 | tf_op jit(solution)/shard_map/ppermute | solution.py:19
  62.8 9.3 %collective-permute-start.21 = (bf16[192,512]{1,0:T(8,128)(2,1)S(1)}, bf16[192,512]{1,0:T(8,128)(2,1)S(1)}, u32[]{:S(2)}, u32[]{:S(2)}) collective-permute-start(bf16[192,512]{1,0:T(8,128)(2,1)S(1)} %collective-permute-done.20.refs_0_), channel_id=1, source_target_pairs={{0,4},{4,0},{8,12},{12,8},{16,20},{20,16},{24,28},{28,24},{1,5},{5... | collective-permute-start | bytes 589832 | tf_op jit(solution)/shard_map/ppermute | solution.py:19
  64.1 12.6 %collective-permute-start.22 = (bf16[192,512]{1,0:T(8,128)(2,1)S(1)}, bf16[192,512]{1,0:T(8,128)(2,1)S(1)}, u32[]{:S(2)}, u32[]{:S(2)}) collective-permute-start(bf16[192,512]{1,0:T(8,128)(2,1)S(1)} %collective-permute-done.20.refs_0_), channel_id=1, source_target_pairs={{0,8},{4,12},{8,0},{12,4},{16,24},{20,28},{24,16},{28,20},{1,9},{5... | collective-permute-start | bytes 589832 | tf_op jit(solution)/shard_map/ppermute | solution.py:19
  64.4 9.1 %collective-permute-start.19 = (bf16[1024,128]{1,0:T(8,128)(2,1)S(1)}, bf16[1024,128]{1,0:T(8,128)(2,1)S(1)}, u32[]{:S(2)}, u32[]{:S(2)}) collective-permute-start(bf16[1024,128]{1,0:T(8,128)(2,1)S(1)} %shard_map.85.refs_0_), channel_id=1, source_target_pairs={{0,2},{1,3},{2,0},{3,1},{4,6},{5,7},{6,4},{7,5},{8,10},{9,11},{10,... | collective-permute-start | bytes 786440 | tf_op jit(solution)/shard_map/ppermute | solution.py:19
  64.8 17.1 %collective-permute-start.25 = (bf16[512,256]{1,0:T(8,128)(2,1)S(1)}, bf16[512,256]{1,0:T(8,128)(2,1)S(1)}, u32[]{:S(2)}, u32[]{:S(2)}) collective-permute-start(bf16[512,256]{1,0:T(8,128)(2,1)S(1)} %collective-permute-done.14.refs_11_), channel_id=1, source_target_pairs={{0,4},{4,0},{8,12},{12,8},{16,20},{20,16},{24,28},{28,24},{1,5},{5... | collective-permute-start | bytes 786440 | tf_op jit(solution)/shard_map/ppermute | solution.py:19
  71.9 10.0 %collective-permute-start.24 = (bf16[1024,128]{1,0:T(8,128)(2,1)S(1)}, bf16[1024,128]{1,0:T(8,128)(2,1)S(1)}, u32[]{:S(2)}, u32[]{:S(2)}) collective-permute-start(bf16[1024,128]{1,0:T(8,128)(2,1)S(1)} %shard_map.86.refs_1_), channel_id=1, source_target_pairs={{0,2},{1,3},{2,0},{3,1},{4,6},{5,7},{6,4},{7,5},{8,10},{9,11},{10,... | collective-permute-start | bytes 786440 | tf_op jit(solution)/shard_map/ppermute | solution.py:19
  72.1 5.7 %collective-permute-start.23 = (bf16[192,512]{1,0:T(8,128)(2,1)S(1)}, bf16[192,512]{1,0:T(8,128)(2,1)S(1)}, u32[]{:S(2)}, u32[]{:S(2)}) collective-permute-start(bf16[192,512]{1,0:T(8,128)(2,1)S(1)} %collective-permute-done.21.refs_1_), channel_id=1, source_target_pairs={{0,8},{4,12},{8,0},{12,4},{16,24},{20,28},{24,16},{28,20},{1,9},{5... | collective-permute-start | bytes 589832 | tf_op jit(solution)/shard_map/ppermute | solution.py:19
  75.7 10.2 %collective-permute-start.26 = (bf16[1024,128]{1,0:T(8,128)(2,1)S(1)}, bf16[1024,128]{1,0:T(8,128)(2,1)S(1)}, u32[]{:S(2)}, u32[]{:S(2)}) collective-permute-start(bf16[1024,128]{1,0:T(8,128)(2,1)S(1)} %shard_map.87.refs_2_), channel_id=1, source_target_pairs={{0,2},{1,3},{2,0},{3,1},{4,6},{5,7},{6,4},{7,5},{8,10},{9,11},{10,... | collective-permute-start | bytes 786440 | tf_op jit(solution)/shard_map/ppermute | solution.py:19
  80.0 7.2 %collective-permute-start.27 = (bf16[1024,128]{1,0:T(8,128)(2,1)S(1)}, bf16[1024,128]{1,0:T(8,128)(2,1)S(1)}, u32[]{:S(2)}, u32[]{:S(2)}) collective-permute-start(bf16[1024,128]{1,0:T(8,128)(2,1)S(1)} %shard_map.88.refs_3_), channel_id=1, source_target_pairs={{0,2},{1,3},{2,0},{3,1},{4,6},{5,7},{6,4},{7,5},{8,10},{9,11},{10,... | collective-permute-start | bytes 786440 | tf_op jit(solution)/shard_map/ppermute | solution.py:19
  87.9 2.7 %collective-permute-start.28 = (bf16[1024,512]{1,0:T(8,128)(2,1)S(1)}, bf16[1024,512]{1,0:T(8,128)(2,1)S(1)}, u32[]{:S(2)}, u32[]{:S(2)}) collective-permute-start(bf16[1024,512]{1,0:T(8,128)(2,1)S(1)} %shard_map.91), channel_id=1, source_target_pairs={{0,1},{1,0},{2,3},{3,2},{4,5},{5,4},{6,7},{7,6},{8,9},{9,8},{10,11... | collective-permute-start | bytes 3145736 | tf_op jit(solution)/shard_map/ppermute | solution.py:19
